TPU v7x, 128 devices: a whole 4x4x4 slice. The times are simulated.
128 devices in a mesh: seq: 16 (over y, z), mp: 8 (over x, core).
Axes of the slice: x: 4, y: 4, z: 4, core: 2. Of those that a mesh axis runs over, the one named last changes fastest.
Arguments:
- stretch_x: bfloat16 [8192, 16384], P(('seq', 'mp')), may hold values from -6 to 6
- stretch_bc: bfloat16 [8192, 2, 2048], P(('seq', 'mp')), may hold values from -1.75 to 1.75
- stretch_dt: bfloat16 [8192, 256], P(('seq', 'mp')), may hold values from -5 to 5
- stretch_q: bfloat16 [8192, 8192], P(('seq', 'mp')), may hold values from -22 to 22
- stretch_kv: bfloat16 [8192, 2, 1024], P(('seq', 'mp')), may hold values from -6 to 6
- stretch_place: int32 [128], P('seq'), may hold values from 0 to 127, as said below
- segment_ids: int32 [8192], P('seq'), may hold values from 0 to 5, never falling along the last dimension, each value on 1 to 4096 neighbouring positions
- ssm_rate: float32 [256], replicated, may hold values from 0.001 to 1
- dt_bias: float32 [256], replicated, may hold values from -5 to -2
- skip_gain: float32 [256], replicated, may hold values from 0.5 to 1.5
Outputs:
- ssm_out: bfloat16 [8192, 16384], P('seq', 'mp')
- attn_out: bfloat16 [8192, 8192], P('seq', 'mp')
Inputs may be any that keep to these rules, and one draw needn't show every extreme that they name: stretch_place holds each of 0 to 127 once. Stretch c goes to owner stretch_place[c] // 8; every owner receives 512 // 64 stretches; at most 1 of the stretches held by one index of seq go to one owner, and every index of seq sends exactly 1 to some owner. `segment_ids`: document ids never fall along the sequence; each document has 1 to 4096 tokens, one exactly that many.
All inputs are finite; a program needn't handle non-finite values.
Results may differ from a plain program's by a relative error of at most 0.0095.
Values may be sent and summed in bfloat16 or wider, within the bound.
No kernel may reach another device: no remote copies, remote signals or barrier semaphores. Data moves between devices by JAX's collectives and lax.ppermute only.
A program may use at most 192 MiB of HBM per device.

v0:
```python
import jax
import jax.numpy as jnp
from jax import lax
from jax.sharding import PartitionSpec as P

SSM_HEADS = 256
HEAD_DIM = 64
GROUPS = 8
Q_HEADS = 64
KV_HEADS = 8
ATT_DIM = 128
BLOCK = 256


NEG_BIG = -1e30


def block_scan(
    inputs_x, step_size, log_decay, b_rows, c_rows, seg_rows, state_start, seg_start, block
):
    length = inputs_x.shape[0]
    count = length // block
    positions = jnp.arange(block)
    causal = positions[:, None] >= positions[None, :]

    def one_block(carry, pieces):
        state_in, prev_seg = carry
        x_blk, size_blk, decay_blk, b_blk, c_blk, seg_blk = pieces
        cumulative = jnp.cumsum(decay_blk, axis=0)
        allowed = causal & (seg_blk[:, None] == seg_blk[None, :])
        gram_matrix = jnp.einsum("tgn,sgn->gts", c_blk, b_blk, preferred_element_type=jnp.float32)
        by_head = jnp.transpose(cumulative, (1, 2, 0))
        log_gaps = by_head[:, :, :, None] - by_head[:, :, None, :]
        weights = jnp.exp(jnp.where(allowed, log_gaps, NEG_BIG))
        mixing = (gram_matrix[:, None] * weights).astype(jnp.bfloat16)
        driven = (size_blk[..., None] * x_blk.astype(jnp.float32)).astype(jnp.bfloat16)
        result = jnp.einsum("ghts,sghp->tghp", mixing, driven, preferred_element_type=jnp.float32)
        carried = jnp.where((seg_blk == prev_seg)[:, None, None], jnp.exp(cumulative), 0.0)
        reached = jnp.einsum(
            "tgn,ghnp->tghp", c_blk.astype(jnp.float32), state_in, precision=lax.Precision.HIGHEST
        )
        result = result + carried[..., None] * reached
        last_seg = seg_blk[block - 1]
        keeping = jnp.where(last_seg == prev_seg, jnp.exp(cumulative[block - 1]), 0.0)
        tail_weight = jnp.where(
            (seg_blk == last_seg)[:, None, None],
            jnp.exp(cumulative[block - 1][None] - cumulative),
            0.0,
        )
        loaded = (tail_weight[..., None] * b_blk.astype(jnp.float32)[:, :, None, :]).astype(
            jnp.bfloat16
        )
        state_out = keeping[..., None, None] * state_in + jnp.einsum(
            "sghn,sghp->ghnp", loaded, driven, preferred_element_type=jnp.float32
        )
        return ((state_out, last_seg), result)

    stacked = tuple(
        (
            array_in.reshape((count, block) + array_in.shape[1:])
            for array_in in (inputs_x, step_size, log_decay, b_rows, c_rows, seg_rows)
        )
    )
    (state_end, last_seen), results = lax.scan(one_block, (state_start, seg_start), stacked)
    return (results.reshape((length,) + results.shape[2:]), state_end)


def shards(
    stretch_x,
    stretch_bc,
    stretch_dt,
    stretch_q,
    stretch_kv,
    stretch_place,
    segment_ids,
    ssm_rate,
    dt_bias,
    skip_gain,
):
    n_seq = lax.axis_size("seq")
    n_mp = lax.axis_size("mp")
    seq_index = lax.axis_index("seq")
    mp_index = lax.axis_index("mp")
    row_count = stretch_x.shape[0]
    flat_x = stretch_x.reshape(row_count, 1, stretch_x.shape[1])
    flat_dt = stretch_dt.reshape(row_count, 1, stretch_dt.shape[1])
    flat_q = stretch_q.reshape(row_count, 1, stretch_q.shape[1])
    split_x, split_bc, split_dt, split_q, split_kv = (
        lax.all_to_all(flat_x, "mp", split_axis=2, concat_axis=0, tiled=True),
        lax.all_to_all(stretch_bc, "mp", split_axis=2, concat_axis=0, tiled=True),
        lax.all_to_all(flat_dt, "mp", split_axis=2, concat_axis=0, tiled=True),
        lax.all_to_all(flat_q, "mp", split_axis=2, concat_axis=0, tiled=True),
        lax.all_to_all(stretch_kv, "mp", split_axis=2, concat_axis=0, tiled=True),
    )
    tok_dev = split_x.shape[0]
    rows_x = split_x.reshape(tok_dev, split_x.shape[2])
    rows_bc = split_bc.reshape(tok_dev, 2 * split_bc.shape[2])
    rows_dt = split_dt.reshape(tok_dev, split_dt.shape[2])
    rows_q = split_q.reshape(tok_dev, split_q.shape[2])
    rows_kv = split_kv.reshape(tok_dev, 2 * split_kv.shape[2])
    per_dev = stretch_place.shape[0]
    stretch_len = tok_dev // per_dev
    capacity = (per_dev + n_seq - 2) // (n_seq - 1)
    owner_ids = stretch_place // per_dev
    dest_slot = stretch_place % per_dev
    stretch_order = jnp.arange(per_dev)
    earlier_same = (owner_ids[:, None] == owner_ids[None, :]) & (
        stretch_order[None, :] < stretch_order[:, None]
    )
    within_rank = jnp.sum(earlier_same.astype(jnp.int32), axis=1)
    slot_ids = owner_ids * capacity + within_rank
    send_map = jnp.arange(n_seq * capacity)[:, None] == slot_ids[None, :]
    send_half = send_map.astype(jnp.bfloat16)
    slot_codes = (
        jnp.dot(
            send_map.astype(jnp.float32),
            (dest_slot + 1).astype(jnp.float32),
            precision=lax.Precision.HIGHEST,
        )
        - 1.0
    )

    def pack_rows(rows_arr):
        row_width = rows_arr.shape[1]
        as_stretches = rows_arr.reshape(per_dev, stretch_len * row_width)
        packed = jnp.dot(send_half, as_stretches, preferred_element_type=jnp.float32).astype(
            jnp.bfloat16
        )
        return packed.reshape(n_seq * capacity * stretch_len, row_width)

    got_x, got_bc, got_dt, got_q, got_kv, got_codes = (
        lax.all_to_all(pack_rows(rows_x), "seq", split_axis=0, concat_axis=0, tiled=True),
        lax.all_to_all(pack_rows(rows_bc), "seq", split_axis=0, concat_axis=0, tiled=True),
        lax.all_to_all(pack_rows(rows_dt), "seq", split_axis=0, concat_axis=0, tiled=True),
        lax.all_to_all(pack_rows(rows_q), "seq", split_axis=0, concat_axis=0, tiled=True),
        lax.all_to_all(pack_rows(rows_kv), "seq", split_axis=0, concat_axis=0, tiled=True),
        lax.all_to_all(
            slot_codes.astype(jnp.bfloat16), "seq", split_axis=0, concat_axis=0, tiled=True
        ),
    )
    recv_map = (
        jnp.arange(per_dev).astype(jnp.float32)[:, None] == got_codes.astype(jnp.float32)[None, :]
    ).astype(jnp.bfloat16)

    def unpack_rows(buffer):
        row_width = buffer.shape[1]
        as_slots = buffer.reshape(n_seq * capacity, stretch_len * row_width)
        placed = jnp.dot(recv_map, as_slots, preferred_element_type=jnp.float32).astype(
            jnp.bfloat16
        )
        return placed.reshape(tok_dev, row_width)

    own_x = unpack_rows(got_x)
    own_bc = unpack_rows(got_bc)
    own_dt = unpack_rows(got_dt)
    own_q = unpack_rows(got_q)
    own_kv = unpack_rows(got_kv)
    heads_mp = own_dt.shape[1]
    per_group = SSM_HEADS // GROUPS
    groups_mp = GROUPS // n_mp
    state_dim = own_bc.shape[1] // (2 * groups_mp)
    head_x, head_dt = (
        lax.all_to_all(own_x, "seq", split_axis=1, concat_axis=0, tiled=True),
        lax.all_to_all(own_dt, "seq", split_axis=1, concat_axis=0, tiled=True),
    )
    heads_dev = head_dt.shape[1]
    group_bc, group_seg = (
        lax.all_gather(own_bc, "seq", axis=0, tiled=True),
        lax.all_gather(segment_ids.astype(jnp.bfloat16), "seq", axis=0, tiled=True),
    )
    whole_seg = group_seg.astype(jnp.int32)
    total_len = head_x.shape[0]
    group_local = seq_index * heads_dev // per_group
    b_rows = lax.dynamic_slice_in_dim(group_bc, group_local * state_dim, state_dim, 1).reshape(
        total_len, 1, state_dim
    )
    c_rows = lax.dynamic_slice_in_dim(
        group_bc, (groups_mp + group_local) * state_dim, state_dim, 1
    ).reshape(total_len, 1, state_dim)
    first_head = mp_index * heads_mp + seq_index * heads_dev
    rates = lax.dynamic_slice_in_dim(ssm_rate, first_head, heads_dev, 0)
    biases = lax.dynamic_slice_in_dim(dt_bias, first_head, heads_dev, 0)
    gains = lax.dynamic_slice_in_dim(skip_gain, first_head, heads_dev, 0)
    step_size = jax.nn.softplus(head_dt.astype(jnp.float32) + biases[None, :])
    log_decay = (-rates[None, :] * step_size).reshape(total_len, 1, heads_dev)
    step_size = step_size.reshape(total_len, 1, heads_dev)
    inputs_x = head_x.reshape(total_len, 1, heads_dev, HEAD_DIM)
    zero_state = jnp.zeros((1, heads_dev, state_dim, HEAD_DIM), jnp.float32)
    scanned, unused_state = block_scan(
        inputs_x, step_size, log_decay, b_rows, c_rows, whole_seg, zero_state, whole_seg[0], BLOCK
    )
    head_out = (scanned + gains[None, None, :, None] * inputs_x.astype(jnp.float32)).astype(
        jnp.bfloat16
    )
    ssm_rows = lax.all_to_all(
        head_out.reshape(total_len, heads_dev * HEAD_DIM),
        "seq",
        split_axis=0,
        concat_axis=1,
        tiled=True,
    )
    kv_local = KV_HEADS // n_mp
    q_local = Q_HEADS // n_mp
    group_size = q_local // kv_local
    scale = ATT_DIM ** (-0.5)
    queries = own_q.reshape(tok_dev, kv_local, group_size, ATT_DIM)
    q_pos = seq_index * tok_dev + jnp.arange(tok_dev, dtype=jnp.int32)

    def attend(carry, kv_blk, seg_blk, blk_start):
        running_max, running_sum, running_acc = carry
        step_rows = kv_blk.shape[0]
        kv_split = kv_blk.reshape(step_rows, 2, kv_local, ATT_DIM)
        scores = (
            jnp.einsum(
                "tkgd,skd->tkgs", queries, kv_split[:, 0], preferred_element_type=jnp.float32
            )
            * scale
        )
        k_pos = blk_start + jnp.arange(step_rows, dtype=jnp.int32)
        allowed = (k_pos[None, :] <= q_pos[:, None]) & (
            seg_blk.astype(jnp.int32)[None, :] == segment_ids[:, None]
        )
        scores = jnp.where(allowed[:, None, None, :], scores, NEG_BIG)
        new_max = jnp.maximum(running_max, jnp.max(scores, axis=-1))
        expo = jnp.where(allowed[:, None, None, :], jnp.exp(scores - new_max[..., None]), 0.0)
        factor = jnp.exp(running_max - new_max)
        new_sum = running_sum * factor + jnp.sum(expo, axis=-1)
        mixed = jnp.einsum(
            "tkgs,skd->tkgd",
            expo.astype(jnp.bfloat16),
            kv_split[:, 1],
            preferred_element_type=jnp.float32,
        )
        new_acc = running_acc * factor[..., None] + mixed
        return (new_max, new_sum, new_acc)

    start_carry = (
        jnp.full((tok_dev, kv_local, group_size), NEG_BIG, jnp.float32),
        jnp.zeros((tok_dev, kv_local, group_size), jnp.float32),
        jnp.zeros((tok_dev, kv_local, group_size, ATT_DIM), jnp.float32),
    )
    kv_piece = lax.all_gather(own_kv, "seq", axis=0, tiled=True)
    seg_piece = lax.all_gather(segment_ids.astype(jnp.bfloat16), "seq", axis=0, tiled=True)
    span_rows = kv_piece.shape[0]
    step_rows = min(span_rows, tok_dev)
    part_count = span_rows // step_rows
    stacked = (
        kv_piece.reshape(part_count, step_rows, kv_piece.shape[1]),
        seg_piece.reshape(part_count, step_rows),
        jnp.arange(part_count, dtype=jnp.int32) * step_rows,
    )

    def one_part(inner, pieces):
        return (attend(inner, pieces[0], pieces[1], pieces[2]), None)

    result, unused = lax.scan(one_part, start_carry, stacked)
    final_max, final_sum, final_acc = result
    attn_rows = (
        (final_acc / final_sum[..., None]).astype(jnp.bfloat16).reshape(tok_dev, q_local * ATT_DIM)
    )
    return (ssm_rows, attn_rows)


def solution(mesh):
    return jax.shard_map(
        shards,
        mesh=mesh,
        in_specs=(
            P(("seq", "mp"), None),
            P(("seq", "mp"), None, None),
            P(("seq", "mp"), None),
            P(("seq", "mp"), None),
            P(("seq", "mp"), None, None),
            P("seq"),
            P("seq"),
            P(),
            P(),
            P(),
        ),
        out_specs=(P("seq", "mp"), P("seq", "mp")),
        check_vma=False,
    )
```

profile of v0, /device:TPU:2, one launch (start us, length us, event | category | flops | bytes accessed | tf_op | source)
XLA Modules:
  0.0 1644.3 jit_solution(688096488938520298)
XLA Ops:
  11.3 4.8 all-to-all-start.4
  17.2 7.8 all-to-all-done.4
  25.0 8.0 all-to-all-start
  44.5 15.8 all-to-all-done.5
  64.2 7.8 all_to_all.174
  78.9 6.3 all-to-all-done.2
  85.2 4.7 all-to-all-start.10
  90.7 4.5 all_to_all.132
  103.6 5.6 all-to-all-done.3
  112.8 12.9 copy.175
  125.7 90.8 %reduce.9 = bf16[16384,64]{1,0:T(8,128)(2,1)} reduce(bf16[16384,1,64]{2,1,0:T(2,128)(2,1)} %bitcast.327, bf16[]{:T(256)} %broadcast.263), dimensions={1}, to_apply=%bitcast.215.reduce_sub_computation | reduce | bytes 4194306
  216.5 7.6 reshape.496
  224.0 5.3 all-to-all-start.6
  229.3 9.2 copy.186
  238.5 46.6 %reduce.10 = bf16[8192,64]{1,0:T(8,128)(2,1)} reduce(bf16[8192,1,64]{2,1,0:T(2,128)(2,1)} %bitcast.332, bf16[]{:T(256)} %broadcast.263), dimensions={1}, to_apply=%bitcast.219.reduce_sub_computation | reduce | bytes 2097154
  289.4 4.8 all-to-all-start.12
  294.2 5.9 reshape.497
  300.1 15.5 copy.176
  318.1 4.4 copy.208
  322.4 7.4 all-to-all-start.7
  334.2 8.2 copy.187
  346.1 43.8 %all-to-all-done.7 = bf16[16,64,2048]{2,1,0:T(8,128)(2,1)} async-done(((bf16[16,64,2048]{2,1,0:T(8,128)(2,1)}), bf16[16,64,2048]{2,1,0:T(8,128)(2,1)}, u32[]{:S(2)}, u32[]{:S(2)}) %all-to-all-start.7) | async-done | bytes 4194336 | tf_op jit(solution)/shard_map/all_to_all | solution.py:132
  389.9 12.8 all-to-all-start.13
  402.7 4.5 copy.209
  410.3 4.4 copy.177
  414.6 17.1 %all-to-all-done.13 = bf16[16,64,1024]{2,1,0:T(8,128)(2,1)} async-done(((bf16[16,64,1024]{2,1,0:T(8,128)(2,1)}), bf16[16,64,1024]{2,1,0:T(8,128)(2,1)}, u32[]{:S(2)}, u32[]{:S(2)}) %all-to-all-start.13) | async-done | bytes 2097184 | tf_op jit(solution)/shard_map/all_to_all | solution.py:135
  435.6 41.2 %all-gather = bf16[16,1,512]{2,1,0:T(2,128)(2,1)S(1)} all-gather(bf16[1,1,512]{2,1,0:T(2,128)(2,1)S(1)} %reshape.460), channel_id=1, replica_groups=mesh['seq'=16,'mp'=8] {'seq'}, dimensions={0}, use_global_device_ids=true | all-gather | bytes 17408 | tf_op jit(solution)/shard_map/all_gather | solution.py:169
  499.3 7.4 constant_dynamic-slice_fusion.4
  506.7 811.7 %while.30 = (s32[]{:T(128)}, f32[1,2,256,64]{2,3,1,0:T(8,128)}, s32[]{:T(128)}, f32[32,256,1,2,64]{1,0,4,3,2:T(8,128)}, s32[32,256]{1,0:T(8,128)}, /*index=5*/f3...) while((s32[]{:T(128)}, f32[1,2,256,64]{2,3,1,0:T(8,128)}, ...), condition=%wide.region_4.5_spmd.clone, body=%wide.region_1.4_spmd.clone.sunk | while | flops 169249296 | bytes 3510261 | solution.py:64
  1318.4 5.2 reshape.448
  1329.9 5.3 all-to-all-start.9
  1335.3 294.6 %while.31 = (s32[]{:T(128)}, f32[512,1,8]{0,2,1:T(8,128)S(1)}, f32[512,1,8]{0,2,1:T(8,128)S(1)}, f32[512,1,8,128]{0,3,2,1:T(8,128)}, s32[16]{0:T(128)S(1)}, /*in...) while((s32[]{:T(128)}, f32[512,1,8]{0,2,1:T(8,128)S(1)}, ...), condition=%wide.region_8.9_spmd.clone, body=%wide.region_5.8_spmd.clone.sunk | while | flops 1103390208 | bytes 66600120 | solution.py:256
  1338.7 4.9 fusion.120
  1343.5 7.5 bitcast_add_fusion.8
  1356.5 4.9 fusion.120
  1361.4 8.1 bitcast_add_fusion.8
  1375.0 4.9 fusion.120
  1379.8 8.1 bitcast_add_fusion.8
  1393.4 4.9 fusion.120
  1398.3 8.1 bitcast_add_fusion.8
  1411.9 4.9 fusion.120
  1416.8 8.1 bitcast_add_fusion.8
  1430.3 4.9 fusion.120
  1435.2 8.1 bitcast_add_fusion.8
  1448.8 4.9 fusion.120
  1453.7 8.1 bitcast_add_fusion.8
  1467.2 4.9 fusion.120
  1472.1 8.1 bitcast_add_fusion.8
  1485.7 4.9 fusion.120
  1490.6 8.1 bitcast_add_fusion.8
  1504.1 4.9 fusion.120
  1509.0 8.1 bitcast_add_fusion.8
  1522.6 4.9 fusion.120
  1527.5 8.1 bitcast_add_fusion.8
  1541.0 4.9 fusion.120
  1545.9 8.1 bitcast_add_fusion.8
  1559.5 4.9 fusion.120
  1564.4 8.1 bitcast_add_fusion.8
  1577.9 4.9 fusion.120
  1582.8 8.1 bitcast_add_fusion.8
  1596.4 4.9 fusion.120
  1601.3 8.1 bitcast_add_fusion.8
  1614.8 4.9 fusion.120
  1619.7 8.1 bitcast_add_fusion.8
  (1509 shorter events, 952.0 us)
Async XLA Ops:
  7.2 9.0 copy-start.16
  11.3 13.7 all-to-all-start.4
  25.0 15.5 all-to-all-start
  36.6 25.7 %copy-start.11 = (bf16[64,256]{1,0:T(8,128)(2,1)S(1)}, bf16[64,256]{1,0:T(8,128)(2,1)}, u32[]{:S(2)}) copy-start(bf16[64,256]{1,0:T(8,128)(2,1)} %param.16) | copy-start | bytes 98308
  40.6 19.7 %all-to-all-start.5 = ((bf16[16,64,512]{2,1,0:T(8,128)(2,1)}), bf16[16,64,512]{2,1,0:T(8,128)(2,1)S(1)}, u32[]{:S(2)}, u32[]{:S(2)}) async-start(bf16[16,64,512]{2,1,0:T(8,128)(2,1)} %bitcast.100), calls=%async_computation.5 | async-start | bytes 2097152 | tf_op jit(solution)/shard_map/all_to_all | solution.py:133
  44.2 33.1 %copy-start.7 = (bf16[64,2,1024]{2,1,0:T(2,128)(2,1)S(1)}, bf16[64,2,1024]{2,1,0:T(2,128)(2,1)}, u32[]{:S(2)}) copy-start(bf16[64,2,1024]{2,1,0:T(2,128)(2,1)} %param.18) | copy-start | bytes 786436
  44.2 455.1 %all-gather.4.cloned.1.call-start = ((), (), s32[]{:S(2)}) async-start(), calls=%async_computation.14 | async-start | bytes 8912896 | tf_op jit(solution)/shard_map/all_gather | solution.py:168
  73.7 11.5 all-to-all-start.2
  85.2 12.3 all-to-all-start.10
  97.4 15.3 copy-start.1
  97.4 11.8 all-to-all-start.3
  109.2 114.8 %all-to-all-start.11 = ((bf16[16,64,256]{2,1,0:T(8,128)(2,1)}), bf16[16,64,256]{2,1,0:T(8,128)(2,1)S(1)}, u32[]{:S(2)}, u32[]{:S(2)}) async-start(bf16[16,64,256]{2,1,0:T(8,128)(2,1)} %bitcast.117), calls=%async_computation.11 | async-start | bytes 1048576 | tf_op jit(solution)/shard_map/all_to_all | solution.py:136
  224.0 14.5 copy-start.2
  224.0 65.4 %all-to-all-start.6 = ((bf16[8,2,65536]{2,1,0:T(2,128)(2,1)}), bf16[8,2,65536]{2,1,0:T(2,128)(2,1)S(1)}, u32[]{:S(2)}, u32[]{:S(2)}) async-start(bf16[8,2,65536]{2,1,0:T(2,128)(2,1)} %reshape.496), calls=%async_computation.6 | async-start | bytes 4194304 | tf_op jit(solution)/shard_map/all_to_all | solution.py:89
  289.4 33.0 %all-to-all-start.12 = ((bf16[8,2,32768]{2,1,0:T(2,128)(2,1)}), bf16[8,2,32768]{2,1,0:T(2,128)(2,1)S(1)}, u32[]{:S(2)}, u32[]{:S(2)}) async-start(bf16[8,2,32768]{2,1,0:T(2,128)(2,1)} %reshape.500), calls=%async_computation.12 | async-start | bytes 2097152 | tf_op jit(solution)/shard_map/all_to_all | solution.py:92
  322.4 67.5 %all-to-all-start.7 = ((bf16[16,64,2048]{2,1,0:T(8,128)(2,1)}), bf16[16,64,2048]{2,1,0:T(8,128)(2,1)}, u32[]{:S(2)}, u32[]{:S(2)}) async-start(bf16[16,64,2048]{2,1,0:T(8,128)(2,1)} %bitcast.334), calls=%async_computation.7 | async-start | bytes 8388608 | tf_op jit(solution)/shard_map/all_to_all | solution.py:132
  389.9 41.8 %all-to-all-start.13 = ((bf16[16,64,1024]{2,1,0:T(8,128)(2,1)}), bf16[16,64,1024]{2,1,0:T(8,128)(2,1)}, u32[]{:S(2)}, u32[]{:S(2)}) async-start(bf16[16,64,1024]{2,1,0:T(8,128)(2,1)} %bitcast.127), calls=%async_computation.13 | async-start | bytes 4194304 | tf_op jit(solution)/shard_map/all_to_all | solution.py:135
  410.3 25.3 %copy-start.9 = (s32[512]{0:T(512)S(1)}, s32[512]{0:T(512)}, u32[]{:S(2)}) copy-start(s32[512]{0:T(512)} %param.20) | copy-start | bytes 6148
  410.3 68.4 %copy-start.13 = (f32[256]{0:T(256)S(1)}, f32[256]{0:T(256)}, u32[]{:S(2)}) copy-start(f32[256]{0:T(256)} %param.22) | copy-start | bytes 3076
  410.3 68.5 %copy-start.14 = (f32[256]{0:T(256)S(1)}, f32[256]{0:T(256)}, u32[]{:S(2)}) copy-start(f32[256]{0:T(256)} %param.23) | copy-start | bytes 3076
  410.3 69.8 %copy-start.15 = (f32[256]{0:T(256)S(1)}, f32[256]{0:T(256)}, u32[]{:S(2)}) copy-start(f32[256]{0:T(256)} %param.21) | copy-start | bytes 3076
  410.3 70.7 %copy-start.3 = (bf16[16,64,256]{2,1,0:T(8,128)(2,1)S(1)}, bf16[16,64,256]{2,1,0:T(8,128)(2,1)}, u32[]{:S(2)}) copy-start(bf16[16,64,256]{2,1,0:T(8,128)(2,1)} %copy-done.2) | copy-start | bytes 1572868
  431.7 56.7 %all-to-all-start.8 = ((bf16[512,16,128]{0,2,1:T(8,128)(2,1)}), bf16[512,16,128]{0,2,1:T(8,128)(2,1)S(1)}, u32[]{:S(2)}, u32[]{:S(2)}) async-start(bf16[512,16,128]{0,2,1:T(8,128)(2,1)} %copy.177), calls=%async_computation.8 | async-start | bytes 4194304 | tf_op jit(solution)/shard_map/all_to_all | solution.py:163
  435.5 899.8 %all-gather.6.cloned.1.call-start = ((), (), s32[]{:S(2)}) async-start(), calls=%async_computation.15 | async-start | bytes 4456448 | tf_op jit(solution)/shard_map/all_gather | solution.py:242
  509.3 3.5 copy-start.6
  533.8 3.5 copy-start.6
  559.2 3.5 copy-start.6
  584.5 3.5 copy-start.6
  609.9 3.5 copy-start.6
  635.3 3.5 copy-start.6
  660.6 3.5 copy-start.6
  686.0 3.5 copy-start.6
  711.4 3.5 copy-start.6
  736.8 3.5 copy-start.6
  762.2 3.5 copy-start.6
  787.6 3.5 copy-start.6
  813.1 3.5 copy-start.6
  838.5 3.5 copy-start.6
  863.9 3.5 copy-start.6
  889.3 3.5 copy-start.6
  914.8 3.5 copy-start.6
  990.9 3.5 copy-start.6
  1067.1 3.5 copy-start.6
  1318.3 5.2 copy-start.12
  1327.4 7.9 copy-start.5
  1327.4 7.9 copy-start.10
  1327.4 7.9 copy-start.17
  1329.9 303.2 %all-to-all-start.9 = ((bf16[16,512,128]{1,2,0:T(8,128)(2,1)}), bf16[16,512,128]{1,2,0:T(8,128)(2,1)}, u32[]{:S(2)}, u32[]{:S(2)}) async-start(bf16[16,512,128]{1,2,0:T(8,128)(2,1)} %copy.183), calls=%async_computation.9 | async-start | bytes 4194304 | tf_op jit(solution)/shard_map/all_to_all | solution.py:195
  1343.5 7.5 copy-start
  1361.4 8.1 copy-start
  1379.8 8.1 copy-start
  1398.3 8.1 copy-start
  1416.7 8.1 copy-start
  1435.2 8.1 copy-start
  1453.6 8.1 copy-start
  1472.1 8.1 copy-start
  1490.5 8.1 copy-start
  1509.0 8.1 copy-start
  1527.4 8.1 copy-start
  1545.9 8.1 copy-start
  1564.3 8.1 copy-start
  1582.8 8.1 copy-start
  1601.2 8.1 copy-start
  1619.7 8.1 copy-start
  (77 other events, 111.9 us)
Sparse Core Ops, SparseCore 0:
  62.4 74.6 all-gather.3
  482.5 50.8 all-gather.5
where the time goes:
time: 1670 us; the launch traced here: 1640 us
  local copies, waits for them, and re-layouts  523 us (31%)
  other arithmetic  458 us (27%)
  matrix products  383 us (23%)
  waiting for transfers between devices  100 us (6%)
  starting transfers between devices  72 us (4%)
  blocking collectives  49 us (3%)
  loops' own time  44.5 us (3%)
    unnamed x7, other arithmetic  138 us
    dynamic_update_slice x64, local copies, waits for them, and re-layouts, block_scan(): lax.scan(one_block, (state_start, seg_start), stacked)  136 us
    dot_general x16, matrix products, attend(): jnp.einsum('tkgs,skd->tkgd', expo.astype(jnp.bfloat16), kv_split[:, 1], p...  129 us
    dynamic_slice x128, local copies, waits for them, and re-layouts, block_scan(): lax.scan(one_block, (state_start, seg_start), stacked)  87.1 us
    dot_general x16, matrix products, attend(): jnp.einsum('tkgd,skd->tkgs', queries, kv_split[:, 0], preferred_element_t...  78 us
    unnamed x59, local copies, waits for them, and re-layouts  59.4 us
    dot_general x32, matrix products, one_block(): jnp.einsum('sghn,sghp->ghnp', loaded, driven, preferred_element_type=jnp....  57 us
    select_n x32, other arithmetic, one_block(): jnp.where((seg_blk == prev_seg)[:, None, None], jnp.exp(cumulative), 0.0)  53.7 us
  transfers between devices with their start and end apart: 15, of which 7 were waited for; matrix products, arithmetic and copies ran while one was open for 82% of the time, Pallas kernels for 0%

commit v1 on v0

v1 whole, which is shorter than its diff:
```python
import functools

import jax
import jax.numpy as jnp
from jax import lax
from jax.experimental import pallas as pl
from jax.experimental.pallas import tpu as pltpu
from jax.sharding import PartitionSpec as P

SSM_HEADS = 256
HEAD_DIM = 64
STATE = 256
GROUPS = 8
Q_HEADS = 64
KV_HEADS = 8
ATT_DIM = 128
LEN = 64
SEQ = 16
MP = 8
STRETCHES = 128
CHUNK = 512
HALF = 256
PER = CHUNK // LEN
LANES = 128
DOCS = 6
TOKENS = 8192

X_ROWS = LEN
BC_ROWS = 16
Q_ROWS = 32
BC_AT = X_ROWS
Q_AT = BC_AT + BC_ROWS
INFO_AT = Q_AT + Q_ROWS
HOP_ROWS = INFO_AT + 16
OWN_ROWS = X_ROWS + BC_ROWS
K_AT, V_AT, B_AT, DT_AT, G_ROWS = 0, 64, 128, 256, 272
NEG_BIG = -1e30
F32 = jnp.float32
BF16 = jnp.bfloat16
MIB = 1 << 20


def params(mib):
    return pltpu.CompilerParams(vmem_limit_bytes=mib * MIB)


def pack_kernel(x_ref, b_ref, c_ref, q_ref, k_ref, v_ref, dt_ref, info_ref, hop_ref, kvb_ref):
    info = info_ref[0:1, :]
    row = lax.broadcasted_iota(jnp.int32, (16, LANES), 0)
    tile = jnp.where(row == 0, jnp.broadcast_to(info, (16, LANES)), 0.0).astype(BF16)
    for s in range(SEQ):
        hop_ref[s, 0, 0:X_ROWS, :] = x_ref[:, s * LANES : (s + 1) * LANES]
        toks = pl.ds((s // 4) * 16, 16)
        source = b_ref if s % 4 < 2 else c_ref
        col = (s % 2) * LANES
        hop_ref[s, 0, BC_AT : BC_AT + BC_ROWS, :] = source[toks, col : col + LANES]
        hop_ref[s, 0, Q_AT : Q_AT + Q_ROWS, :] = q_ref[
            pl.ds((s % 2) * Q_ROWS, Q_ROWS), (s // 2) * LANES : (s // 2 + 1) * LANES
        ]
        hop_ref[s, 0, INFO_AT:HOP_ROWS, :] = tile
    kvb_ref[0, K_AT : K_AT + LEN, :] = k_ref[...]
    kvb_ref[0, V_AT : V_AT + LEN, :] = v_ref[...]
    kvb_ref[0, B_AT : B_AT + LEN, :] = b_ref[:, 0:LANES]
    kvb_ref[0, B_AT + LEN : B_AT + 2 * LEN, :] = b_ref[:, LANES : 2 * LANES]
    kvb_ref[0, DT_AT:G_ROWS, :] = dt_ref[...]


def pack(x, b, c, q, k, v, dt_rows, info):
    cols = lambda rows, width: pl.BlockSpec((rows, width), lambda m: (0, m))
    return pl.pallas_call(
        pack_kernel,
        grid=(MP,),
        in_specs=[
            cols(LEN, SEQ * LANES),
            cols(LEN, STATE),
            cols(LEN, STATE),
            cols(LEN, PER * LANES),
            cols(LEN, ATT_DIM),
            cols(LEN, ATT_DIM),
            pl.BlockSpec((16, LANES), lambda m: (m, 0)),
            pl.BlockSpec((8, LANES), lambda m: (0, 0)),
        ],
        out_specs=[
            pl.BlockSpec((SEQ, 1, HOP_ROWS, LANES), lambda m: (0, m, 0, 0)),
            pl.BlockSpec((1, G_ROWS, LANES), lambda m: (m, 0, 0)),
        ],
        out_shape=[
            jax.ShapeDtypeStruct((SEQ, MP, HOP_ROWS, LANES), BF16),
            jax.ShapeDtypeStruct((MP, G_ROWS, LANES), BF16),
        ],
        compiler_params=params(32),
        cost_estimate=pl.CostEstimate(flops=0, bytes_accessed=9 * MIB, transcendentals=0),
        name="pack",
    )(x, b, c, q, k, v, dt_rows, info)


def place_kernel(inv_ref, hop_ref, out_ref, sem):
    def start(p, carry):
        pltpu.make_async_copy(
            hop_ref.at[inv_ref[p], pl.ds(0, OWN_ROWS)], out_ref.at[p], sem
        ).start()
        return carry

    lax.fori_loop(0, STRETCHES, start, 0)
    pltpu.make_async_copy(out_ref, out_ref, sem).wait()


def place(inv, hop):
    return pl.pallas_call(
        place_kernel,
        grid_spec=pltpu.PrefetchScalarGridSpec(
            num_scalar_prefetch=1,
            grid=(),
            in_specs=[pl.BlockSpec(memory_space=pl.ANY)],
            out_specs=pl.BlockSpec(memory_space=pl.ANY),
            scratch_shapes=[pltpu.SemaphoreType.DMA],
        ),
        out_shape=jax.ShapeDtypeStruct((STRETCHES, OWN_ROWS, LANES), BF16),
        cost_estimate=pl.CostEstimate(flops=0, bytes_accessed=6 * MIB, transcendentals=0),
        name="place",
    )(inv, hop)


def doc_start(bounds_ref, pos):
    first = jnp.zeros_like(pos)
    for v in range(1, DOCS):
        first = jnp.maximum(first, jnp.where(bounds_ref[v] <= pos, bounds_ref[v], 0))
    return first


def next_doc(bounds_ref, pos):
    after = jnp.full_like(pos, TOKENS)
    for v in range(1, DOCS):
        after = jnp.minimum(after, jnp.where(bounds_ref[v] > pos, bounds_ref[v], TOKENS))
    return after


def running_sums(rows):
    width = rows.shape[1]
    upper = lax.broadcasted_iota(jnp.int32, (width, width), 0) <= lax.broadcasted_iota(
        jnp.int32, (width, width), 1
    )
    return lax.dot(
        rows, upper.astype(F32), precision=lax.Precision.HIGHEST, preferred_element_type=F32
    )


def mid_kernel(
    inv_ref,
    bounds_ref,
    gath_hbm,
    hop_hbm,
    step_ref,
    decay_ref,
    out_ref,
    gath,
    hop,
    sums,
    state,
    peak,
    total,
    acc,
    sem_g,
    sem_h,
):
    def start(p, carry):
        src = inv_ref[p]
        pltpu.make_async_copy(gath_hbm.at[src, pl.ds(0, DT_AT)], gath.at[p], sem_g).start()
        pltpu.make_async_copy(hop_hbm.at[src, pl.ds(0, INFO_AT)], hop.at[p], sem_h).start()
        return carry

    lax.fori_loop(0, STRETCHES, start, 0)
    sums[...] = running_sums(decay_ref[...].reshape(SEQ * 8, CHUNK)).reshape(SEQ, 8, CHUNK)
    state[...] = jnp.zeros_like(state)
    pltpu.make_async_copy(gath, gath, sem_g).wait()
    pltpu.make_async_copy(hop, hop, sem_h).wait()

    lane = lax.broadcasted_iota(jnp.int32, (1, LANES), 1)
    first_head = lane < HEAD_DIM

    def scan_chunk(c, carry):
        start_pos = c * CHUNK
        span = pl.ds(c * PER, PER)
        last_doc = doc_start(bounds_ref, start_pos + CHUNK - 1)
        log_sum = sums[c]
        log_end = log_sum[:, CHUNK - 1 : CHUNK]
        pos = lax.broadcasted_iota(jnp.int32, (8, CHUNK), 1) + start_pos
        weight = jnp.where(pos >= last_doc, step_ref[c] * jnp.exp(log_end - log_sum), 0.0)
        weight = jnp.transpose(weight)
        weight = jnp.where(first_head, weight[:, 0:1], weight[:, 1:2])
        xs = hop[span, 0:X_ROWS, :].reshape(CHUNK, LANES)
        driven = (weight * xs.astype(F32)).astype(BF16)
        keep = jnp.where(last_doc < start_pos, jnp.exp(log_end), 0.0)
        keep = jnp.where(first_head, keep[0:1, :], keep[1:2, :])
        out_ref[c, 0:STATE, :] = state[...].astype(BF16)
        for part in range(2):
            at = B_AT + part * LEN
            b_part = gath[span, at : at + LEN, :].reshape(CHUNK, LANES)
            added = lax.dot_general(
                b_part, driven, (((0,), (0,)), ((), ())), preferred_element_type=F32
            )
            rows = pl.ds(part * LANES, LANES)
            state[rows, :] = keep * state[rows, :] + added
        return carry

    lax.fori_loop(0, SEQ, scan_chunk, 0)

    half = bounds_ref[DOCS]
    q_rows = PER * Q_ROWS
    row = lax.broadcasted_iota(jnp.int32, (q_rows, 1), 0)
    in_chunk = (row // Q_ROWS) * LEN + half * Q_ROWS + row % Q_ROWS
    key_at = lax.broadcasted_iota(jnp.int32, (q_rows, CHUNK), 1)
    scale = ATT_DIM**-0.5 * 1.4426950408889634

    def attend_chunk(i, carry):
        span = pl.ds(i * PER, PER)
        queries = hop[span, Q_AT : Q_AT + Q_ROWS, :].reshape(q_rows, ATT_DIM)
        q_pos = i * CHUNK + in_chunk
        q_doc = doc_start(bounds_ref, q_pos)

        def scores_of(j):
            keys = gath[pl.ds(j * PER, PER), K_AT : K_AT + LEN, :].reshape(CHUNK, ATT_DIM)
            dots = lax.dot_general(
                queries, keys, (((1,), (1,)), ((), ())), preferred_element_type=F32
            )
            return dots * scale

        def mixed(probs, j):
            values = gath[pl.ds(j * PER, PER), V_AT : V_AT + LEN, :].reshape(CHUNK, ATT_DIM)
            return jnp.dot(probs.astype(BF16), values, preferred_element_type=F32)

        allowed = (key_at <= in_chunk) & (key_at >= q_doc - i * CHUNK)
        scores = jnp.where(allowed, scores_of(i), NEG_BIG)
        top = jnp.max(scores, axis=1, keepdims=True)
        probs = jnp.exp2(scores - top)
        peak[...] = top
        total[...] = jnp.sum(probs, axis=1, keepdims=True)
        acc[...] = mixed(probs, i)

        def one_tile(j, inner):
            scores = jnp.where(key_at >= q_doc - j * CHUNK, scores_of(j), NEG_BIG)
            old = peak[...]
            top = jnp.maximum(old, jnp.max(scores, axis=1, keepdims=True))
            probs = jnp.exp2(scores - top)
            factor = jnp.exp2(old - top)
            peak[...] = top
            total[...] = total[...] * factor + jnp.sum(probs, axis=1, keepdims=True)
            acc[...] = acc[...] * factor + mixed(probs, j)
            return inner

        lax.fori_loop(doc_start(bounds_ref, i * CHUNK) // CHUNK, i, one_tile, 0)
        out_ref[i, STATE:CHUNK, :] = (acc[...] / total[...]).astype(BF16)
        return carry

    lax.fori_loop(0, SEQ, attend_chunk, 0)


def mid(inv, bounds, gathered, hop, steps, decays):
    whole = lambda *shape: pl.BlockSpec(shape, lambda *_: (0,) * len(shape))
    return pl.pallas_call(
        mid_kernel,
        grid_spec=pltpu.PrefetchScalarGridSpec(
            num_scalar_prefetch=2,
            grid=(1,),
            in_specs=[
                pl.BlockSpec(memory_space=pl.ANY),
                pl.BlockSpec(memory_space=pl.ANY),
                whole(SEQ, 8, CHUNK),
                whole(SEQ, 8, CHUNK),
            ],
            out_specs=whole(SEQ, CHUNK, LANES),
            scratch_shapes=[
                pltpu.VMEM((STRETCHES, DT_AT, LANES), BF16),
                pltpu.VMEM((STRETCHES, INFO_AT, LANES), BF16),
                pltpu.VMEM((SEQ, 8, CHUNK), F32),
                pltpu.VMEM((STATE, LANES), F32),
                pltpu.VMEM((PER * Q_ROWS, 1), F32),
                pltpu.VMEM((PER * Q_ROWS, 1), F32),
                pltpu.VMEM((PER * Q_ROWS, ATT_DIM), F32),
                pltpu.SemaphoreType.DMA,
                pltpu.SemaphoreType.DMA,
            ],
        ),
        out_shape=jax.ShapeDtypeStruct((SEQ, CHUNK, LANES), BF16),
        compiler_params=params(40),
        cost_estimate=pl.CostEstimate(
            flops=8_000_000_000, bytes_accessed=16 * MIB, transcendentals=16 * MIB
        ),
        name="mid",
    )(inv, bounds, gathered, hop, steps, decays)


def own_kernel(
    bounds_ref,
    own_ref,
    state_ref,
    attn_ref,
    step_ref,
    decay_ref,
    gain_ref,
    ssm_ref,
    out_ref,
    proj,
    b_turned,
    grams,
    sums,
):
    pair = pl.program_id(0)
    base = bounds_ref[DOCS + 1] * CHUNK

    @pl.when(pair == 0)
    def _():
        for s in range(SEQ):
            piece = own_ref[s, :, X_ROWS:OWN_ROWS, :]
            proj[:, s // 4, :, (s % 4) * LANES : (s % 4 + 1) * LANES] = piece
        row = lax.broadcasted_iota(jnp.int32, (HALF, 1), 0)
        col = lax.broadcasted_iota(jnp.int32, (HALF, HALF), 1)
        for blk in range(2):
            part = proj[blk * 4 : blk * 4 + 4].reshape(HALF, 2 * STATE)
            b_blk, c_blk = part[:, :STATE], part[:, STATE:]
            gram = lax.dot_general(
                c_blk, b_blk, (((1,), (1,)), ((), ())), preferred_element_type=F32
            )
            pos = base + blk * HALF + row
            first = doc_start(bounds_ref, pos) - (base + blk * HALF)
            grams[blk] = jnp.where((col <= row) & (col >= first), gram, 0.0)
            if blk == 0:
                b_turned[...] = jnp.transpose(b_blk.astype(F32)).astype(BF16)
            part_sums = running_sums(
                decay_ref[:, :, blk * HALF : (blk + 1) * HALF].reshape(SEQ * 8, HALF)
            )
            sums[:, :, blk * HALF : (blk + 1) * HALF] = part_sums.reshape(SEQ, 8, HALF)
        for s in range(SEQ):
            for st in range(PER):
                at = st * LEN + (s % 2) * Q_ROWS
                out_ref[at : at + Q_ROWS, (s // 2) * LANES : (s // 2 + 1) * LANES] = attn_ref[
                    s, st * Q_ROWS : (st + 1) * Q_ROWS, :
                ]

    lane = lax.broadcasted_iota(jnp.int32, (1, LANES), 1)
    first_head = lane < HEAD_DIM
    both = lambda cols: jnp.where(first_head, cols[:, 0:1], cols[:, 1:2])
    log_sum = sums[pair]
    step = step_ref[pair]
    pos = lax.broadcasted_iota(jnp.int32, (8, CHUNK), 1) + base
    mid_pos = base + HALF - 1
    log_half = log_sum[:, HALF - 1 : HALF]
    load = jnp.where(pos >= doc_start(bounds_ref, mid_pos), jnp.exp(log_half - log_sum), 0.0)
    load = step * load
    reach_end = jnp.where(
        pos <= mid_pos,
        jnp.where(base > 0, next_doc(bounds_ref, base - 1), 0),
        next_doc(bounds_ref, mid_pos),
    )
    reach = jnp.where(pos < reach_end, jnp.exp(log_sum), 0.0)
    keep = jnp.where(
        (base > 0) & (doc_start(bounds_ref, mid_pos) < base), jnp.exp(log_half), 0.0
    )
    keep = jnp.where(first_head, keep[0:1, :], keep[1:2, :])
    step_col = jnp.transpose(step)
    sum_col = jnp.transpose(log_sum)
    reach_col = jnp.transpose(reach)
    load_col = jnp.transpose(load[:, :HALF])
    gain = gain_ref[pair][0:1, :]

    state_in = state_ref[0]
    for blk in range(2):
        rows = slice(blk * HALF, (blk + 1) * HALF)
        xs = own_ref[pair, blk * 4 : blk * 4 + 4, 0:X_ROWS, :].reshape(HALF, LANES).astype(F32)
        driven = (both(step_col[rows]) * xs).astype(BF16)
        c_blk = proj[blk * 4 : blk * 4 + 4, :, :, STATE:].reshape(HALF, STATE)
        gram = grams[blk]
        inner = []
        for head in range(2):
            gap = sum_col[rows, head : head + 1] - log_sum[head : head + 1, rows]
            mixing = (gram * jnp.exp(jnp.minimum(gap, 0.0))).astype(BF16)
            inner.append(jnp.dot(mixing, driven, preferred_element_type=F32))
        result = jnp.where(first_head, inner[0], inner[1])
        reached = jnp.dot(c_blk, state_in, preferred_element_type=F32)
        result = result + both(reach_col[rows]) * reached + gain * xs
        ssm_ref[rows, :] = result.astype(BF16)
        if blk == 0:
            loaded = (both(load_col) * xs).astype(BF16)
            added = jnp.dot(b_turned[...], loaded, preferred_element_type=F32)
            state_in = (keep * state_in.astype(F32) + added).astype(BF16)


def own(bounds, rows, mixed, steps, decays, gains):
    whole = lambda *shape: pl.BlockSpec(shape, lambda *_: (0,) * len(shape))
    return pl.pallas_call(
        own_kernel,
        grid_spec=pltpu.PrefetchScalarGridSpec(
            num_scalar_prefetch=1,
            grid=(SEQ,),
            in_specs=[
                whole(SEQ, PER, OWN_ROWS, LANES),
                pl.BlockSpec((1, STATE, LANES), lambda p, *_: (p, 0, 0)),
                pl.BlockSpec((SEQ, HALF, LANES), lambda p, *_: (0, 1, 0)),
                whole(SEQ, 8, CHUNK),
                whole(SEQ, 8, CHUNK),
                whole(SEQ, 8, LANES),
            ],
            out_specs=[
                pl.BlockSpec((CHUNK, LANES), lambda p, *_: (0, p)),
                whole(CHUNK, PER * LANES),
            ],
            scratch_shapes=[
                pltpu.VMEM((PER, 4, 16, 2 * STATE), BF16),
                pltpu.VMEM((STATE, HALF), BF16),
                pltpu.VMEM((2, HALF, HALF), F32),
                pltpu.VMEM((SEQ, 8, CHUNK), F32),
            ],
        ),
        out_shape=[
            jax.ShapeDtypeStruct((CHUNK, SEQ * LANES), BF16),
            jax.ShapeDtypeStruct((CHUNK, PER * LANES), BF16),
        ],
        compiler_params=params(40),
        cost_estimate=pl.CostEstimate(
            flops=4_000_000_000, bytes_accessed=10 * MIB, transcendentals=4 * MIB
        ),
        name="own",
    )(bounds, rows, mixed, mixed, steps, decays, gains)


def fold_steps(raw, bias, rate):
    step = jax.nn.softplus(raw.astype(F32) + bias[..., None])
    decay = -rate[..., None] * step
    widen = lambda rows: jnp.pad(rows, ((0, 0), (0, 6), (0, 0)))
    return widen(step), widen(decay)


def shards(
    stretch_x,
    stretch_bc,
    stretch_dt,
    stretch_q,
    stretch_kv,
    stretch_place,
    segment_ids,
    ssm_rate,
    dt_bias,
    skip_gain,
):
    seq_index = lax.axis_index("seq")
    mp_index = lax.axis_index("mp")
    exchange = functools.partial(lax.all_to_all, split_axis=0, concat_axis=0, tiled=True)

    my_docs = lax.dynamic_slice_in_dim(segment_ids, mp_index * LEN, LEN, 0)
    my_place = lax.dynamic_slice_in_dim(stretch_place, mp_index, 1, 0)
    info = jnp.concatenate([my_docs, my_place, jnp.zeros((LEN - 1,), jnp.int32)])
    info = jnp.broadcast_to(info.astype(F32)[None, :], (8, LANES))
    to_heads, to_groups = pack(
        stretch_x,
        stretch_bc[:, 0, :],
        stretch_bc[:, 1, :],
        stretch_q,
        stretch_kv[:, 0, :],
        stretch_kv[:, 1, :],
        stretch_dt.T.reshape(STRETCHES, LANES),
        info,
    )
    group_rows = exchange(to_groups, "mp")
    gathered = lax.all_gather(group_rows, "seq", axis=0, tiled=True)
    hop = exchange(to_heads.reshape(STRETCHES, HOP_ROWS, LANES), ("seq", "mp"))

    told = hop[:, INFO_AT, :].astype(jnp.int32)
    places, docs = told[:, LEN], told[:, :LEN]
    order = jnp.arange(STRETCHES, dtype=jnp.int32)
    inv = jnp.sum(jnp.where(places[None, :] == order[:, None], order[None, :], 0), axis=1)
    bounds = jnp.stack(
        [jnp.sum((docs < v).astype(jnp.int32)) for v in range(DOCS)]
        + [seq_index % 2, seq_index]
    )
    own_rows = exchange(place(inv, hop).reshape(SEQ, PER * OWN_ROWS, LANES), "seq")

    raw = gathered[:, DT_AT:G_ROWS, :]
    mine = lax.dynamic_index_in_dim(raw, seq_index, 1, False)
    chosen = (places[None, :] == order[:, None]).astype(BF16)
    pick = functools.partial(jnp.dot, preferred_element_type=F32)
    mine = pick(chosen, mine).reshape(SEQ, PER, 2, LEN)
    mine = jnp.transpose(mine, (0, 2, 1, 3)).reshape(SEQ, 2, CHUNK)
    heads = lambda vec, first, count: lax.dynamic_slice_in_dim(vec, first, count, 0)
    group_first = mp_index * (SSM_HEADS // GROUPS)
    head_first = group_first + seq_index * 2
    steps, decays = fold_steps(
        mine, heads(dt_bias, head_first, 2)[None], heads(ssm_rate, head_first, 2)[None]
    )
    mixed = exchange(mid(inv, bounds, gathered, hop, steps, decays), "seq")

    ours = pick(heads(chosen, seq_index * PER, PER), raw.reshape(STRETCHES, 16 * LANES))
    ours = ours.reshape(PER, SEQ, 2, LEN)
    ours = jnp.transpose(ours, (1, 2, 0, 3)).reshape(SEQ, 2, CHUNK)
    of_group = lambda vec: heads(vec, group_first, SSM_HEADS // GROUPS).reshape(SEQ, 2)
    own_steps, own_decays = fold_steps(ours, of_group(dt_bias), of_group(ssm_rate))
    gains = jnp.broadcast_to(
        jnp.repeat(of_group(skip_gain), HEAD_DIM, axis=1)[:, None, :], (SEQ, 8, LANES)
    )
    return own(
        bounds,
        own_rows.reshape(SEQ, PER, OWN_ROWS, LANES),
        mixed,
        own_steps,
        own_decays,
        gains,
    )


def solution(mesh):
    return jax.shard_map(
        shards,
        mesh=mesh,
        in_specs=(
            P(("seq", "mp"), None),
            P(("seq", "mp"), None, None),
            P(("seq", "mp"), None),
            P(("seq", "mp"), None),
            P(("seq", "mp"), None, None),
            P("seq"),
            P("seq"),
            P(),
            P(),
            P(),
        ),
        out_specs=(P("seq", "mp"), P("seq", "mp")),
        check_vma=False,
    )
```

time: 1670 us -> 324 us (0.19); the launches traced: 1640 us -> 325 us
  local copies, waits for them, and re-layouts: 523 us -> 26.2 us
  other arithmetic: 458 us -> 2.84 us
  matrix products: 383 us -> 1.74 us
  Pallas kernels: 0 us -> 161 us
  waiting for transfers between devices: 100 us -> 25.2 us
  starting transfers between devices: 72 us -> 12.3 us
  loops' own time: 44.5 us -> 0 us
  blocking collectives: 49 us -> 81.9 us
    dot_general x139 -> x2, matrix products: 345 us -> 1.74 us  [the longest x1 1.53 us: shards(): pick(heads(chosen, seq_index * PER, PER), raw.reshape(STRETCHES, 16 * LAN...]
    pallas_call x0 -> x4, Pallas kernels: none -> 161 us  [the longest x1 81.2 us: place(): pl.pallas_call(place_kernel, grid_spec=pltpu.PrefetchScalarGridSpec(num_s...]
    unnamed x7 -> x0, other arithmetic: 138 us -> none
    dynamic_update_slice x64 -> x0, local copies, waits for them, and re-layouts: 136 us -> none  [block_scan(): lax.scan(one_block, (state_start, seg_start), stacked)]
    dynamic_slice x179 -> x6, local copies, waits for them, and re-layouts: 122 us -> 1.71 us  [the longest x1 0.75 us: shards(): my_docs = lax.dynamic_slice_in_dim(segment_ids, mp_index * LEN, LEN, 0)]
    select_n x97 -> x0, other arithmetic: 82.9 us -> none  [the longest x32 53.7 us: one_block(): jnp.where((seg_blk == prev_seg)[:, None, None], jnp.exp(cumulative), 0.0)]
    all_to_all x13 -> x2, waiting for transfers between devices: 100 us -> 25.2 us  [the longest x1 25.2 us: shards(): mixed = exchange(mid(inv, bounds, gathered, hop, steps, decays), 'seq')]
    all_to_all x1 -> x2, blocking collectives: 7.82 us -> 81.9 us  [the longest x1 67.9 us: shards(): hop = exchange(to_heads.reshape(STRETCHES, HOP_ROWS, LANES), ('seq', 'mp'))]
  transfers between devices with their start and end apart: 15 -> 3, of which waited for: 7 -> 1; matrix products, arithmetic and copies ran while one was open for 82% -> 3% of each run, Pallas kernels for 0% -> 43%
where the time goes in v1:
time: 324 us; the launch traced here: 325 us
  Pallas kernels  161 us (50%)
  blocking collectives  81.9 us (25%)
  local copies, waits for them, and re-layouts  26.2 us (8%)
  waiting for transfers between devices  25.2 us (8%)
  between operations  14.3 us (4%)
  starting transfers between devices  12.3 us (4%)
    pallas_call x1, Pallas kernels, place(): pl.pallas_call(place_kernel, grid_spec=pltpu.PrefetchScalarGridSpec(num_s...  81.2 us
    all_to_all x1, blocking collectives, shards(): hop = exchange(to_heads.reshape(STRETCHES, HOP_ROWS, LANES), ('seq', 'mp'))  67.9 us
    pallas_call x1, Pallas kernels, mid(): pl.pallas_call(mid_kernel, grid_spec=pltpu.PrefetchScalarGridSpec(num_sca...  57.1 us
    all_to_all x1, waiting for transfers between devices, shards(): mixed = exchange(mid(inv, bounds, gathered, hop, steps, decays), 'seq')  25.2 us
    pallas_call x1, Pallas kernels, own(): pl.pallas_call(own_kernel, grid_spec=pltpu.PrefetchScalarGridSpec(num_sca...  21.1 us
    all_to_all x1, blocking collectives, shards(): group_rows = exchange(to_groups, 'mp')  14 us
    unnamed x22, local copies, waits for them, and re-layouts  8.74 us
    all_to_all x1, starting transfers between devices, shards(): mixed = exchange(mid(inv, bounds, gathered, hop, steps, decays), 'seq')  7.39 us
  transfers between devices with their start and end apart: 3, of which 1 were waited for; matrix products, arithmetic and copies ran while one was open for 3% of the time, Pallas kernels for 43%

profile of v1, /device:TPU:2, one launch (start us, length us, event | category | flops | bytes accessed | tf_op | source)
XLA Modules:
  0.0 325.3 jit_solution(3496166917889160751)
XLA Ops:
  7.2 0.0 copy-start.10
  7.2 0.0 all-gather.2.cloned.1.call-start
  7.2 0.9 copy.36
  8.1 0.1 reshape.85.dt_ref
  8.2 0.0 copy-start.3
  8.2 2.3 fusion.8
  10.5 2.9 fusion.7
  13.5 0.8 dynamic_slice.28
  14.2 0.0 copy-done.10
  14.2 0.6 dynamic_slice.29
  14.9 1.0 copy_bitcast_fusion.2
  15.9 1.3 copy_bitcast_fusion
  17.3 0.7 add_convert_fusion
  18.0 0.0 copy-done.3
  18.0 1.2 copy-done.5
  19.2 1.6 pack.1
  20.8 0.0 copy-start.2
  20.8 2.0 copy-done.2
  22.8 14.0 %all_to_all.20 = bf16[8,272,128]{2,1,0:T(8,128)(2,1)} all-to-all(bf16[8,272,128]{2,1,0:T(8,128)(2,1)S(1)} %get-tuple-element.5), channel_id=1, replica_groups=mesh['seq'=16,'mp'=8] {'mp'}, dimensions={0} | all-to-all | bytes 1114112 | tf_op jit(solution)/shard_map/all_to_all | solution.py:463
  36.8 0.0 all-gather.2.cloned.1.call-update
  36.8 67.9 %all_to_all.21.hop_ref.hop_hbm = bf16[128,128,128]{2,1,0:T(8,128)(2,1)S(1)} all-to-all(bf16[128,128,128]{2,1,0:T(8,128)(2,1)} %bitcast.54), channel_id=1, replica_groups=mesh['seq'=16,'mp'=8] {'seq','mp'}, dimensions={0} | all-to-all | bytes 8388608 | tf_op jit(solution)/shard_map/all_to_all | solution.py:465
  104.7 2.0 copy-done
  106.7 0.1 slice_convert_fusion
  106.8 0.2 slice_reduce_fusion
  106.9 0.7 select_reduce_fusion.inv_ref
  107.6 81.2 %place.1 = bf16[128,80,128]{2,1,0:T(8,128)(2,1)} custom-call(s32[128]{0:T(128)} %select_reduce_fusion.inv_ref, bf16[128,128,128]{2,1,0:T(8,128)(2,1)} %copy-done), custom_call_target="tpu_custom_call" | custom-call | bytes 6291456 | tf_op jit(solution)/shard_map/place/pallas_call | solution.py:109
  188.8 0.0 copy-start.7
  188.8 0.0 copy-start.9
  188.8 4.8 %all-to-all-start.1 = ((bf16[16,640,128]{2,1,0:T(8,128)(2,1)}), bf16[16,640,128]{2,1,0:T(8,128)(2,1)S(1)}, u32[]{:S(2)}, u32[]{:S(2)}) async-start(bf16[16,640,128]{2,1,0:T(8,128)(2,1)} %bitcast.56), calls=%async_computation.1 | async-start | bytes 5242880 | tf_op jit(solution)/shard_map/all_to_all | solution.py:475
  193.7 0.0 copy-start.6
  193.7 0.0 copy-done.7
  193.7 0.1 dynamic_slice.31
  193.8 0.0 copy-done.9
  193.8 0.1 dynamic-slice_negate_fusion.1
  193.9 0.8 convert_reduce_fusion
  194.6 3.8 %stack.35.bounds_ref = s32[8]{0:T(128)S(1)} concatenate(s32[1]{0:T(128)} %bitcast.7, s32[1]{0:T(128)} %bitcast.8, s32[1]{0:T(128)} %bitcast.9, s32[1]{0:T(128)} %bitcast.10, s32[1]{0:T(128)} %bitcast.11, s32[1]{0:T(128)} %bitcast.12, s32[1]{0:T(128)} %bitcast.13, s32[1]{0:T(128)} %bitcast.14), dimensions={0} | concatenate | bytes 64 | tf_op jit(solution)/shard_map/stack | solution.py:471
  198.4 1.1 slice.35
  199.5 0.1 constant_dynamic-slice_fusion
  199.6 0.1 copy.49
  199.7 0.2 convolution_bitcast_fusion.1
  199.9 0.1 reshape.89
  200.1 0.2 broadcast_multiply_fusion
  200.4 0.0 copy-done.6
  200.4 0.0 copy-start.1
  200.4 2.2 copy-done.1
  202.6 57.1 %mid.1 = bf16[16,512,128]{2,1,0:T(8,128)(2,1)S(1)} custom-call(s32[128]{0:T(128)S(1)} %copy-done.6, s32[8]{0:T(128)S(1)} %stack.35.bounds_ref, bf16[128,272,128]{2,1,0:T(8,128)(2,1)} %all-gather.2.cloned.1.call-done.gath_hbm, bf16[128,128,128]{2,1,0:T(8,128)(2,1)S(1)} %copy-done.1, f32[16,8,512]{2,1,0:T(8,128)S(1)} %pad.13.step_ref, ...), custom_call_target="tpu_custom_call" | custom-call | flops 8000000000 | bytes 16777216 | tf_op jit(solution)/shard_map/mid/pallas_call | solution.py:260
  259.6 0.0 copy-start.4
  259.6 1.3 copy-done.4
  260.9 0.0 all-to-all-done.1
  260.9 7.4 %all-to-all-start.3 = ((bf16[16,512,128]{2,1,0:T(8,128)(2,1)}), bf16[16,512,128]{2,1,0:T(8,128)(2,1)}, u32[]{:S(2)}, u32[]{:S(2)}) async-start(bf16[16,512,128]{2,1,0:T(8,128)(2,1)} %copy-done.4), calls=%async_computation.3 | async-start | bytes 4194304 | tf_op jit(solution)/shard_map/all_to_all | solution.py:489
  268.3 0.1 dynamic_slice.34
  268.4 0.1 dynamic_slice.36
  268.5 0.1 add.77
  268.6 0.1 dynamic-slice_negate_fusion
  268.7 0.1 neg.26
  268.7 0.1 reshape.92
  268.8 0.1 broadcast_in_dim.38
  268.9 0.1 broadcast_in_dim.39
  269.0 1.2 copy.39
  270.3 1.5 convolution_bitcast_fusion
  271.8 0.1 reshape.91
  271.9 0.2 broadcast_multiply_fusion.1
  272.2 25.2 %all-to-all-done.3.state_ref.attn_ref = bf16[16,512,128]{2,1,0:T(8,128)(2,1)} async-done(((bf16[16,512,128]{2,1,0:T(8,128)(2,1)}), bf16[16,512,128]{2,1,0:T(8,128)(2,1)}, u32[]{:S(2)}, u32[]{:S(2)}) %all-to-all-start.3) | async-done | bytes 2097184 | tf_op jit(solution)/shard_map/all_to_all | solution.py:489
  297.4 21.1 %own.1 = (bf16[512,2048]{1,0:T(8,128)(2,1)}, bf16[512,1024]{1,0:T(8,128)(2,1)}) custom-call(s32[8]{0:T(128)S(1)} %stack.35.bounds_ref, bf16[16,8,80,128]{3,2,1,0:T(8,128)(2,1)S(1)} %bitcast.55, bf16[16,512,128]{2,1,0:T(8,128)(2,1)} %all-to-all-done.3.state_ref.attn_ref, bf16[16,512,128]{2,1,0:T(8,128)(2,1)} %all-to-all-done.3.state_ref.attn_ref, ...), custom_call_target="tpu_custom_call" | custom-call | flops 4000000000 | bytes 10485760 | tf_op jit(solution)/shard_map/own/pallas_call | solution.py:390
  (14 shorter events, 0.1 us)
Async XLA Ops:
  7.2 7.1 %copy-start.10 = (s32[8]{0:T(128)S(1)}, s32[8]{0:T(128)}, u32[]{:S(2)}) copy-start(s32[8]{0:T(128)} %param.15) | copy-start | bytes 100
  7.2 191.2 %all-gather.2.cloned.1.call-start = ((), (), s32[]{:S(2)}) async-start(), calls=%async_computation.4 | async-start | bytes 9469952 | tf_op jit(solution)/shard_map/all_gather | solution.py:464
  8.2 9.8 %copy-start.3 = (bf16[64,16384]{1,0:T(8,128)(2,1)S(1)}, bf16[64,16384]{1,0:T(8,128)(2,1)}, u32[]{:S(2)}) copy-start(bf16[64,16384]{1,0:T(8,128)(2,1)} %x_ref.1) | copy-start | bytes 6291460
  18.0 1.2 copy-start.5
  20.8 2.0 copy-start.2
  104.7 2.0 copy-start
  188.8 4.9 %copy-start.7 = (f32[256]{0:T(256)S(1)}, f32[256]{0:T(256)}, u32[]{:S(2)}) copy-start(f32[256]{0:T(256)} %param.18) | copy-start | bytes 3076
  188.8 5.0 %copy-start.9 = (f32[256]{0:T(256)S(1)}, f32[256]{0:T(256)}, u32[]{:S(2)}) copy-start(f32[256]{0:T(256)} %param.17) | copy-start | bytes 3076
  188.8 72.1 %all-to-all-start.1 = ((bf16[16,640,128]{2,1,0:T(8,128)(2,1)}), bf16[16,640,128]{2,1,0:T(8,128)(2,1)S(1)}, u32[]{:S(2)}, u32[]{:S(2)}) async-start(bf16[16,640,128]{2,1,0:T(8,128)(2,1)} %bitcast.56), calls=%async_computation.1 | async-start | bytes 5242880 | tf_op jit(solution)/shard_map/all_to_all | solution.py:475
  193.7 6.7 %copy-start.6 = (s32[128]{0:T(128)S(1)}, s32[128]{0:T(128)}, u32[]{:S(2)}) copy-start(s32[128]{0:T(128)} %select_reduce_fusion.inv_ref) | copy-start | bytes 1540
  200.4 2.2 copy-start.1
  259.6 1.3 copy-start.4
  260.9 7.5 %copy-start.8 = (f32[256]{0:T(256)S(1)}, f32[256]{0:T(256)}, u32[]{:S(2)}) copy-start(f32[256]{0:T(256)} %param.19) | copy-start | bytes 3076
  260.9 36.5 %all-to-all-start.3 = ((bf16[16,512,128]{2,1,0:T(8,128)(2,1)}), bf16[16,512,128]{2,1,0:T(8,128)(2,1)}, u32[]{:S(2)}, u32[]{:S(2)}) async-start(bf16[16,512,128]{2,1,0:T(8,128)(2,1)} %copy-done.4), calls=%async_computation.3 | async-start | bytes 4194304 | tf_op jit(solution)/shard_map/all_to_all | solution.py:489
Sparse Core Ops, SparseCore 0:
  36.9 115.6 all-gather.1

commit v2 on v1

v2 whole, which is shorter than its diff:
```python
import functools

import jax
import jax.numpy as jnp
from jax import lax
from jax.experimental import pallas as pl
from jax.experimental.pallas import tpu as pltpu
from jax.sharding import PartitionSpec as P

SSM_HEADS = 256
HEAD_DIM = 64
STATE = 256
GROUPS = 8
Q_HEADS = 64
KV_HEADS = 8
ATT_DIM = 128
LEN = 64
SEQ = 16
MP = 8
STRETCHES = 128
CHUNK = 512
HALF = 256
PER = CHUNK // LEN
LANES = 128
DOCS = 6
TOKENS = 8192

X_ROWS = LEN
BC_ROWS = 16
Q_ROWS = 32
BC_AT = X_ROWS
Q_AT = BC_AT + BC_ROWS
INFO_AT = Q_AT + Q_ROWS
HOP_ROWS = INFO_AT + 16
OWN_ROWS = X_ROWS + BC_ROWS
OWNER_ROWS = PER * OWN_ROWS + 16
K_AT, V_AT, G_ROWS = 0, 64, 128
GROUP_HEADS = SSM_HEADS // GROUPS
PAIRS = 2
NEG_BIG = -1e30
F32 = jnp.float32
BF16 = jnp.bfloat16
MIB = 1 << 20


def params(mib):
    return pltpu.CompilerParams(vmem_limit_bytes=mib * MIB)


def pack_kernel(x_ref, bc_ref, q_ref, dt_ref, info_ref, hop_ref):
    row = lax.broadcasted_iota(jnp.int32, (16, LANES), 0)
    told = jnp.where(row == 0, jnp.broadcast_to(info_ref[0:1, :], (16, LANES)), 0.0)
    raw = dt_ref[...].astype(F32)
    for s in range(SEQ):
        hop_ref[s, 0, 0:X_ROWS, :] = x_ref[:, s * LANES : (s + 1) * LANES]
        col = (s % 2) * LANES
        hop_ref[s, 0, BC_AT : BC_AT + BC_ROWS, :] = bc_ref[
            pl.ds((s // 4) * 16, 16), (s % 4) // 2, col : col + LANES
        ]
        hop_ref[s, 0, Q_AT : Q_AT + Q_ROWS, :] = q_ref[
            pl.ds((s % 2) * Q_ROWS, Q_ROWS), (s // 2) * LANES : (s // 2 + 1) * LANES
        ]
        tile = jnp.where(row == 1, jnp.broadcast_to(raw[s : s + 1, :], (16, LANES)), told)
        hop_ref[s, 0, INFO_AT:HOP_ROWS, :] = tile.astype(BF16)


def pack(x, bc, q, dt_rows, info):
    cols = lambda width: pl.BlockSpec((LEN, width), lambda m: (0, m))
    return pl.pallas_call(
        pack_kernel,
        grid=(MP,),
        in_specs=[
            cols(SEQ * LANES),
            pl.BlockSpec((LEN, 2, STATE), lambda m: (0, 0, m)),
            cols(PER * LANES),
            pl.BlockSpec((16, LANES), lambda m: (m, 0)),
            pl.BlockSpec((8, LANES), lambda m: (0, 0)),
        ],
        out_specs=pl.BlockSpec((SEQ, 1, HOP_ROWS, LANES), lambda m: (0, m, 0, 0)),
        out_shape=jax.ShapeDtypeStruct((SEQ, MP, HOP_ROWS, LANES), BF16),
        compiler_params=params(32),
        cost_estimate=pl.CostEstimate(flops=0, bytes_accessed=9 * MIB, transcendentals=0),
        name="pack",
    )(x, bc, q, dt_rows, info)


def pack_kv_kernel(kv_ref, out_ref):
    for m in range(MP):
        for half in range(2):
            out_ref[m, half * LEN : (half + 1) * LEN, :] = kv_ref[
                :, half, m * ATT_DIM : (m + 1) * ATT_DIM
            ]


def pack_kv(kv):
    return pl.pallas_call(
        pack_kv_kernel,
        grid=(1,),
        in_specs=[pl.BlockSpec((LEN, 2, KV_HEADS * ATT_DIM), lambda _: (0, 0, 0))],
        out_specs=pl.BlockSpec((MP, G_ROWS, LANES), lambda _: (0, 0, 0)),
        out_shape=jax.ShapeDtypeStruct((MP, G_ROWS, LANES), BF16),
        compiler_params=params(16),
        name="pack_kv",
    )(kv)


def place_kernel(inv_ref, hop_ref, out_ref, q_ref):
    lane = lax.broadcasted_iota(jnp.int32, (1, LANES), 1)
    early = lane < LEN
    row = lax.broadcasted_iota(jnp.int32, (16, LANES), 0)

    def chunk(c, carry):
        raw = []
        for k in range(PER):
            src = inv_ref[c * PER + k]
            out_ref[c, k * OWN_ROWS : (k + 1) * OWN_ROWS, :] = hop_ref[src, 0:OWN_ROWS, :]
            q_ref[c, k * Q_ROWS : (k + 1) * Q_ROWS, :] = hop_ref[src, Q_AT : Q_AT + Q_ROWS, :]
            raw.append(hop_ref[src, INFO_AT:HOP_ROWS, :].astype(F32)[1:2, :])
        turned = [jnp.roll(r, LEN, axis=1) for r in raw]
        tile = jnp.zeros((16, LANES), F32)
        for q in range(4):
            first = jnp.where(early, raw[2 * q], turned[2 * q + 1])
            second = jnp.where(early, turned[2 * q], raw[2 * q + 1])
            tile = jnp.where(row == q, first, jnp.where(row == 4 + q, second, tile))
        out_ref[c, PER * OWN_ROWS : OWNER_ROWS, :] = tile.astype(BF16)
        return carry

    lax.fori_loop(0, SEQ, chunk, 0)


def place(inv, hop):
    return pl.pallas_call(
        place_kernel,
        grid_spec=pltpu.PrefetchScalarGridSpec(
            num_scalar_prefetch=1,
            grid=(1,),
            in_specs=[pl.BlockSpec((STRETCHES, HOP_ROWS, LANES), lambda *_: (0, 0, 0))],
            out_specs=[
                pl.BlockSpec((SEQ, OWNER_ROWS, LANES), lambda *_: (0, 0, 0)),
                pl.BlockSpec((SEQ, PER * Q_ROWS, LANES), lambda *_: (0, 0, 0)),
            ],
        ),
        out_shape=[
            jax.ShapeDtypeStruct((SEQ, OWNER_ROWS, LANES), BF16),
            jax.ShapeDtypeStruct((SEQ, PER * Q_ROWS, LANES), BF16),
        ],
        compiler_params=params(24),
        cost_estimate=pl.CostEstimate(flops=0, bytes_accessed=6 * MIB, transcendentals=0),
        name="place",
    )(inv, hop)


def doc_start(bounds_ref, pos):
    first = jnp.zeros_like(pos)
    for v in range(1, DOCS):
        first = jnp.maximum(first, jnp.where(bounds_ref[v] <= pos, bounds_ref[v], 0))
    return first


def next_doc(bounds_ref, pos):
    after = jnp.full_like(pos, TOKENS)
    for v in range(1, DOCS):
        after = jnp.minimum(after, jnp.where(bounds_ref[v] > pos, bounds_ref[v], TOKENS))
    return after


def running_sums(rows):
    width = rows.shape[1]
    upper = lax.broadcasted_iota(jnp.int32, (width, width), 0) <= lax.broadcasted_iota(
        jnp.int32, (width, width), 1
    )
    return lax.dot(
        rows, upper.astype(F32), precision=lax.Precision.HIGHEST, preferred_element_type=F32
    )


def whole(*shape):
    return pl.BlockSpec(shape, lambda *_: (0,) * len(shape))


SUM_ROWS = 16


def attend_kernel(
    inv_ref, bounds_ref, kv_hbm, q_hbm, out_ref, kv_ref, q_ref, keys_all, turned, peak, acc, top_far, acc_far, sems
):
    kv_copy = pltpu.make_async_copy(kv_hbm, kv_ref, sems.at[0])
    q_copy = pltpu.make_async_copy(q_hbm, q_ref, sems.at[1])
    kv_copy.start()
    q_copy.start()
    half = bounds_ref[DOCS]
    q_rows = PER * Q_ROWS

    def arrange(i, carry):
        values = []
        for k in range(PER):
            src = inv_ref[i * PER + k]
            keys_all[pl.ds(i * CHUNK + k * LEN, LEN), :] = kv_ref[src, K_AT : K_AT + LEN, :]
            values.append(kv_ref[src, V_AT : V_AT + LEN, :])
        turned[i, 0:ATT_DIM, :] = jnp.transpose(jnp.concatenate(values, axis=0))
        turned[i, ATT_DIM : ATT_DIM + SUM_ROWS, :] = jnp.ones((SUM_ROWS, CHUNK), BF16)
        return carry

    kv_copy.wait()
    lax.fori_loop(0, SEQ, arrange, 0, unroll=2)
    q_copy.wait()

    row = lax.broadcasted_iota(jnp.int32, (1, q_rows), 1)
    in_chunk = (row // Q_ROWS) * LEN + half * Q_ROWS + row % Q_ROWS
    key_at = lax.broadcasted_iota(jnp.int32, (CHUNK, q_rows), 0)
    scale = ATT_DIM**-0.5 * 1.4426950408889634

    def scores_of(queries, j):
        keys = keys_all[pl.ds(pl.multiple_of(j * CHUNK, CHUNK), CHUNK), :]
        return lax.dot_general(
            keys, queries, (((1,), (1,)), ((), ())), preferred_element_type=F32
        )

    def mixed(scores, top, j):
        probs = jnp.exp2((scores - top) * scale)
        return jnp.dot(turned[j], probs.astype(BF16), preferred_element_type=F32)

    def peak_of(scores):
        return jnp.max(scores, axis=0, keepdims=True)

    def near_tiles(i, carry):
        queries = q_ref[i]
        first = doc_start(bounds_ref, i * CHUNK + in_chunk) - i * CHUNK
        before = jnp.maximum(i - 1, 0)
        own = (key_at <= in_chunk) & (key_at >= first)
        here = jnp.where(own, scores_of(queries, i), NEG_BIG)
        there = jnp.where(key_at >= first + CHUNK, scores_of(queries, before), NEG_BIG)
        top = jnp.maximum(peak_of(here), peak_of(there))
        peak[i] = top
        acc[i] = mixed(here, top, i) + mixed(there, top, before)
        return carry

    lax.fori_loop(0, SEQ, near_tiles, 0, unroll=2)

    def far_tiles(i, carry):
        first = doc_start(bounds_ref, i * CHUNK) // CHUNK
        last_doc = doc_start(bounds_ref, i * CHUNK + CHUNK - 1)
        end = jnp.maximum(i - 1, first)
        clear = jnp.clip((last_doc + CHUNK - 1) // CHUNK, first, end)
        n_clear = (end - clear) // 2
        clear = end - 2 * n_clear
        n_mask = (clear - first) // 2

        queries = q_ref[i]
        q_doc = doc_start(bounds_ref, i * CHUNK + in_chunk)

        def add_tiles(js, masks):
            old = top_far[...]
            scores = [scores_of(queries, j) for j in js]
            if masks:
                scores = [
                    jnp.where(key_at >= q_doc - j * CHUNK, s, NEG_BIG) for s, j in zip(scores, js)
                ]
            top = old
            for s in scores:
                top = jnp.maximum(top, peak_of(s))
            top_far[...] = top
            added = sum(mixed(s, top, j) for s, j in zip(scores, js))
            acc_far[...] = acc_far[...] * jnp.exp2((old - top) * scale) + added

        top_far[...] = peak[i]
        acc_far[...] = acc[i]

        @pl.when((clear - first) % 2 == 1)
        def _():
            add_tiles([first], True)

        def masked(t, c):
            j = clear - 2 * n_mask + 2 * t
            add_tiles([j, j + 1], True)
            return c

        def plain(t, c):
            j = clear + 2 * t
            add_tiles([j, j + 1], False)
            return c

        lax.fori_loop(0, n_mask, masked, 0)
        lax.fori_loop(0, n_clear, plain, 0)
        acc[i] = acc_far[...]
        return carry

    lax.fori_loop(2, SEQ, far_tiles, 0)

    def finish(i, carry):
        result = acc[i, 0:ATT_DIM, :] / acc[i, ATT_DIM : ATT_DIM + 1, :]
        out_ref[i, STATE:CHUNK, :] = jnp.transpose(result).astype(BF16)
        return carry

    lax.fori_loop(0, SEQ, finish, 0, unroll=4)


def attend(inv, bounds, kv, queries):
    return pl.pallas_call(
        attend_kernel,
        grid_spec=pltpu.PrefetchScalarGridSpec(
            num_scalar_prefetch=2,
            grid=(1,),
            in_specs=[pl.BlockSpec(memory_space=pl.ANY), pl.BlockSpec(memory_space=pl.ANY)],
            out_specs=whole(SEQ, CHUNK, LANES),
            scratch_shapes=[
                pltpu.VMEM((STRETCHES, G_ROWS, LANES), BF16),
                pltpu.VMEM((SEQ, PER * Q_ROWS, LANES), BF16),
                pltpu.VMEM((TOKENS, ATT_DIM), BF16),
                pltpu.VMEM((SEQ, ATT_DIM + SUM_ROWS, CHUNK), BF16),
                pltpu.VMEM((SEQ, 1, PER * Q_ROWS), F32),
                pltpu.VMEM((SEQ, ATT_DIM + SUM_ROWS, PER * Q_ROWS), F32),
                pltpu.VMEM((1, PER * Q_ROWS), F32),
                pltpu.VMEM((ATT_DIM + SUM_ROWS, PER * Q_ROWS), F32),
                pltpu.SemaphoreType.DMA((2,)),
            ],
        ),
        out_shape=jax.ShapeDtypeStruct((SEQ, CHUNK, LANES), BF16),
        compiler_params=params(60),
        cost_estimate=pl.CostEstimate(flops=8_000_000_000, bytes_accessed=6 * MIB, transcendentals=8 * MIB),
        name="attend",
    )(inv, bounds, kv, queries)


def pair_lanes(first, width, rows):
    row = lax.broadcasted_iota(jnp.int32, (rows, width), 0) % GROUP_HEADS
    lane = lax.broadcasted_iota(jnp.int32, (rows, width), 1)
    return (row == first + lane // (width // 2)).astype(BF16)


def as_parts(rows, count):
    left = jnp.transpose(rows)
    parts = []
    for _ in range(count):
        part = left.astype(BF16)
        parts.append(part)
        left = left - part.astype(F32)
    return jnp.concatenate(parts, axis=1)


def spread_heads(parts, pair, width):
    sel = pair_lanes(2 * pair, width, parts.shape[1])
    return jnp.dot(parts, sel, preferred_element_type=F32)


def channels(own_ref, pair):
    parts = [own_ref[pair, st * OWN_ROWS : st * OWN_ROWS + X_ROWS, :] for st in range(PER)]
    return jnp.concatenate(parts, axis=0).astype(F32)


def gather_proj(own_ref, proj, group):
    for tg in range(4):
        for cg in range(2):
            for st in range(PER):
                at = st * OWN_ROWS + X_ROWS
                proj[st, tg, :, cg * LANES : (cg + 1) * LANES] = own_ref[
                    tg * 4 + group * 2 + cg, at : at + BC_ROWS, :
                ]


def softplus(v):
    return jnp.maximum(v, 0.0) + jnp.log1p(jnp.exp(-jnp.abs(v)))


def ends_kernel(bounds_ref, own_ref, bias_ref, rate_ref, out_ref, step_ref, decay_ref, proj, turned, parts):
    base = bounds_ref[DOCS + 1] * CHUNK

    @pl.when(pl.program_id(0) == 0)
    def _():
        for s in range(SEQ):
            tile = own_ref[s, PER * OWN_ROWS : OWNER_ROWS, :].astype(F32)
            for head in range(2):
                for q in range(4):
                    step_ref[2 * s + head : 2 * s + head + 1, q * LANES : (q + 1) * LANES] = tile[
                        4 * head + q : 4 * head + q + 1, :
                    ]
        step_ref[...] = softplus(step_ref[...] + bias_ref[...])
        decay_ref[...] = -rate_ref[...] * step_ref[...]
        gather_proj(own_ref, proj, 0)
        turned[...] = jnp.transpose(proj[...].reshape(CHUNK, STATE))
        log_sum = running_sums(decay_ref[...])
        pos = lax.broadcasted_iota(jnp.int32, (GROUP_HEADS, CHUNK), 1) + base
        last_doc = doc_start(bounds_ref, base + CHUNK - 1)
        load = jnp.exp(log_sum[:, CHUNK - 1 : CHUNK] - log_sum)
        parts[...] = as_parts(jnp.where(pos >= last_doc, step_ref[...] * load, 0.0), 2)

    for k in range(PAIRS):
        pair = pl.program_id(0) * PAIRS + k
        xs = channels(own_ref, pair)
        driven = (spread_heads(parts[...], pair, LANES) * xs).astype(BF16)
        out_ref[k] = jnp.dot(turned[...], driven, preferred_element_type=F32).astype(BF16)


def ends(bounds, rows, biases, rates):
    return pl.pallas_call(
        ends_kernel,
        grid_spec=pltpu.PrefetchScalarGridSpec(
            num_scalar_prefetch=1,
            grid=(SEQ // PAIRS,),
            in_specs=[
                whole(SEQ, OWNER_ROWS, LANES),
                whole(GROUP_HEADS, 1),
                whole(GROUP_HEADS, 1),
            ],
            out_specs=[
                pl.BlockSpec((PAIRS, STATE, LANES), lambda g, *_: (g, 0, 0)),
                whole(GROUP_HEADS, CHUNK),
                whole(GROUP_HEADS, CHUNK),
            ],
            scratch_shapes=[
                pltpu.VMEM((PER, 4, 16, STATE), BF16),
                pltpu.VMEM((STATE, CHUNK), BF16),
                pltpu.VMEM((CHUNK, 2 * GROUP_HEADS), BF16),
            ],
        ),
        out_shape=[
            jax.ShapeDtypeStruct((SEQ, STATE, LANES), BF16),
            jax.ShapeDtypeStruct((GROUP_HEADS, CHUNK), F32),
            jax.ShapeDtypeStruct((GROUP_HEADS, CHUNK), F32),
        ],
        compiler_params=params(24),
        cost_estimate=pl.CostEstimate(
            flops=1_000_000_000, bytes_accessed=4 * MIB, transcendentals=0
        ),
        name="ends",
    )(bounds, rows, biases, rates)


def chain_kernel(bounds_ref, ends_ref, total_ref, both_in, both_out, states, sem):
    state = jnp.zeros((STATE, LANES), F32)
    for c in range(SEQ):
        states[c] = state.astype(BF16)
        if c < SEQ - 1:
            last_doc = doc_start(bounds_ref, jnp.int32((c + 1) * CHUNK - 1))
            keep = jnp.where(last_doc < c * CHUNK, total_ref[c : c + 1, :], 0.0)
            state = keep * state + ends_ref[c].astype(F32)
    copy = pltpu.make_async_copy(states, both_out.at[:, pl.ds(0, STATE), :], sem)
    copy.start()
    copy.wait()


def chain(bounds, arrived, totals, both):
    return pl.pallas_call(
        chain_kernel,
        grid_spec=pltpu.PrefetchScalarGridSpec(
            num_scalar_prefetch=1,
            grid=(1,),
            in_specs=[
                whole(SEQ, STATE, LANES),
                whole(SEQ, LANES),
                pl.BlockSpec(memory_space=pl.ANY),
            ],
            out_specs=pl.BlockSpec(memory_space=pl.ANY),
            scratch_shapes=[pltpu.VMEM((SEQ, STATE, LANES), BF16), pltpu.SemaphoreType.DMA],
        ),
        out_shape=jax.ShapeDtypeStruct((SEQ, CHUNK, LANES), BF16),
        input_output_aliases={3: 0},
        compiler_params=params(60),
        cost_estimate=pl.CostEstimate(flops=0, bytes_accessed=3 * MIB, transcendentals=0),
        name="chain",
    )(bounds, arrived, totals, both)


def inner_kernel(
    bounds_ref,
    own_ref,
    step_ref,
    decay_ref,
    gain_ref,
    out_ref,
    c_out,
    reach_out,
    proj_b,
    proj_c,
    turned,
    grams,
    sums,
    sum_rows,
    sum_parts,
    step_parts,
    load_parts,
    reach_parts,
):
    base = bounds_ref[DOCS + 1] * CHUNK

    @pl.when(pl.program_id(0) == 0)
    def _():
        gather_proj(own_ref, proj_b, 0)
        gather_proj(own_ref, proj_c, 1)
        row = lax.broadcasted_iota(jnp.int32, (HALF, 1), 0)
        col = lax.broadcasted_iota(jnp.int32, (HALF, HALF), 1)
        for blk in range(2):
            b_blk = proj_b[blk * 4 : blk * 4 + 4].reshape(HALF, STATE)
            c_blk = proj_c[blk * 4 : blk * 4 + 4].reshape(HALF, STATE)
            c_out[blk * HALF : (blk + 1) * HALF, :] = c_blk
            gram = lax.dot_general(
                c_blk, b_blk, (((1,), (1,)), ((), ())), preferred_element_type=F32
            )
            start = base + blk * HALF
            first = doc_start(bounds_ref, start + row) - start
            grams[blk] = jnp.where((col <= row) & (col >= first), gram, 0.0)
            if blk == 0:
                turned[...] = jnp.transpose(b_blk)
            sums[:, blk * HALF : (blk + 1) * HALF] = running_sums(
                decay_ref[:, blk * HALF : (blk + 1) * HALF]
            )
        log_sum = sums[...]
        for head in range(GROUP_HEADS):
            sum_rows[head] = log_sum[head : head + 1, :]
        log_half = log_sum[:, HALF - 1 : HALF]
        pos = lax.broadcasted_iota(jnp.int32, (GROUP_HEADS, HALF), 1) + base
        mid_pos = base + HALF - 1
        load = jnp.where(
            pos >= doc_start(bounds_ref, mid_pos), jnp.exp(log_half - log_sum[:, :HALF]), 0.0
        )
        later = jnp.where(
            pos + HALF < next_doc(bounds_ref, mid_pos), jnp.exp(log_sum[:, HALF:]), 0.0
        )
        whole_sum = jnp.concatenate([log_sum[:, :HALF], log_sum[:, HALF:] + log_half], axis=1)
        pos = lax.broadcasted_iota(jnp.int32, (GROUP_HEADS, CHUNK), 1) + base
        reach_end = jnp.where(base > 0, next_doc(bounds_ref, base - 1), 0)
        reach = jnp.where(pos < reach_end, jnp.exp(whole_sum), 0.0)
        sum_parts[...] = as_parts(log_sum, 3)
        step_parts[...] = as_parts(step_ref[...], 2)
        load_parts[...] = as_parts(step_ref[:, :HALF] * load, 2)
        reach_parts[...] = as_parts(later, 2)
        reach_out[...] = as_parts(reach, 2)

    first_head = lax.broadcasted_iota(jnp.int32, (1, LANES), 1) < HEAD_DIM
    quarter = HALF // 2
    for k in range(PAIRS):
        pair = pl.program_id(0) * PAIRS + k
        gain = gain_ref[pair]
        sum_cols = spread_heads(sum_parts[...], pair, 2 * LANES)
        steps = spread_heads(step_parts[...], pair, LANES)
        loads = spread_heads(load_parts[...], pair, LANES)
        reach = spread_heads(reach_parts[...], pair, LANES)
        xs = channels(own_ref, pair)
        driven = (steps * xs).astype(BF16)
        loaded = (loads * xs[:HALF]).astype(BF16)
        state = jnp.dot(turned[...], loaded, preferred_element_type=F32).astype(BF16)
        for blk in range(2):
            for part in range(2):
                at = blk * HALF + part * quarter
                width = (part + 1) * quarter
                heads = []
                for head in range(2):
                    log_row = sum_rows[2 * pair + head][:, blk * HALF : blk * HALF + width]
                    log_col = sum_cols[at : at + quarter, head * LANES : (head + 1) * LANES]
                    log_col = jnp.concatenate([log_col] * (part + 1), axis=1)
                    weight = jnp.exp(jnp.minimum(log_col - log_row, 0.0))
                    gram = grams[blk, part * quarter : (part + 1) * quarter, 0:width]
                    heads.append(
                        jnp.dot(
                            (gram * weight).astype(BF16),
                            driven[blk * HALF : blk * HALF + width],
                            preferred_element_type=F32,
                        )
                    )
                result = jnp.where(first_head, heads[0], heads[1]) + gain * xs[at : at + quarter]
                if blk == 1:
                    c_part = c_out[at : at + quarter, :]
                    result += reach[part * quarter : (part + 1) * quarter] * jnp.dot(
                        c_part, state, preferred_element_type=F32
                    )
                out_ref[at : at + quarter, k * LANES : (k + 1) * LANES] = result


def inner(bounds, rows, steps, decays, gains):
    return pl.pallas_call(
        inner_kernel,
        grid_spec=pltpu.PrefetchScalarGridSpec(
            num_scalar_prefetch=1,
            grid=(SEQ // PAIRS,),
            in_specs=[
                whole(SEQ, OWNER_ROWS, LANES),
                whole(GROUP_HEADS, CHUNK),
                whole(GROUP_HEADS, CHUNK),
                whole(SEQ, 1, LANES),
            ],
            out_specs=[
                pl.BlockSpec((CHUNK, PAIRS * LANES), lambda g, *_: (0, g)),
                whole(CHUNK, STATE),
                whole(CHUNK, 2 * GROUP_HEADS),
            ],
            scratch_shapes=[
                pltpu.VMEM((PER, 4, 16, STATE), BF16),
                pltpu.VMEM((PER, 4, 16, STATE), BF16),
                pltpu.VMEM((STATE, HALF), BF16),
                pltpu.VMEM((2, HALF, HALF), F32),
                pltpu.VMEM((GROUP_HEADS, CHUNK), F32),
                pltpu.VMEM((GROUP_HEADS, 1, CHUNK), F32),
                pltpu.VMEM((CHUNK, 3 * GROUP_HEADS), BF16),
                pltpu.VMEM((CHUNK, 2 * GROUP_HEADS), BF16),
                pltpu.VMEM((HALF, 2 * GROUP_HEADS), BF16),
                pltpu.VMEM((HALF, 2 * GROUP_HEADS), BF16),
            ],
        ),
        out_shape=[
            jax.ShapeDtypeStruct((CHUNK, SEQ * LANES), F32),
            jax.ShapeDtypeStruct((CHUNK, STATE), BF16),
            jax.ShapeDtypeStruct((CHUNK, 2 * GROUP_HEADS), BF16),
        ],
        compiler_params=params(32),
        cost_estimate=pl.CostEstimate(
            flops=4_000_000_000, bytes_accessed=8 * MIB, transcendentals=4 * MIB
        ),
        name="inner",
    )(bounds, rows, steps, decays, gains)


def finish_kernel(state_ref, attn_ref, inner_ref, c_ref, reach_ref, ssm_ref, out_ref):
    @pl.when(pl.program_id(0) == 0)
    def _():
        for s in range(SEQ):
            for st in range(PER):
                at = st * LEN + (s % 2) * Q_ROWS
                out_ref[at : at + Q_ROWS, (s // 2) * LANES : (s // 2 + 1) * LANES] = attn_ref[
                    s, st * Q_ROWS : (st + 1) * Q_ROWS, :
                ]

    for k in range(PAIRS):
        pair = pl.program_id(0) * PAIRS + k
        cols = slice(k * LANES, (k + 1) * LANES)
        reached = jnp.dot(c_ref[...], state_ref[k], preferred_element_type=F32)
        reached = spread_heads(reach_ref[...], pair, LANES) * reached
        ssm_ref[:, cols] = (inner_ref[:, cols] + reached).astype(BF16)


def finish(both, inner_out, c_rows, reach):
    return pl.pallas_call(
        finish_kernel,
        grid=(SEQ // PAIRS,),
        in_specs=[
            pl.BlockSpec((PAIRS, STATE, LANES), lambda g: (g, 0, 0)),
            pl.BlockSpec((SEQ, HALF, LANES), lambda g: (0, 1, 0)),
            pl.BlockSpec((CHUNK, PAIRS * LANES), lambda g: (0, g)),
            whole(CHUNK, STATE),
            whole(CHUNK, 2 * GROUP_HEADS),
        ],
        out_specs=[
            pl.BlockSpec((CHUNK, PAIRS * LANES), lambda g: (0, g)),
            whole(CHUNK, PER * LANES),
        ],
        out_shape=[
            jax.ShapeDtypeStruct((CHUNK, SEQ * LANES), BF16),
            jax.ShapeDtypeStruct((CHUNK, PER * LANES), BF16),
        ],
        compiler_params=params(24),
        cost_estimate=pl.CostEstimate(
            flops=1_000_000_000, bytes_accessed=9 * MIB, transcendentals=0
        ),
        name="finish",
    )(both, both, inner_out, c_rows, reach)


def shards(
    stretch_x,
    stretch_bc,
    stretch_dt,
    stretch_q,
    stretch_kv,
    stretch_place,
    segment_ids,
    ssm_rate,
    dt_bias,
    skip_gain,
):
    seq_index = lax.axis_index("seq")
    mp_index = lax.axis_index("mp")
    exchange = functools.partial(lax.all_to_all, split_axis=0, concat_axis=0, tiled=True)
    cut = functools.partial(lax.dynamic_slice_in_dim, axis=0)

    my_docs = cut(segment_ids, mp_index * LEN, LEN)
    my_place = cut(stretch_place, mp_index, 1)
    info = jnp.concatenate([my_docs, my_place, jnp.zeros((LEN - 1,), jnp.int32)])
    info = jnp.broadcast_to(info.astype(F32)[None, :], (8, LANES))
    to_heads = pack(
        stretch_x, stretch_bc, stretch_q, stretch_dt.T.reshape(STRETCHES, LANES), info
    )
    kv_rows, to_heads = lax.optimization_barrier(
        (exchange(pack_kv(stretch_kv), "mp"), to_heads)
    )
    kv = lax.all_gather(kv_rows, "seq", axis=0, tiled=True)
    hop = exchange(to_heads.reshape(STRETCHES, HOP_ROWS, LANES), ("seq", "mp"))

    told = hop[:, INFO_AT, :].astype(jnp.int32)
    places, docs = told[:, LEN], told[:, :LEN]
    order = jnp.arange(STRETCHES, dtype=jnp.int32)
    inv = jnp.sum(jnp.where(places[None, :] == order[:, None], order[None, :], 0), axis=1)
    bounds = jnp.stack(
        [jnp.sum((docs < v).astype(jnp.int32)) for v in range(DOCS)] + [seq_index % 2, seq_index]
    )
    to_owners, queries = place(inv, hop)
    own_rows = exchange(to_owners, "seq")
    group_first = mp_index * GROUP_HEADS
    biases = cut(dt_bias, group_first, GROUP_HEADS)
    rates = cut(ssm_rate, group_first, GROUP_HEADS)
    gains = cut(skip_gain, group_first, GROUP_HEADS)
    own_ends, steps, decays = ends(bounds, own_rows, biases[:, None], rates[:, None])
    arrived = exchange(own_ends, "seq")

    mine = hop[:, INFO_AT + 1, :].astype(F32)
    mine = mine.reshape(STRETCHES, 2, LEN) + cut(biases, 2 * seq_index, 2)[:, None]
    lost = -cut(rates, 2 * seq_index, 2) * jnp.sum(jax.nn.softplus(mine), axis=2)
    chunk_of = (places // PER)[None, :, None] == jnp.arange(SEQ)[:, None, None]
    lost = jnp.sum(jnp.where(chunk_of, lost[None], 0.0), axis=1)
    totals = jnp.repeat(jnp.exp(lost), HEAD_DIM, axis=1)

    both = exchange(chain(bounds, arrived, totals, attend(inv, bounds, kv, queries)), "seq")
    inner_out, c_rows, reach = inner(
        bounds, own_rows, steps, decays, jnp.repeat(gains.reshape(SEQ, 1, 2), HEAD_DIM, axis=2)
    )
    return tuple(finish(both, inner_out, c_rows, reach))


def solution(mesh):
    return jax.shard_map(
        shards,
        mesh=mesh,
        in_specs=(
            P(("seq", "mp"), None),
            P(("seq", "mp"), None, None),
            P(("seq", "mp"), None),
            P(("seq", "mp"), None),
            P(("seq", "mp"), None, None),
            P("seq"),
            P("seq"),
            P(),
            P(),
            P(),
        ),
        out_specs=(P("seq", "mp"), P("seq", "mp")),
        check_vma=False,
    )
```

time: 324 us -> 249 us (0.77)
  Pallas kernels: 161 us -> 59.9 us
  waiting for transfers between devices: 25.2 us -> 58.1 us
  blocking collectives: 81.9 us -> 66.5 us
  starting transfers between devices: 12.3 us -> 22.5 us
    pallas_call x1, Pallas kernels: 81.2 us -> 1.99 us  [place(): pl.pallas_call(place_kernel, grid_spec=pltpu.PrefetchScalarGridSpec(num_s...]
    all_to_all x2 -> x4, waiting for transfers between devices: 25.2 us -> 58.1 us  [the longest x1 43.7 us: shards(): own_rows = exchange(to_owners, 'seq')]
    pallas_call x3 -> x7, Pallas kernels: 79.7 us -> 58 us  [the longest x1 28.7 us: attend(): pl.pallas_call(attend_kernel, grid_spec=pltpu.PrefetchScalarGridSpec(num_...]
    all_to_all x1 -> x0, blocking collectives: 14 us -> none  [shards(): group_rows = exchange(to_groups, 'mp')]
    all_to_all x2 -> x4, starting transfers between devices: 12.2 us -> 22.4 us  [the longest x1 7.17 us: shards(): exchange(chain(bounds, arrived, totals, attend(inv, bounds, kv, queries))...]
    unnamed x22 -> x38, local copies, waits for them, and re-layouts: 8.74 us -> 16.9 us
    slice x4 -> x0, local copies, waits for them, and re-layouts: 7.6 us -> none  [the longest x1 2.94 us: shards(): stretch_bc[:, 1, :]]
  transfers between devices with their start and end apart: 3 -> 5, of which waited for: 1 -> 2; matrix products, arithmetic and copies ran while one was open for 3% -> 4% of each run, Pallas kernels for 43% -> 20%
where the time goes in v2:
time: 249 us
  blocking collectives  66.5 us (27%)
  Pallas kernels  59.9 us (24%)
  waiting for transfers between devices  58.1 us (23%)
  local copies, waits for them, and re-layouts  25.5 us (10%)
  starting transfers between devices  22.5 us (9%)
  between operations  14.3 us (6%)
    all_to_all x1, blocking collectives, shards(): hop = exchange(to_heads.reshape(STRETCHES, HOP_ROWS, LANES), ('seq', 'mp'))  66.5 us
    all_to_all x1, waiting for transfers between devices, shards(): own_rows = exchange(to_owners, 'seq')  43.7 us
    pallas_call x1, Pallas kernels, attend(): pl.pallas_call(attend_kernel, grid_spec=pltpu.PrefetchScalarGridSpec(num_...  28.7 us
    unnamed x38, local copies, waits for them, and re-layouts  16.9 us
    all_to_all x1, waiting for transfers between devices, shards(): exchange(chain(bounds, arrived, totals, attend(inv, bounds, kv, queries))...  14.4 us
    pallas_call x1, Pallas kernels, inner(): pl.pallas_call(inner_kernel, grid_spec=pltpu.PrefetchScalarGridSpec(num_s...  10.9 us
    all_to_all x1, starting transfers between devices, shards(): exchange(chain(bounds, arrived, totals, attend(inv, bounds, kv, queries))...  7.17 us
    all_to_all x1, starting transfers between devices, shards(): arrived = exchange(own_ends, 'seq')  6.58 us
  transfers between devices with their start and end apart: 5, of which 2 were waited for; matrix products, arithmetic and copies ran while one was open for 4% of the time, Pallas kernels for 20%

profile of v2, /device:TPU:2, one launch (start us, length us, event | category | flops | bytes accessed | tf_op | source)
XLA Modules:
  0.0 248.9 jit_solution(4386200018055702701)
XLA Ops:
  7.2 0.0 copy-start.10
  7.2 0.9 copy-done.10
  8.1 1.3 pack_kv.1
  9.4 4.8 %all-to-all-start = ((bf16[8,128,128]{2,1,0:T(8,128)(2,1)}), bf16[8,128,128]{2,1,0:T(8,128)(2,1)S(1)}, u32[]{:S(2)}, u32[]{:S(2)}) async-start(bf16[8,128,128]{2,1,0:T(8,128)(2,1)} %pack_kv.1), calls=%async_computation | async-start | bytes 524288 | tf_op jit(solution)/shard_map/all_to_all | solution.py:682
  14.2 0.0 all-gather.2.cloned.1.call-start
  14.2 0.9 copy.30
  15.1 0.1 reshape.122.dt_ref
  15.2 1.2 dynamic_slice.24
  16.5 0.8 dynamic_slice.23
  17.2 0.7 add_convert_fusion
  18.0 1.6 copy-done.6
  19.5 1.2 copy-done.7
  20.8 1.0 copy-done.9
  21.8 2.3 pack.1
  24.1 0.0 copy-start
  24.1 2.0 copy-done
  26.1 0.0 all-to-all-done
  26.1 0.7 copy-done.15
  26.8 0.0 all-gather.2.cloned.1.call-update
  26.8 66.5 %all_to_all.25.hop_ref = bf16[128,128,128]{2,1,0:T(8,128)(2,1)S(1)} all-to-all(bf16[128,128,128]{2,1,0:T(8,128)(2,1)} %bitcast.16), channel_id=1, replica_groups=mesh['seq'=16,'mp'=8] {'seq','mp'}, dimensions={0} | all-to-all | bytes 8388608 | tf_op jit(solution)/shard_map/all_to_all | solution.py:685
  93.3 0.1 slice_convert_fusion
  93.5 0.2 slice_reduce_fusion
  93.6 0.1 select_reduce_fusion.inv_ref
  93.8 2.0 place.1
  95.8 1.5 copy-done.5
  97.3 1.0 copy-done.14
  98.3 3.9 %all-to-all-start.2 = ((bf16[16,656,128]{2,1,0:T(8,128)(2,1)}), bf16[16,656,128]{2,1,0:T(8,128)(2,1)S(1)}, u32[]{:S(2)}, u32[]{:S(2)}) async-start(bf16[16,656,128]{2,1,0:T(8,128)(2,1)} %copy-done.5), calls=%async_computation.2 | async-start | bytes 5373952 | tf_op jit(solution)/shard_map/all_to_all | solution.py:695
  102.2 0.1 dynamic-slice_bitcast_fusion
  102.3 0.1 copy.31.bias_ref
  102.4 0.1 copy.32.rate_ref
  102.5 0.1 dynamic_slice.29
  102.5 0.1 dynamic-slice_negate_fusion
  102.6 0.1 copy.33
  102.7 0.8 convert_reduce_fusion
  103.5 3.9 %stack.35.bounds_ref = s32[8]{0:T(128)S(1)} concatenate(s32[1]{0:T(128)} %bitcast.3, s32[1]{0:T(128)} %bitcast.4, s32[1]{0:T(128)} %bitcast.5, s32[1]{0:T(128)} %bitcast.6, s32[1]{0:T(128)} %bitcast.7, s32[1]{0:T(128)} %bitcast.8, s32[1]{0:T(128)} %bitcast.9, s32[1]{0:T(128)} %bitcast.10), dimensions={0} | concatenate | bytes 64 | tf_op jit(solution)/shard_map/stack | solution.py:691
  107.4 0.1 fusion
  107.6 43.7 %all-to-all-done.2.own_ref = bf16[16,656,128]{2,1,0:T(8,128)(2,1)S(1)} async-done(((bf16[16,656,128]{2,1,0:T(8,128)(2,1)}), bf16[16,656,128]{2,1,0:T(8,128)(2,1)S(1)}, u32[]{:S(2)}, u32[]{:S(2)}) %all-to-all-start.2) | async-done | bytes 2687008 | tf_op jit(solution)/shard_map/all_to_all | solution.py:695
  151.2 6.4 %ends.1 = (bf16[16,256,128]{2,1,0:T(8,128)(2,1)S(1)}, f32[32,512]{1,0:T(8,128)S(1)}, f32[32,512]{1,0:T(8,128)S(1)}) custom-call(s32[8]{0:T(128)S(1)} %stack.35.bounds_ref, bf16[16,656,128]{2,1,0:T(8,128)(2,1)S(1)} %all-to-all-done.2.own_ref, f32[32,1]{1,0:T(8,128)S(1)} %copy.31.bias_ref, f32[32,1]{1,0:T(8,128)S(1)} %copy.32.rate_ref), custom_call_target="tpu_custom_call" | custom-call | flops 1000000000 | bytes 4194304 | tf_op jit(solution)/shard_map/ends/pallas_call | solution.py:395
  157.6 0.0 copy-start.8
  157.6 1.0 copy-done.8
  158.6 0.0 copy-done.11
  158.6 6.6 %all-to-all-start.3 = ((bf16[16,256,128]{2,1,0:T(8,128)(2,1)}), bf16[16,256,128]{2,1,0:T(8,128)(2,1)}, u32[]{:S(2)}, u32[]{:S(2)}) async-start(bf16[16,256,128]{2,1,0:T(8,128)(2,1)} %copy-done.8), calls=%async_computation.3 | async-start | bytes 2097152 | tf_op jit(solution)/shard_map/all_to_all | solution.py:701
  165.2 0.1 broadcast_multiply_fusion
  165.3 0.1 select_reduce_fusion.1
  165.4 0.1 copy.34
  165.4 0.1 broadcast_in_dim.70
  165.5 0.7 reshape.124.total_ref
  166.2 28.7 %attend.1.both_in = bf16[16,512,128]{2,1,0:T(8,128)(2,1)} custom-call(s32[128]{0:T(128)} %copy-done.13, s32[8]{0:T(128)} %copy-done.11, bf16[128,128,128]{2,1,0:T(8,128)(2,1)} %all-gather.2.cloned.1.call-done.kv_hbm, bf16[16,256,128]{2,1,0:T(8,128)(2,1)} %copy-done.14), custom_call_target="tpu_custom_call" | custom-call | flops 8000000000 | bytes 6291456 | tf_op jit(solution)/shard_map/attend/pallas_call | solution.py:299
  194.9 0.0 all-to-all-done.3.ends_ref
  194.9 3.1 %chain.1 = bf16[16,512,128]{2,1,0:T(8,128)(2,1)} custom-call(s32[8]{0:T(128)} %copy-done.11, bf16[16,256,128]{2,1,0:T(8,128)(2,1)} %all-to-all-done.3.ends_ref, f32[16,128]{1,0:T(8,128)} %reshape.124.total_ref, bf16[16,512,128]{2,1,0:T(8,128)(2,1)} %attend.1.both_in), custom_call_target="tpu_custom_call", output_to_operand_aliasing={{}: (3, {})} | custom-call | bytes 3145728 | tf_op jit(solution)/shard_map/chain/pallas_call | solution.py:443
  198.1 0.0 copy-start.18
  198.1 0.0 copy-start.12
  198.1 7.2 %all-to-all-start.4 = ((bf16[16,512,128]{2,1,0:T(8,128)(2,1)}), bf16[16,512,128]{2,1,0:T(8,128)(2,1)S(1)}, u32[]{:S(2)}, u32[]{:S(2)}) async-start(bf16[16,512,128]{2,1,0:T(8,128)(2,1)} %chain.1), calls=%async_computation.4 | async-start | bytes 4194304 | tf_op jit(solution)/shard_map/all_to_all | solution.py:710
  205.3 0.1 dynamic_slice.30
  205.3 0.1 reshape.125
  205.4 0.1 broadcast_in_dim.71
  205.5 0.1 broadcast_in_dim.72.gain_ref
  205.6 0.0 copy-done.12
  205.6 1.8 copy-done.4
  207.4 10.9 %inner.1 = (f32[512,2048]{1,0:T(8,128)S(1)}, bf16[512,256]{1,0:T(8,128)(2,1)S(1)}, bf16[512,64]{1,0:T(8,128)(2,1)S(1)}) custom-call(s32[8]{0:T(128)S(1)} %copy-done.12, bf16[16,656,128]{2,1,0:T(8,128)(2,1)S(1)} %copy-done.4, f32[32,512]{1,0:T(8,128)S(1)} %get-tuple-element.17.step_ref, f32[32,512]{1,0:T(8,128)S(1)} %get-tuple-element.18.decay_ref, ...), custom_call_target="tpu_custom_call" | custom-call | flops 4000000000 | bytes 8388608 | tf_op jit(solution)/shard_map/inner/pallas_call | solution.py:570
  218.3 1.9 copy-done.1
  220.2 14.4 %all-to-all-done.4.state_ref.attn_ref = bf16[16,512,128]{2,1,0:T(8,128)(2,1)S(1)} async-done(((bf16[16,512,128]{2,1,0:T(8,128)(2,1)}), bf16[16,512,128]{2,1,0:T(8,128)(2,1)S(1)}, u32[]{:S(2)}, u32[]{:S(2)}) %all-to-all-start.4) | async-done | bytes 2097184 | tf_op jit(solution)/shard_map/all_to_all | solution.py:710
  234.6 2.2 copy-done.2
  236.8 5.3 %finish.1 = (bf16[512,2048]{1,0:T(8,128)(2,1)}, bf16[512,1024]{1,0:T(8,128)(2,1)}) custom-call(bf16[16,512,128]{2,1,0:T(8,128)(2,1)S(1)} %all-to-all-done.4.state_ref.attn_ref, bf16[16,512,128]{2,1,0:T(8,128)(2,1)S(1)} %all-to-all-done.4.state_ref.attn_ref, f32[512,2048]{1,0:T(8,128)S(1)} %copy-done.2, bf16[512,256]{1,0:T(8,128)(2,1)S(1)} %get-tuple-element.20.c_ref, ...), custom_call_target="tpu_custom_call" | custom-call | flops 1000000000 | bytes 9437184 | tf_op jit(solution)/shard_map/finish/pallas_call | solution.py:631
  (25 shorter events, 0.1 us)
Async XLA Ops:
  7.2 1.0 copy-start.10
  9.4 16.6 %all-to-all-start = ((bf16[8,128,128]{2,1,0:T(8,128)(2,1)}), bf16[8,128,128]{2,1,0:T(8,128)(2,1)S(1)}, u32[]{:S(2)}, u32[]{:S(2)}) async-start(bf16[8,128,128]{2,1,0:T(8,128)(2,1)} %pack_kv.1), calls=%async_computation | async-start | bytes 524288 | tf_op jit(solution)/shard_map/all_to_all | solution.py:682
  14.2 152.0 %all-gather.2.cloned.1.call-start = ((), (), s32[]{:S(2)}) async-start(), calls=%async_computation.5 | async-start | bytes 4456448 | tf_op jit(solution)/shard_map/all_gather | solution.py:684
  18.0 1.6 copy-start.6
  19.5 1.2 copy-start.7
  20.8 1.0 copy-start.9
  24.1 2.0 copy-start
  26.1 0.7 copy-start.15
  93.8 4.5 %copy-start.13 = (s32[128]{0:T(128)}, s32[128]{0:T(128)S(1)}, u32[]{:S(2)}) copy-start(s32[128]{0:T(128)S(1)} %select_reduce_fusion.inv_ref) | copy-start | bytes 1540
  95.8 1.6 copy-start.5
  97.3 1.0 copy-start.14
  98.3 3.9 %copy-start.16 = (f32[256]{0:T(256)S(1)}, f32[256]{0:T(256)}, u32[]{:S(2)}) copy-start(f32[256]{0:T(256)} %param.18) | copy-start | bytes 3076
  98.3 3.9 %copy-start.17 = (f32[256]{0:T(256)S(1)}, f32[256]{0:T(256)}, u32[]{:S(2)}) copy-start(f32[256]{0:T(256)} %param.17) | copy-start | bytes 3076
  98.3 52.9 %all-to-all-start.2 = ((bf16[16,656,128]{2,1,0:T(8,128)(2,1)}), bf16[16,656,128]{2,1,0:T(8,128)(2,1)S(1)}, u32[]{:S(2)}, u32[]{:S(2)}) async-start(bf16[16,656,128]{2,1,0:T(8,128)(2,1)} %copy-done.5), calls=%async_computation.2 | async-start | bytes 5373952 | tf_op jit(solution)/shard_map/all_to_all | solution.py:695
  107.4 51.2 %copy-start.11 = (s32[8]{0:T(128)}, s32[8]{0:T(128)S(1)}, u32[]{:S(2)}) copy-start(s32[8]{0:T(128)S(1)} %stack.35.bounds_ref) | copy-start | bytes 100
  151.2 7.4 %copy-start.3 = (bf16[16,656,128]{2,1,0:T(8,128)(2,1)}, bf16[16,656,128]{2,1,0:T(8,128)(2,1)S(1)}, u32[]{:S(2)}) copy-start(bf16[16,656,128]{2,1,0:T(8,128)(2,1)S(1)} %all-to-all-done.2.own_ref) | copy-start | bytes 8060932
  157.6 1.0 copy-start.8
  158.6 36.3 %all-to-all-start.3 = ((bf16[16,256,128]{2,1,0:T(8,128)(2,1)}), bf16[16,256,128]{2,1,0:T(8,128)(2,1)}, u32[]{:S(2)}, u32[]{:S(2)}) async-start(bf16[16,256,128]{2,1,0:T(8,128)(2,1)} %copy-done.8), calls=%async_computation.3 | async-start | bytes 2097152 | tf_op jit(solution)/shard_map/all_to_all | solution.py:701
  198.1 7.2 %copy-start.18 = (f32[256]{0:T(256)S(1)}, f32[256]{0:T(256)}, u32[]{:S(2)}) copy-start(f32[256]{0:T(256)} %param.19) | copy-start | bytes 3076
  198.1 7.5 %copy-start.12 = (s32[8]{0:T(128)S(1)}, s32[8]{0:T(128)}, u32[]{:S(2)}) copy-start(s32[8]{0:T(128)} %copy-done.11) | copy-start | bytes 100
  198.1 36.5 %all-to-all-start.4 = ((bf16[16,512,128]{2,1,0:T(8,128)(2,1)}), bf16[16,512,128]{2,1,0:T(8,128)(2,1)S(1)}, u32[]{:S(2)}, u32[]{:S(2)}) async-start(bf16[16,512,128]{2,1,0:T(8,128)(2,1)} %chain.1), calls=%async_computation.4 | async-start | bytes 4194304 | tf_op jit(solution)/shard_map/all_to_all | solution.py:710
  205.6 1.8 copy-start.4
  218.2 1.9 copy-start.1
  234.6 2.2 copy-start.2
Sparse Core Ops, SparseCore 0:
  26.9 123.4 all-gather.1

commit v3 on v2

--- a/solution.py
+++ b/solution.py
@@ -31,7 +31,8 @@
 BC_AT = X_ROWS
 Q_AT = BC_AT + BC_ROWS
 INFO_AT = Q_AT + Q_ROWS
-HOP_ROWS = INFO_AT + 16
+INFO_ROWS = 8
+HOP_ROWS = INFO_AT + INFO_ROWS
 OWN_ROWS = X_ROWS + BC_ROWS
 OWNER_ROWS = PER * OWN_ROWS + 16
 K_AT, V_AT, G_ROWS = 0, 64, 128
@@ -48,8 +49,8 @@
 
 
 def pack_kernel(x_ref, bc_ref, q_ref, dt_ref, info_ref, hop_ref):
-    row = lax.broadcasted_iota(jnp.int32, (16, LANES), 0)
-    told = jnp.where(row == 0, jnp.broadcast_to(info_ref[0:1, :], (16, LANES)), 0.0)
+    row = lax.broadcasted_iota(jnp.int32, (INFO_ROWS, LANES), 0)
+    told = jnp.where(row == 0, jnp.broadcast_to(info_ref[0:1, :], (INFO_ROWS, LANES)), 0.0)
     raw = dt_ref[...].astype(F32)
     for s in range(SEQ):
         hop_ref[s, 0, 0:X_ROWS, :] = x_ref[:, s * LANES : (s + 1) * LANES]
@@ -60,7 +61,7 @@
         hop_ref[s, 0, Q_AT : Q_AT + Q_ROWS, :] = q_ref[
             pl.ds((s % 2) * Q_ROWS, Q_ROWS), (s // 2) * LANES : (s // 2 + 1) * LANES
         ]
-        tile = jnp.where(row == 1, jnp.broadcast_to(raw[s : s + 1, :], (16, LANES)), told)
+        tile = jnp.where(row == 1, jnp.broadcast_to(raw[s : s + 1, :], (INFO_ROWS, LANES)), told)
         hop_ref[s, 0, INFO_AT:HOP_ROWS, :] = tile.astype(BF16)
 
 
@@ -78,7 +79,7 @@
         ],
         out_specs=pl.BlockSpec((SEQ, 1, HOP_ROWS, LANES), lambda m: (0, m, 0, 0)),
         out_shape=jax.ShapeDtypeStruct((SEQ, MP, HOP_ROWS, LANES), BF16),
-        compiler_params=params(32),
+        compiler_params=params(60),
         cost_estimate=pl.CostEstimate(flops=0, bytes_accessed=9 * MIB, transcendentals=0),
         name="pack",
     )(x, bc, q, dt_rows, info)
@@ -144,7 +145,7 @@
             jax.ShapeDtypeStruct((SEQ, OWNER_ROWS, LANES), BF16),
             jax.ShapeDtypeStruct((SEQ, PER * Q_ROWS, LANES), BF16),
         ],
-        compiler_params=params(24),
+        compiler_params=params(60),
         cost_estimate=pl.CostEstimate(flops=0, bytes_accessed=6 * MIB, transcendentals=0),
         name="place",
     )(inv, hop)
@@ -239,50 +240,44 @@
 
     def far_tiles(i, carry):
         first = doc_start(bounds_ref, i * CHUNK) // CHUNK
-        last_doc = doc_start(bounds_ref, i * CHUNK + CHUNK - 1)
-        end = jnp.maximum(i - 1, first)
-        clear = jnp.clip((last_doc + CHUNK - 1) // CHUNK, first, end)
-        n_clear = (end - clear) // 2
-        clear = end - 2 * n_clear
-        n_mask = (clear - first) // 2
-
+        count = jnp.maximum(i - 1 - first, 0)
+        fours = (count + 1) // 4
         queries = q_ref[i]
         q_doc = doc_start(bounds_ref, i * CHUNK + in_chunk)
 
-        def add_tiles(js, masks):
+        def add_tiles(last, number):
             old = top_far[...]
-            scores = [scores_of(queries, j) for j in js]
-            if masks:
-                scores = [
-                    jnp.where(key_at >= q_doc - j * CHUNK, s, NEG_BIG) for s, j in zip(scores, js)
-                ]
-            top = old
-            for s in scores:
-                top = jnp.maximum(top, peak_of(s))
+            scores = []
+            for k in range(number):
+                dots = scores_of(queries, jnp.maximum(last - k, 0))
+                scores.append(jnp.where(key_at >= q_doc - (last - k) * CHUNK, dots, NEG_BIG))
+            added, top = acc_far[...], old
+            for k, dots in enumerate(scores):
+                new = jnp.maximum(top, peak_of(dots))
+                added = added * jnp.exp2((top - new) * scale) + mixed(
+                    dots, new, jnp.maximum(last - k, 0)
+                )
+                top = new
             top_far[...] = top
-            added = sum(mixed(s, top, j) for s, j in zip(scores, js))
-            acc_far[...] = acc_far[...] * jnp.exp2((old - top) * scale) + added
-
-        top_far[...] = peak[i]
-        acc_far[...] = acc[i]
-
-        @pl.when((clear - first) % 2 == 1)
+            acc_far[...] = added
+
+        @pl.when(count > 0)
         def _():
-            add_tiles([first], True)
-
-        def masked(t, c):
-            j = clear - 2 * n_mask + 2 * t
-            add_tiles([j, j + 1], True)
-            return c
-
-        def plain(t, c):
-            j = clear + 2 * t
-            add_tiles([j, j + 1], False)
-            return c
-
-        lax.fori_loop(0, n_mask, masked, 0)
-        lax.fori_loop(0, n_clear, plain, 0)
-        acc[i] = acc_far[...]
+            top_far[...] = peak[i]
+            acc_far[...] = acc[i]
+
+            def four(t, c):
+                add_tiles(i - 2 - 4 * t, 4)
+                return c
+
+            lax.fori_loop(0, fours, four, 0)
+
+            @pl.when(count > 4 * fours)
+            def _():
+                add_tiles(i - 2 - 4 * fours, 2)
+
+            acc[i] = acc_far[...]
+
         return carry
 
     lax.fori_loop(2, SEQ, far_tiles, 0)
@@ -563,7 +558,7 @@
                     result += reach[part * quarter : (part + 1) * quarter] * jnp.dot(
                         c_part, state, preferred_element_type=F32
                     )
-                out_ref[at : at + quarter, k * LANES : (k + 1) * LANES] = result
+                out_ref[at : at + quarter, k * LANES : (k + 1) * LANES] = result.astype(BF16)
 
 
 def inner(bounds, rows, steps, decays, gains):
@@ -597,7 +592,7 @@
             ],
         ),
         out_shape=[
-            jax.ShapeDtypeStruct((CHUNK, SEQ * LANES), F32),
+            jax.ShapeDtypeStruct((CHUNK, SEQ * LANES), BF16),
             jax.ShapeDtypeStruct((CHUNK, STATE), BF16),
             jax.ShapeDtypeStruct((CHUNK, 2 * GROUP_HEADS), BF16),
         ],
@@ -624,7 +619,7 @@
         cols = slice(k * LANES, (k + 1) * LANES)
         reached = jnp.dot(c_ref[...], state_ref[k], preferred_element_type=F32)
         reached = spread_heads(reach_ref[...], pair, LANES) * reached
-        ssm_ref[:, cols] = (inner_ref[:, cols] + reached).astype(BF16)
+        ssm_ref[:, cols] = (inner_ref[:, cols].astype(F32) + reached).astype(BF16)
 
 
 def finish(both, inner_out, c_rows, reach):
@@ -675,13 +670,10 @@
     my_place = cut(stretch_place, mp_index, 1)
     info = jnp.concatenate([my_docs, my_place, jnp.zeros((LEN - 1,), jnp.int32)])
     info = jnp.broadcast_to(info.astype(F32)[None, :], (8, LANES))
+    kv = lax.all_gather(exchange(pack_kv(stretch_kv), "mp"), "seq", axis=0, tiled=True)
     to_heads = pack(
         stretch_x, stretch_bc, stretch_q, stretch_dt.T.reshape(STRETCHES, LANES), info
     )
-    kv_rows, to_heads = lax.optimization_barrier(
-        (exchange(pack_kv(stretch_kv), "mp"), to_heads)
-    )
-    kv = lax.all_gather(kv_rows, "seq", axis=0, tiled=True)
     hop = exchange(to_heads.reshape(STRETCHES, HOP_ROWS, LANES), ("seq", "mp"))
 
     told = hop[:, INFO_AT, :].astype(jnp.int32)
@@ -697,7 +689,8 @@
     biases = cut(dt_bias, group_first, GROUP_HEADS)
     rates = cut(ssm_rate, group_first, GROUP_HEADS)
     gains = cut(skip_gain, group_first, GROUP_HEADS)
-    own_ends, steps, decays = ends(bounds, own_rows, biases[:, None], rates[:, None])
+    attended, own_bounds = lax.optimization_barrier((attend(inv, bounds, kv, queries), bounds))
+    own_ends, steps, decays = ends(own_bounds, own_rows, biases[:, None], rates[:, None])
     arrived = exchange(own_ends, "seq")
 
     mine = hop[:, INFO_AT + 1, :].astype(F32)
@@ -707,7 +700,7 @@
     lost = jnp.sum(jnp.where(chunk_of, lost[None], 0.0), axis=1)
     totals = jnp.repeat(jnp.exp(lost), HEAD_DIM, axis=1)
 
-    both = exchange(chain(bounds, arrived, totals, attend(inv, bounds, kv, queries)), "seq")
+    both = exchange(chain(bounds, arrived, totals, attended), "seq")
     inner_out, c_rows, reach = inner(
         bounds, own_rows, steps, decays, jnp.repeat(gains.reshape(SEQ, 1, 2), HEAD_DIM, axis=2)
     )

time: 249 us -> 234 us (0.940); the launches traced: 249 us -> 231 us
  waiting for transfers between devices: 58.1 us -> 38.6 us
  local copies, waits for them, and re-layouts: 25.5 us -> 17.5 us
  blocking collectives: 66.5 us -> 70.1 us
  Pallas kernels: 59.9 us -> 63.4 us
    all_to_all x1, waiting for transfers between devices: 43.7 us -> 4.27 us  [shards(): own_rows = exchange(to_owners, 'seq')]
    all_to_all x1, waiting for transfers between devices: 0.01 us -> 15.6 us  [shards(): arrived = exchange(own_ends, 'seq')]
    all_to_all x0 -> x1, blocking collectives: none -> 10.8 us  [shards(): exchange(pack_kv(stretch_kv), 'mp')]
    all_to_all x1, starting transfers between devices: 6.58 us -> 16.4 us  [shards(): arrived = exchange(own_ends, 'seq')]
    unnamed x38 -> x24, local copies, waits for them, and re-layouts: 16.9 us -> 7.19 us
    all_to_all x2 -> x1, starting transfers between devices: 12 us -> 3.73 us  [shards(): both = exchange(chain(bounds, arrived, totals, attended), 'seq')]
    all_to_all x1, blocking collectives: 66.5 us -> 59.3 us  [shards(): hop = exchange(to_heads.reshape(STRETCHES, HOP_ROWS, LANES), ('seq', 'mp'))]
    pallas_call x1, Pallas kernels: 2.26 us -> 7.14 us  [pack(): pl.pallas_call(pack_kernel, grid=(MP,), in_specs=[cols(SEQ * LANES), pl.B...]
  transfers between devices with their start and end apart: 5 -> 4, of which waited for: 2 -> 4; matrix products, arithmetic and copies ran while one was open for 4% -> 6% of each run, Pallas kernels for 20% -> 21%
where the time goes in v3:
time: 234 us; the launch traced here: 231 us
  blocking collectives  70.1 us (30%)
  Pallas kernels  63.4 us (27%)
  waiting for transfers between devices  38.6 us (16%)
  starting transfers between devices  24 us (10%)
  local copies, waits for them, and re-layouts  17.5 us (7%)
  between operations  14.2 us (6%)
  other arithmetic  3.02 us (1%)
    all_to_all x1, blocking collectives, shards(): hop = exchange(to_heads.reshape(STRETCHES, HOP_ROWS, LANES), ('seq', 'mp'))  59.3 us
    pallas_call x1, Pallas kernels, attend(): pl.pallas_call(attend_kernel, grid_spec=pltpu.PrefetchScalarGridSpec(num_...  23.9 us
    all_to_all x1, starting transfers between devices, shards(): arrived = exchange(own_ends, 'seq')  16.4 us
    all_to_all x1, waiting for transfers between devices, shards(): arrived = exchange(own_ends, 'seq')  15.6 us
    all_to_all x1, waiting for transfers between devices, shards(): both = exchange(chain(bounds, arrived, totals, attended), 'seq')  14.2 us
    all_to_all x1, blocking collectives, shards(): exchange(pack_kv(stretch_kv), 'mp')  10.8 us
    pallas_call x1, Pallas kernels, inner(): pl.pallas_call(inner_kernel, grid_spec=pltpu.PrefetchScalarGridSpec(num_s...  10.8 us
    unnamed x24, local copies, waits for them, and re-layouts  7.19 us
  transfers between devices with their start and end apart: 4, of which 4 were waited for; matrix products, arithmetic and copies ran while one was open for 6% of the time, Pallas kernels for 21%

profile of v3, /device:TPU:2, one launch (start us, length us, event | category | flops | bytes accessed | tf_op | source)
XLA Modules:
  0.0 231.0 jit_solution(10025958396759933687)
XLA Ops:
  7.2 0.0 all-gather.2.cloned.1.call-start
  7.2 0.0 copy-start.5
  7.2 0.9 copy-done.5
  8.2 0.6 pack_kv.1
  8.7 10.8 %all_to_all.25 = bf16[8,128,128]{2,1,0:T(8,128)(2,1)} all-to-all(bf16[8,128,128]{2,1,0:T(8,128)(2,1)S(1)} %pack_kv.1), channel_id=1, replica_groups=mesh['seq'=16,'mp'=8] {'mp'}, dimensions={0} | all-to-all | bytes 524288 | tf_op jit(solution)/shard_map/all_to_all | solution.py:673
  19.6 0.0 all-gather.2.cloned.1.call-update
  19.6 0.9 copy.30
  20.5 0.7 reshape.122.dt_ref
  21.2 0.8 dynamic_slice.23
  21.9 1.2 dynamic_slice.24
  23.2 0.7 add_convert_fusion
  23.9 0.6 broadcast_in_dim.62.info_ref
  24.5 7.1 %pack.1 = bf16[16,8,120,128]{3,2,1,0:T(8,128)(2,1)} custom-call(bf16[64,16384]{1,0:T(8,128)(2,1)} %x_ref.1, bf16[64,2,2048]{2,1,0:T(2,128)(2,1)} %bc_ref.1, bf16[64,8192]{1,0:T(8,128)(2,1)} %q_ref.1, bf16[128,128]{1,0:T(8,128)(2,1)} %reshape.122.dt_ref, f32[8,128]{1,0:T(8,128)} %broadcast_in_dim.62.info_ref), custom_call_target="tpu_custom_call" | custom-call | bytes 9437184 | tf_op jit(solution)/shard_map/pack/pallas_call | solution.py:70
  31.6 59.3 %all_to_all.26.hop_ref = bf16[128,120,128]{2,1,0:T(8,128)(2,1)S(1)} all-to-all(bf16[128,120,128]{2,1,0:T(8,128)(2,1)} %bitcast.16), channel_id=1, replica_groups=mesh['seq'=16,'mp'=8] {'seq','mp'}, dimensions={0} | all-to-all | bytes 7864320 | tf_op jit(solution)/shard_map/all_to_all | solution.py:677
  91.0 0.1 slice_convert_fusion
  91.1 0.2 slice_reduce_fusion
  91.3 1.0 select_reduce_fusion.inv_ref
  92.2 0.6 copy-done.8
  92.8 6.2 %place.1 = (bf16[16,656,128]{2,1,0:T(8,128)(2,1)}, bf16[16,256,128]{2,1,0:T(8,128)(2,1)}) custom-call(s32[128]{0:T(128)} %select_reduce_fusion.inv_ref, bf16[128,120,128]{2,1,0:T(8,128)(2,1)} %copy-done.8), custom_call_target="tpu_custom_call" | custom-call | bytes 6291456 | tf_op jit(solution)/shard_map/place/pallas_call | solution.py:133
  99.0 3.9 %all-to-all-start.2 = ((bf16[16,656,128]{2,1,0:T(8,128)(2,1)}), bf16[16,656,128]{2,1,0:T(8,128)(2,1)S(1)}, u32[]{:S(2)}, u32[]{:S(2)}) async-start(bf16[16,656,128]{2,1,0:T(8,128)(2,1)} %get-tuple-element.14), calls=%async_computation.2 | async-start | bytes 5373952 | tf_op jit(solution)/shard_map/all_to_all | solution.py:687
  102.9 0.0 copy-done.9
  102.9 0.0 copy-done.10
  102.9 0.1 dynamic-slice_bitcast_fusion
  103.0 0.1 copy.31.bias_ref
  103.1 0.1 copy.32.rate_ref
  103.2 0.1 dynamic_slice.29
  103.3 0.8 convert_reduce_fusion
  104.1 4.3 %stack.35.bounds_ref = s32[8]{0:T(128)} concatenate(s32[1]{0:T(128)} %bitcast.3, s32[1]{0:T(128)} %bitcast.4, s32[1]{0:T(128)} %bitcast.5, s32[1]{0:T(128)} %bitcast.6, s32[1]{0:T(128)} %bitcast.7, s32[1]{0:T(128)} %bitcast.8, s32[1]{0:T(128)} %bitcast.9, s32[1]{0:T(128)} %bitcast.10), dimensions={0} | concatenate | bytes 64 | tf_op jit(solution)/shard_map/stack | solution.py:683
  108.4 4.6 %all-gather.2.cloned.1.call-done.kv_hbm = bf16[128,128,128]{2,1,0:T(8,128)(2,1)} async-done(((bf16[8,128,128]{2,1,0:T(8,128)(2,1)}), bf16[128,128,128]{2,1,0:T(8,128)(2,1)}) %all-gather.2.cloned.1.call-update) | async-done | bytes 4194320 | tf_op jit(solution)/shard_map/all_gather | solution.py:673
  113.0 23.9 %attend.1.both_in = bf16[16,512,128]{2,1,0:T(8,128)(2,1)} custom-call(s32[128]{0:T(128)} %select_reduce_fusion.inv_ref, s32[8]{0:T(128)} %stack.35.bounds_ref, bf16[128,128,128]{2,1,0:T(8,128)(2,1)} %all-gather.2.cloned.1.call-done.kv_hbm, bf16[16,256,128]{2,1,0:T(8,128)(2,1)} %get-tuple-element.12.q_hbm), custom_call_target="tpu_custom_call" | custom-call | flops 8000000000 | bytes 6291456 | tf_op jit(solution)/shard_map/attend/pallas_call | solution.py:294
  136.9 4.3 %all-to-all-done.2.own_ref = bf16[16,656,128]{2,1,0:T(8,128)(2,1)S(1)} async-done(((bf16[16,656,128]{2,1,0:T(8,128)(2,1)}), bf16[16,656,128]{2,1,0:T(8,128)(2,1)S(1)}, u32[]{:S(2)}, u32[]{:S(2)}) %all-to-all-start.2) | async-done | bytes 2687008 | tf_op jit(solution)/shard_map/all_to_all | solution.py:687
  141.2 0.0 copy-done.6
  141.2 6.4 %ends.1 = (bf16[16,256,128]{2,1,0:T(8,128)(2,1)S(1)}, f32[32,512]{1,0:T(8,128)S(1)}, f32[32,512]{1,0:T(8,128)S(1)}) custom-call(s32[8]{0:T(128)S(1)} %copy-done.6, bf16[16,656,128]{2,1,0:T(8,128)(2,1)S(1)} %all-to-all-done.2.own_ref, f32[32,1]{1,0:T(8,128)S(1)} %copy.31.bias_ref, f32[32,1]{1,0:T(8,128)S(1)} %copy.32.rate_ref), custom_call_target="tpu_custom_call" | custom-call | flops 1000000000 | bytes 4194304 | tf_op jit(solution)/shard_map/ends/pallas_call | solution.py:390
  147.6 0.0 copy-start.4
  147.6 1.0 copy-done.4
  148.5 0.0 copy-done
  148.6 16.4 %all-to-all-start.3 = ((bf16[16,256,128]{2,1,0:T(8,128)(2,1)}), bf16[16,256,128]{2,1,0:T(8,128)(2,1)}, u32[]{:S(2)}, u32[]{:S(2)}) async-start(bf16[16,256,128]{2,1,0:T(8,128)(2,1)} %copy-done.4), calls=%async_computation.3 | async-start | bytes 2097152 | tf_op jit(solution)/shard_map/all_to_all | solution.py:694
  165.0 0.1 dynamic-slice_negate_fusion
  165.0 0.1 copy.33
  165.1 0.1 fusion
  165.3 0.1 broadcast_multiply_fusion
  165.4 0.1 select_reduce_fusion.1
  165.5 0.1 copy.34
  165.5 0.1 broadcast_in_dim.70
  165.6 0.7 reshape.124.total_ref
  166.3 15.6 %all-to-all-done.3.ends_ref = bf16[16,256,128]{2,1,0:T(8,128)(2,1)} async-done(((bf16[16,256,128]{2,1,0:T(8,128)(2,1)}), bf16[16,256,128]{2,1,0:T(8,128)(2,1)}, u32[]{:S(2)}, u32[]{:S(2)}) %all-to-all-start.3) | async-done | bytes 1048608 | tf_op jit(solution)/shard_map/all_to_all | solution.py:694
  181.9 3.1 %chain.1 = bf16[16,512,128]{2,1,0:T(8,128)(2,1)} custom-call(s32[8]{0:T(128)} %stack.35.bounds_ref, bf16[16,256,128]{2,1,0:T(8,128)(2,1)} %all-to-all-done.3.ends_ref, f32[16,128]{1,0:T(8,128)} %reshape.124.total_ref, bf16[16,512,128]{2,1,0:T(8,128)(2,1)} %attend.1.both_in), custom_call_target="tpu_custom_call", output_to_operand_aliasing={{}: (3, {})} | custom-call | bytes 3145728 | tf_op jit(solution)/shard_map/chain/pallas_call | solution.py:438
  185.0 0.0 copy-start.11
  185.1 0.0 copy-start.7
  185.1 3.7 %all-to-all-start.4 = ((bf16[16,512,128]{2,1,0:T(8,128)(2,1)}), bf16[16,512,128]{2,1,0:T(8,128)(2,1)S(1)}, u32[]{:S(2)}, u32[]{:S(2)}) async-start(bf16[16,512,128]{2,1,0:T(8,128)(2,1)} %chain.1), calls=%async_computation.4 | async-start | bytes 4194304 | tf_op jit(solution)/shard_map/all_to_all | solution.py:703
  188.8 0.0 copy-done.11
  188.8 0.1 dynamic_slice.30
  188.9 0.1 reshape.125
  189.0 0.1 broadcast_in_dim.71
  189.1 0.1 broadcast_in_dim.72.gain_ref
  189.2 0.0 copy-done.7
  189.2 0.0 copy-start.1
  189.2 1.8 copy-done.1
  190.9 10.8 %inner.1 = (bf16[512,2048]{1,0:T(8,128)(2,1)S(1)}, bf16[512,256]{1,0:T(8,128)(2,1)S(1)}, bf16[512,64]{1,0:T(8,128)(2,1)S(1)}) custom-call(s32[8]{0:T(128)S(1)} %copy-done.7, bf16[16,656,128]{2,1,0:T(8,128)(2,1)S(1)} %copy-done.1, f32[32,512]{1,0:T(8,128)S(1)} %get-tuple-element.17.step_ref, f32[32,512]{1,0:T(8,128)S(1)} %get-tuple-element.18.decay_ref, ...), custom_call_target="tpu_custom_call" | custom-call | flops 4000000000 | bytes 8388608 | tf_op jit(solution)/shard_map/inner/pallas_call | solution.py:565
  201.7 0.0 copy-start.2
  201.7 1.3 copy-done.2
  203.1 14.2 %all-to-all-done.4.state_ref.attn_ref = bf16[16,512,128]{2,1,0:T(8,128)(2,1)S(1)} async-done(((bf16[16,512,128]{2,1,0:T(8,128)(2,1)}), bf16[16,512,128]{2,1,0:T(8,128)(2,1)S(1)}, u32[]{:S(2)}, u32[]{:S(2)}) %all-to-all-start.4) | async-done | bytes 2097184 | tf_op jit(solution)/shard_map/all_to_all | solution.py:703
  217.2 1.6 copy-done.3
  218.8 5.3 %finish.1 = (bf16[512,2048]{1,0:T(8,128)(2,1)}, bf16[512,1024]{1,0:T(8,128)(2,1)}) custom-call(bf16[16,512,128]{2,1,0:T(8,128)(2,1)S(1)} %all-to-all-done.4.state_ref.attn_ref, bf16[16,512,128]{2,1,0:T(8,128)(2,1)S(1)} %all-to-all-done.4.state_ref.attn_ref, bf16[512,2048]{1,0:T(8,128)(2,1)S(1)} %copy-done.3, bf16[512,256]{1,0:T(8,128)(2,1)S(1)} %get-tuple-element.20.c_ref, ...), custom_call_target="tpu_custom_call" | custom-call | flops 1000000000 | bytes 9437184 | tf_op jit(solution)/shard_map/finish/pallas_call | solution.py:626
  (10 shorter events, 0.0 us)
Async XLA Ops:
  7.2 105.8 %all-gather.2.cloned.1.call-start = ((), (), s32[]{:S(2)}) async-start(), calls=%async_computation.5 | async-start | bytes 4456448 | tf_op jit(solution)/shard_map/all_gather | solution.py:673
  7.2 1.0 copy-start.5
  91.0 1.9 copy-start.8
  99.0 3.9 %copy-start.9 = (f32[256]{0:T(256)S(1)}, f32[256]{0:T(256)}, u32[]{:S(2)}) copy-start(f32[256]{0:T(256)} %param.18) | copy-start | bytes 3076
  99.0 3.9 %copy-start.10 = (f32[256]{0:T(256)S(1)}, f32[256]{0:T(256)}, u32[]{:S(2)}) copy-start(f32[256]{0:T(256)} %param.17) | copy-start | bytes 3076
  99.0 42.2 %all-to-all-start.2 = ((bf16[16,656,128]{2,1,0:T(8,128)(2,1)}), bf16[16,656,128]{2,1,0:T(8,128)(2,1)S(1)}, u32[]{:S(2)}, u32[]{:S(2)}) async-start(bf16[16,656,128]{2,1,0:T(8,128)(2,1)} %get-tuple-element.14), calls=%async_computation.2 | async-start | bytes 5373952 | tf_op jit(solution)/shard_map/all_to_all | solution.py:687
  113.0 28.2 %copy-start.6 = (s32[8]{0:T(128)S(1)}, s32[8]{0:T(128)}, u32[]{:S(2)}) copy-start(s32[8]{0:T(128)} %stack.35.bounds_ref) | copy-start | bytes 100
  141.2 7.4 %copy-start = (bf16[16,656,128]{2,1,0:T(8,128)(2,1)}, bf16[16,656,128]{2,1,0:T(8,128)(2,1)S(1)}, u32[]{:S(2)}) copy-start(bf16[16,656,128]{2,1,0:T(8,128)(2,1)S(1)} %all-to-all-done.2.own_ref) | copy-start | bytes 8060932
  147.6 1.0 copy-start.4
  148.6 33.4 %all-to-all-start.3 = ((bf16[16,256,128]{2,1,0:T(8,128)(2,1)}), bf16[16,256,128]{2,1,0:T(8,128)(2,1)}, u32[]{:S(2)}, u32[]{:S(2)}) async-start(bf16[16,256,128]{2,1,0:T(8,128)(2,1)} %copy-done.4), calls=%async_computation.3 | async-start | bytes 2097152 | tf_op jit(solution)/shard_map/all_to_all | solution.py:694
  185.0 3.8 %copy-start.11 = (f32[256]{0:T(256)S(1)}, f32[256]{0:T(256)}, u32[]{:S(2)}) copy-start(f32[256]{0:T(256)} %param.19) | copy-start | bytes 3076
  185.1 4.1 %copy-start.7 = (s32[8]{0:T(128)S(1)}, s32[8]{0:T(128)}, u32[]{:S(2)}) copy-start(s32[8]{0:T(128)} %stack.35.bounds_ref) | copy-start | bytes 100
  185.1 32.2 %all-to-all-start.4 = ((bf16[16,512,128]{2,1,0:T(8,128)(2,1)}), bf16[16,512,128]{2,1,0:T(8,128)(2,1)S(1)}, u32[]{:S(2)}, u32[]{:S(2)}) async-start(bf16[16,512,128]{2,1,0:T(8,128)(2,1)} %chain.1), calls=%async_computation.4 | async-start | bytes 4194304 | tf_op jit(solution)/shard_map/all_to_all | solution.py:703
  189.2 1.8 copy-start.1
  201.7 1.4 copy-start.2
  217.2 1.6 copy-start.3
Sparse Core Ops, SparseCore 0:
  19.7 93.2 all-gather.1

commit v4 on v3

--- a/solution.py
+++ b/solution.py
@@ -179,10 +179,12 @@
     return pl.BlockSpec(shape, lambda *_: (0,) * len(shape))
 
 
+CALL_CHUNKS = SEQ // 2
 SUM_ROWS = 16
 
 
 def attend_kernel(
+    begin,
     inv_ref, bounds_ref, kv_hbm, q_hbm, out_ref, kv_ref, q_ref, keys_all, turned, peak, acc, top_far, acc_far, sems
 ):
     kv_copy = pltpu.make_async_copy(kv_hbm, kv_ref, sems.at[0])
@@ -203,7 +205,7 @@
         return carry
 
     kv_copy.wait()
-    lax.fori_loop(0, SEQ, arrange, 0, unroll=2)
+    lax.fori_loop(0, begin + CALL_CHUNKS, arrange, 0, unroll=2)
     q_copy.wait()
 
     row = lax.broadcasted_iota(jnp.int32, (1, q_rows), 1)
@@ -224,7 +226,8 @@
     def peak_of(scores):
         return jnp.max(scores, axis=0, keepdims=True)
 
-    def near_tiles(i, carry):
+    def near_tiles(n, carry):
+        i = begin + n
         queries = q_ref[i]
         first = doc_start(bounds_ref, i * CHUNK + in_chunk) - i * CHUNK
         before = jnp.maximum(i - 1, 0)
@@ -232,13 +235,14 @@
         here = jnp.where(own, scores_of(queries, i), NEG_BIG)
         there = jnp.where(key_at >= first + CHUNK, scores_of(queries, before), NEG_BIG)
         top = jnp.maximum(peak_of(here), peak_of(there))
-        peak[i] = top
-        acc[i] = mixed(here, top, i) + mixed(there, top, before)
+        peak[n] = top
+        acc[n] = mixed(here, top, i) + mixed(there, top, before)
         return carry
 
-    lax.fori_loop(0, SEQ, near_tiles, 0, unroll=2)
-
-    def far_tiles(i, carry):
+    lax.fori_loop(0, CALL_CHUNKS, near_tiles, 0, unroll=2)
+
+    def far_tiles(n, carry):
+        i = begin + n
         first = doc_start(bounds_ref, i * CHUNK) // CHUNK
         count = jnp.maximum(i - 1 - first, 0)
         fours = (count + 1) // 4
@@ -263,8 +267,8 @@
 
         @pl.when(count > 0)
         def _():
-            top_far[...] = peak[i]
-            acc_far[...] = acc[i]
+            top_far[...] = peak[n]
+            acc_far[...] = acc[n]
 
             def four(t, c):
                 add_tiles(i - 2 - 4 * t, 4)
@@ -276,44 +280,44 @@
             def _():
                 add_tiles(i - 2 - 4 * fours, 2)
 
-            acc[i] = acc_far[...]
+            acc[n] = acc_far[...]
 
         return carry
 
-    lax.fori_loop(2, SEQ, far_tiles, 0)
+    lax.fori_loop(2 if begin == 0 else 0, CALL_CHUNKS, far_tiles, 0)
 
     def finish(i, carry):
         result = acc[i, 0:ATT_DIM, :] / acc[i, ATT_DIM : ATT_DIM + 1, :]
-        out_ref[i, STATE:CHUNK, :] = jnp.transpose(result).astype(BF16)
+        out_ref[i] = jnp.transpose(result).astype(BF16)
         return carry
 
-    lax.fori_loop(0, SEQ, finish, 0, unroll=4)
-
-
-def attend(inv, bounds, kv, queries):
+    lax.fori_loop(0, CALL_CHUNKS, finish, 0, unroll=4)
+
+
+def attend(begin, inv, bounds, kv, queries):
     return pl.pallas_call(
-        attend_kernel,
+        functools.partial(attend_kernel, begin),
         grid_spec=pltpu.PrefetchScalarGridSpec(
             num_scalar_prefetch=2,
             grid=(1,),
             in_specs=[pl.BlockSpec(memory_space=pl.ANY), pl.BlockSpec(memory_space=pl.ANY)],
-            out_specs=whole(SEQ, CHUNK, LANES),
+            out_specs=whole(CALL_CHUNKS, HALF, LANES),
             scratch_shapes=[
                 pltpu.VMEM((STRETCHES, G_ROWS, LANES), BF16),
                 pltpu.VMEM((SEQ, PER * Q_ROWS, LANES), BF16),
                 pltpu.VMEM((TOKENS, ATT_DIM), BF16),
                 pltpu.VMEM((SEQ, ATT_DIM + SUM_ROWS, CHUNK), BF16),
-                pltpu.VMEM((SEQ, 1, PER * Q_ROWS), F32),
-                pltpu.VMEM((SEQ, ATT_DIM + SUM_ROWS, PER * Q_ROWS), F32),
+                pltpu.VMEM((CALL_CHUNKS, 1, PER * Q_ROWS), F32),
+                pltpu.VMEM((CALL_CHUNKS, ATT_DIM + SUM_ROWS, PER * Q_ROWS), F32),
                 pltpu.VMEM((1, PER * Q_ROWS), F32),
                 pltpu.VMEM((ATT_DIM + SUM_ROWS, PER * Q_ROWS), F32),
                 pltpu.SemaphoreType.DMA((2,)),
             ],
         ),
-        out_shape=jax.ShapeDtypeStruct((SEQ, CHUNK, LANES), BF16),
+        out_shape=jax.ShapeDtypeStruct((CALL_CHUNKS, HALF, LANES), BF16),
         compiler_params=params(60),
-        cost_estimate=pl.CostEstimate(flops=8_000_000_000, bytes_accessed=6 * MIB, transcendentals=8 * MIB),
-        name="attend",
+        cost_estimate=pl.CostEstimate(flops=4_000_000_000, bytes_accessed=6 * MIB, transcendentals=4 * MIB),
+        name=f"attend{begin}",
     )(inv, bounds, kv, queries)
 
 
@@ -421,20 +425,19 @@
     )(bounds, rows, biases, rates)
 
 
-def chain_kernel(bounds_ref, ends_ref, total_ref, both_in, both_out, states, sem):
+def chain_kernel(bounds_ref, ends_ref, total_ref, early_ref, late_ref, out_ref):
     state = jnp.zeros((STATE, LANES), F32)
     for c in range(SEQ):
-        states[c] = state.astype(BF16)
+        out_ref[c, 0:STATE, :] = state.astype(BF16)
+        rows = early_ref if c < CALL_CHUNKS else late_ref
+        out_ref[c, STATE:CHUNK, :] = rows[c % CALL_CHUNKS]
         if c < SEQ - 1:
             last_doc = doc_start(bounds_ref, jnp.int32((c + 1) * CHUNK - 1))
             keep = jnp.where(last_doc < c * CHUNK, total_ref[c : c + 1, :], 0.0)
             state = keep * state + ends_ref[c].astype(F32)
-    copy = pltpu.make_async_copy(states, both_out.at[:, pl.ds(0, STATE), :], sem)
-    copy.start()
-    copy.wait()
-
-
-def chain(bounds, arrived, totals, both):
+
+
+def chain(bounds, arrived, totals, early, late):
     return pl.pallas_call(
         chain_kernel,
         grid_spec=pltpu.PrefetchScalarGridSpec(
@@ -443,17 +446,16 @@
             in_specs=[
                 whole(SEQ, STATE, LANES),
                 whole(SEQ, LANES),
-                pl.BlockSpec(memory_space=pl.ANY),
-            ],
-            out_specs=pl.BlockSpec(memory_space=pl.ANY),
-            scratch_shapes=[pltpu.VMEM((SEQ, STATE, LANES), BF16), pltpu.SemaphoreType.DMA],
+                whole(CALL_CHUNKS, HALF, LANES),
+                whole(CALL_CHUNKS, HALF, LANES),
+            ],
+            out_specs=whole(SEQ, CHUNK, LANES),
         ),
         out_shape=jax.ShapeDtypeStruct((SEQ, CHUNK, LANES), BF16),
-        input_output_aliases={3: 0},
-        compiler_params=params(60),
-        cost_estimate=pl.CostEstimate(flops=0, bytes_accessed=3 * MIB, transcendentals=0),
+        compiler_params=params(24),
+        cost_estimate=pl.CostEstimate(flops=0, bytes_accessed=5 * MIB, transcendentals=0),
         name="chain",
-    )(bounds, arrived, totals, both)
+    )(bounds, arrived, totals, early, late)
 
 
 def inner_kernel(
@@ -689,7 +691,8 @@
     biases = cut(dt_bias, group_first, GROUP_HEADS)
     rates = cut(ssm_rate, group_first, GROUP_HEADS)
     gains = cut(skip_gain, group_first, GROUP_HEADS)
-    attended, own_bounds = lax.optimization_barrier((attend(inv, bounds, kv, queries), bounds))
+    early, own_bounds = lax.optimization_barrier((attend(0, inv, bounds, kv, queries), bounds))
+    late = attend(CALL_CHUNKS, inv, own_bounds, kv, queries)
     own_ends, steps, decays = ends(own_bounds, own_rows, biases[:, None], rates[:, None])
     arrived = exchange(own_ends, "seq")
 
@@ -700,7 +703,7 @@
     lost = jnp.sum(jnp.where(chunk_of, lost[None], 0.0), axis=1)
     totals = jnp.repeat(jnp.exp(lost), HEAD_DIM, axis=1)
 
-    both = exchange(chain(bounds, arrived, totals, attended), "seq")
+    both = exchange(chain(bounds, arrived, totals, early, late), "seq")
     inner_out, c_rows, reach = inner(
         bounds, own_rows, steps, decays, jnp.repeat(gains.reshape(SEQ, 1, 2), HEAD_DIM, axis=2)
     )

time: 234 us -> 229 us (0.979)
  waiting for transfers between devices: 38.6 us -> 32.7 us
  starting transfers between devices: 24 us -> 19.8 us
  Pallas kernels: 63.4 us -> 67.6 us
    all_to_all x1, waiting for transfers between devices: 15.6 us -> 2.27 us  [shards(): arrived = exchange(own_ends, 'seq')]
    all_to_all x1, waiting for transfers between devices: 4.27 us -> 11.7 us  [shards(): own_rows = exchange(to_owners, 'seq')]
    pallas_call x1 -> x2, Pallas kernels: 23.9 us -> 30.5 us  [attend(): pl.pallas_call(functools.partial(attend_kernel, begin), grid_spec=pltpu.P...]
    all_to_all x1, starting transfers between devices: 16.4 us -> 10.8 us  [shards(): arrived = exchange(own_ends, 'seq')]
    unnamed x24 -> x30, local copies, waits for them, and re-layouts: 7.19 us -> 9.57 us
  transfers between devices with their start and end apart: 4 -> 4, of which waited for: 4 -> 4; matrix products, arithmetic and copies ran while one was open for 6% -> 6% of each run, Pallas kernels for 21% -> 24%
where the time goes in v4:
time: 229 us; the launch traced here: 227 us
  blocking collectives  70.1 us (31%)
  Pallas kernels  67.6 us (30%)
  waiting for transfers between devices  32.7 us (14%)
  starting transfers between devices  19.8 us (9%)
  local copies, waits for them, and re-layouts  19.4 us (8%)
  between operations  14.2 us (6%)
  other arithmetic  3.01 us (1%)
    all_to_all x1, blocking collectives, shards(): hop = exchange(to_heads.reshape(STRETCHES, HOP_ROWS, LANES), ('seq', 'mp'))  59.3 us
    pallas_call x2, Pallas kernels, attend(): pl.pallas_call(functools.partial(attend_kernel, begin), grid_spec=pltpu.P...  30.5 us
    all_to_all x1, waiting for transfers between devices, shards(): both = exchange(chain(bounds, arrived, totals, early, late), 'seq')  14.4 us
    all_to_all x1, waiting for transfers between devices, shards(): own_rows = exchange(to_owners, 'seq')  11.7 us
    all_to_all x1, blocking collectives, shards(): exchange(pack_kv(stretch_kv), 'mp')  10.8 us
    all_to_all x1, starting transfers between devices, shards(): arrived = exchange(own_ends, 'seq')  10.8 us
    pallas_call x1, Pallas kernels, inner(): pl.pallas_call(inner_kernel, grid_spec=pltpu.PrefetchScalarGridSpec(num_s...  10.8 us
    unnamed x30, local copies, waits for them, and re-layouts  9.57 us
  transfers between devices with their start and end apart: 4, of which 4 were waited for; matrix products, arithmetic and copies ran while one was open for 6% of the time, Pallas kernels for 24%

profile of v4, /device:TPU:2, one launch (start us, length us, event | category | flops | bytes accessed | tf_op | source)
XLA Modules:
  0.0 226.9 jit_solution(17480359302202843934)
XLA Ops:
  7.2 0.0 all-gather.2.cloned.1.call-start
  7.2 0.0 copy-start.8
  7.2 0.9 copy-done.8
  8.2 0.6 pack_kv.1
  8.7 10.8 %all_to_all.25 = bf16[8,128,128]{2,1,0:T(8,128)(2,1)} all-to-all(bf16[8,128,128]{2,1,0:T(8,128)(2,1)S(1)} %pack_kv.1), channel_id=1, replica_groups=mesh['seq'=16,'mp'=8] {'mp'}, dimensions={0} | all-to-all | bytes 524288 | tf_op jit(solution)/shard_map/all_to_all | solution.py:675
  19.6 0.0 all-gather.2.cloned.1.call-update
  19.6 0.9 copy.29
  20.5 0.7 reshape.122.dt_ref
  21.2 1.2 dynamic_slice.24
  22.4 0.8 dynamic_slice.23
  23.2 0.7 add_convert_fusion
  23.9 0.6 broadcast_in_dim.62.info_ref
  24.5 7.1 %pack.1 = bf16[16,8,120,128]{3,2,1,0:T(8,128)(2,1)} custom-call(bf16[64,16384]{1,0:T(8,128)(2,1)} %x_ref.1, bf16[64,2,2048]{2,1,0:T(2,128)(2,1)} %bc_ref.1, bf16[64,8192]{1,0:T(8,128)(2,1)} %q_ref.1, bf16[128,128]{1,0:T(8,128)(2,1)} %reshape.122.dt_ref, f32[8,128]{1,0:T(8,128)} %broadcast_in_dim.62.info_ref), custom_call_target="tpu_custom_call" | custom-call | bytes 9437184 | tf_op jit(solution)/shard_map/pack/pallas_call | solution.py:70
  31.6 59.3 %all_to_all.26.hop_ref = bf16[128,120,128]{2,1,0:T(8,128)(2,1)S(1)} all-to-all(bf16[128,120,128]{2,1,0:T(8,128)(2,1)} %bitcast.16), channel_id=1, replica_groups=mesh['seq'=16,'mp'=8] {'seq','mp'}, dimensions={0} | all-to-all | bytes 7864320 | tf_op jit(solution)/shard_map/all_to_all | solution.py:679
  91.0 0.1 slice_convert_fusion
  91.1 0.2 slice_reduce_fusion
  91.3 1.0 select_reduce_fusion.inv_ref
  92.2 0.6 copy-done.11
  92.8 6.2 %place.1 = (bf16[16,656,128]{2,1,0:T(8,128)(2,1)}, bf16[16,256,128]{2,1,0:T(8,128)(2,1)}) custom-call(s32[128]{0:T(128)} %select_reduce_fusion.inv_ref, bf16[128,120,128]{2,1,0:T(8,128)(2,1)} %copy-done.11), custom_call_target="tpu_custom_call" | custom-call | bytes 6291456 | tf_op jit(solution)/shard_map/place/pallas_call | solution.py:133
  99.0 3.9 %all-to-all-start.2 = ((bf16[16,656,128]{2,1,0:T(8,128)(2,1)}), bf16[16,656,128]{2,1,0:T(8,128)(2,1)S(1)}, u32[]{:S(2)}, u32[]{:S(2)}) async-start(bf16[16,656,128]{2,1,0:T(8,128)(2,1)} %get-tuple-element.14), calls=%async_computation.2 | async-start | bytes 5373952 | tf_op jit(solution)/shard_map/all_to_all | solution.py:689
  102.9 0.0 copy-done.12
  102.9 0.0 copy-done.13
  102.9 0.1 dynamic-slice_bitcast_fusion
  103.0 0.1 copy.30.bias_ref
  103.1 0.1 copy.31.rate_ref
  103.2 0.1 dynamic_slice.29
  103.2 0.1 dynamic-slice_negate_fusion
  103.3 0.1 copy.32
  103.4 0.8 convert_reduce_fusion
  104.2 4.4 %stack.35.bounds_ref = s32[8]{0:T(128)} concatenate(s32[1]{0:T(128)} %bitcast.3, s32[1]{0:T(128)} %bitcast.4, s32[1]{0:T(128)} %bitcast.5, s32[1]{0:T(128)} %bitcast.6, s32[1]{0:T(128)} %bitcast.7, s32[1]{0:T(128)} %bitcast.8, s32[1]{0:T(128)} %bitcast.9, s32[1]{0:T(128)} %bitcast.10), dimensions={0} | concatenate | bytes 64 | tf_op jit(solution)/shard_map/stack | solution.py:685
  108.7 4.3 %all-gather.2.cloned.1.call-done.kv_hbm = bf16[128,128,128]{2,1,0:T(8,128)(2,1)} async-done(((bf16[8,128,128]{2,1,0:T(8,128)(2,1)}), bf16[128,128,128]{2,1,0:T(8,128)(2,1)}) %all-gather.2.cloned.1.call-update) | async-done | bytes 4194320 | tf_op jit(solution)/shard_map/all_gather | solution.py:675
  113.0 16.3 %attend0.1.early_ref = bf16[8,256,128]{2,1,0:T(8,128)(2,1)} custom-call(s32[128]{0:T(128)} %select_reduce_fusion.inv_ref, s32[8]{0:T(128)} %stack.35.bounds_ref, bf16[128,128,128]{2,1,0:T(8,128)(2,1)} %all-gather.2.cloned.1.call-done.kv_hbm, bf16[16,256,128]{2,1,0:T(8,128)(2,1)} %get-tuple-element.12.q_hbm), custom_call_target="tpu_custom_call" | custom-call | flops 4000000000 | bytes 6291456 | tf_op jit(solution)/shard_map/attend0/pallas_call | solution.py:298
  129.4 11.7 %all-to-all-done.2.own_ref = bf16[16,656,128]{2,1,0:T(8,128)(2,1)S(1)} async-done(((bf16[16,656,128]{2,1,0:T(8,128)(2,1)}), bf16[16,656,128]{2,1,0:T(8,128)(2,1)S(1)}, u32[]{:S(2)}, u32[]{:S(2)}) %all-to-all-start.2) | async-done | bytes 2687008 | tf_op jit(solution)/shard_map/all_to_all | solution.py:689
  141.0 0.0 copy-done.9
  141.0 6.4 %ends.1 = (bf16[16,256,128]{2,1,0:T(8,128)(2,1)S(1)}, f32[32,512]{1,0:T(8,128)S(1)}, f32[32,512]{1,0:T(8,128)S(1)}) custom-call(s32[8]{0:T(128)S(1)} %copy-done.9, bf16[16,656,128]{2,1,0:T(8,128)(2,1)S(1)} %all-to-all-done.2.own_ref, f32[32,1]{1,0:T(8,128)S(1)} %copy.30.bias_ref, f32[32,1]{1,0:T(8,128)S(1)} %copy.31.rate_ref), custom_call_target="tpu_custom_call" | custom-call | flops 1000000000 | bytes 4194304 | tf_op jit(solution)/shard_map/ends/pallas_call | solution.py:394
  147.4 0.0 copy-start.5
  147.4 1.0 copy-done.5
  148.4 0.0 copy-done.1
  148.4 10.8 %all-to-all-start.3 = ((bf16[16,256,128]{2,1,0:T(8,128)(2,1)}), bf16[16,256,128]{2,1,0:T(8,128)(2,1)S(1)}, u32[]{:S(2)}, u32[]{:S(2)}) async-start(bf16[16,256,128]{2,1,0:T(8,128)(2,1)} %copy-done.5), calls=%async_computation.3 | async-start | bytes 2097152 | tf_op jit(solution)/shard_map/all_to_all | solution.py:697
  159.2 0.1 fusion
  159.3 0.1 broadcast_multiply_fusion
  159.4 0.1 select_reduce_fusion.1
  159.5 0.1 copy.33
  159.6 0.1 broadcast_in_dim.70
  159.7 0.1 reshape.124.total_ref
  159.8 14.1 %attend8.1.late_ref = bf16[8,256,128]{2,1,0:T(8,128)(2,1)} custom-call(s32[128]{0:T(128)} %select_reduce_fusion.inv_ref, s32[8]{0:T(128)} %stack.35.bounds_ref, bf16[128,128,128]{2,1,0:T(8,128)(2,1)} %all-gather.2.cloned.1.call-done.kv_hbm, bf16[16,256,128]{2,1,0:T(8,128)(2,1)} %get-tuple-element.12.q_hbm), custom_call_target="tpu_custom_call" | custom-call | flops 4000000000 | bytes 6291456 | tf_op jit(solution)/shard_map/attend8/pallas_call | solution.py:298
  173.9 2.3 all-to-all-done.3.ends_ref
  176.1 0.0 copy-done.6
  176.1 0.0 copy-done.10
  176.1 1.0 copy-done.7
  177.2 0.8 chain.1
  178.0 0.0 copy-start
  178.0 1.3 copy-done
  179.3 5.1 %all-to-all-start.4 = ((bf16[16,512,128]{2,1,0:T(8,128)(2,1)}), bf16[16,512,128]{2,1,0:T(8,128)(2,1)S(1)}, u32[]{:S(2)}, u32[]{:S(2)}) async-start(bf16[16,512,128]{2,1,0:T(8,128)(2,1)} %copy-done), calls=%async_computation.4 | async-start | bytes 4194304 | tf_op jit(solution)/shard_map/all_to_all | solution.py:706
  184.5 0.1 dynamic_slice.30
  184.5 0.1 reshape.125
  184.6 0.1 broadcast_in_dim.71
  184.7 0.1 broadcast_in_dim.72.gain_ref
  184.8 1.8 copy-done.2
  186.6 10.8 %inner.1 = (bf16[512,2048]{1,0:T(8,128)(2,1)S(1)}, bf16[512,256]{1,0:T(8,128)(2,1)S(1)}, bf16[512,64]{1,0:T(8,128)(2,1)S(1)}) custom-call(s32[8]{0:T(128)S(1)} %copy-done.10, bf16[16,656,128]{2,1,0:T(8,128)(2,1)S(1)} %copy-done.2, f32[32,512]{1,0:T(8,128)S(1)} %get-tuple-element.17.step_ref, f32[32,512]{1,0:T(8,128)S(1)} %get-tuple-element.18.decay_ref, ...), custom_call_target="tpu_custom_call" | custom-call | flops 4000000000 | bytes 8388608 | tf_op jit(solution)/shard_map/inner/pallas_call | solution.py:567
  197.4 1.3 copy-done.3
  198.7 14.4 %all-to-all-done.4.state_ref.attn_ref = bf16[16,512,128]{2,1,0:T(8,128)(2,1)S(1)} async-done(((bf16[16,512,128]{2,1,0:T(8,128)(2,1)}), bf16[16,512,128]{2,1,0:T(8,128)(2,1)S(1)}, u32[]{:S(2)}, u32[]{:S(2)}) %all-to-all-start.4) | async-done | bytes 2097184 | tf_op jit(solution)/shard_map/all_to_all | solution.py:706
  213.1 1.6 copy-done.4
  214.7 5.3 %finish.1 = (bf16[512,2048]{1,0:T(8,128)(2,1)}, bf16[512,1024]{1,0:T(8,128)(2,1)}) custom-call(bf16[16,512,128]{2,1,0:T(8,128)(2,1)S(1)} %all-to-all-done.4.state_ref.attn_ref, bf16[16,512,128]{2,1,0:T(8,128)(2,1)S(1)} %all-to-all-done.4.state_ref.attn_ref, bf16[512,2048]{1,0:T(8,128)(2,1)S(1)} %copy-done.4, bf16[512,256]{1,0:T(8,128)(2,1)S(1)} %get-tuple-element.20.c_ref, ...), custom_call_target="tpu_custom_call" | custom-call | flops 1000000000 | bytes 9437184 | tf_op jit(solution)/shard_map/finish/pallas_call | solution.py:628
  (17 shorter events, 0.0 us)
Async XLA Ops:
  7.2 105.8 %all-gather.2.cloned.1.call-start = ((), (), s32[]{:S(2)}) async-start(), calls=%async_computation.5 | async-start | bytes 4456448 | tf_op jit(solution)/shard_map/all_gather | solution.py:675
  7.2 1.0 copy-start.8
  91.0 1.9 copy-start.11
  99.0 3.9 %copy-start.12 = (f32[256]{0:T(256)S(1)}, f32[256]{0:T(256)}, u32[]{:S(2)}) copy-start(f32[256]{0:T(256)} %param.18) | copy-start | bytes 3076
  99.0 3.9 %copy-start.13 = (f32[256]{0:T(256)S(1)}, f32[256]{0:T(256)}, u32[]{:S(2)}) copy-start(f32[256]{0:T(256)} %param.17) | copy-start | bytes 3076
  99.0 42.0 %all-to-all-start.2 = ((bf16[16,656,128]{2,1,0:T(8,128)(2,1)}), bf16[16,656,128]{2,1,0:T(8,128)(2,1)S(1)}, u32[]{:S(2)}, u32[]{:S(2)}) async-start(bf16[16,656,128]{2,1,0:T(8,128)(2,1)} %get-tuple-element.14), calls=%async_computation.2 | async-start | bytes 5373952 | tf_op jit(solution)/shard_map/all_to_all | solution.py:689
  113.0 28.0 %copy-start.9 = (s32[8]{0:T(128)S(1)}, s32[8]{0:T(128)}, u32[]{:S(2)}) copy-start(s32[8]{0:T(128)} %stack.35.bounds_ref) | copy-start | bytes 100
  141.0 7.4 %copy-start.1 = (bf16[16,656,128]{2,1,0:T(8,128)(2,1)}, bf16[16,656,128]{2,1,0:T(8,128)(2,1)S(1)}, u32[]{:S(2)}) copy-start(bf16[16,656,128]{2,1,0:T(8,128)(2,1)S(1)} %all-to-all-done.2.own_ref) | copy-start | bytes 8060932
  147.4 1.0 copy-start.5
  148.4 27.8 %all-to-all-start.3 = ((bf16[16,256,128]{2,1,0:T(8,128)(2,1)}), bf16[16,256,128]{2,1,0:T(8,128)(2,1)S(1)}, u32[]{:S(2)}, u32[]{:S(2)}) async-start(bf16[16,256,128]{2,1,0:T(8,128)(2,1)} %copy-done.5), calls=%async_computation.3 | async-start | bytes 2097152 | tf_op jit(solution)/shard_map/all_to_all | solution.py:697
  159.7 16.4 %copy-start.6 = (bf16[8,256,128]{2,1,0:T(8,128)(2,1)S(1)}, bf16[8,256,128]{2,1,0:T(8,128)(2,1)}, u32[]{:S(2)}) copy-start(bf16[8,256,128]{2,1,0:T(8,128)(2,1)} %attend0.1.early_ref) | copy-start | bytes 1572868
  159.7 16.4 %copy-start.10 = (s32[8]{0:T(128)S(1)}, s32[8]{0:T(128)}, u32[]{:S(2)}) copy-start(s32[8]{0:T(128)} %stack.35.bounds_ref) | copy-start | bytes 100
  176.1 1.0 copy-start.7
  178.0 1.3 copy-start
  179.3 5.1 %copy-start.14 = (f32[256]{0:T(256)S(1)}, f32[256]{0:T(256)}, u32[]{:S(2)}) copy-start(f32[256]{0:T(256)} %param.19) | copy-start | bytes 3076
  179.3 33.8 %all-to-all-start.4 = ((bf16[16,512,128]{2,1,0:T(8,128)(2,1)}), bf16[16,512,128]{2,1,0:T(8,128)(2,1)S(1)}, u32[]{:S(2)}, u32[]{:S(2)}) async-start(bf16[16,512,128]{2,1,0:T(8,128)(2,1)} %copy-done), calls=%async_computation.4 | async-start | bytes 4194304 | tf_op jit(solution)/shard_map/all_to_all | solution.py:706
  184.8 1.8 copy-start.2
  197.3 1.3 copy-start.3
  213.1 1.6 copy-start.4
Sparse Core Ops, SparseCore 0:
  19.7 93.2 all-gather.1

commit v5 on v4

--- a/solution.py
+++ b/solution.py
@@ -38,6 +38,7 @@
 K_AT, V_AT, G_ROWS = 0, 64, 128
 GROUP_HEADS = SSM_HEADS // GROUPS
 PAIRS = 2
+MANY = 4
 NEG_BIG = -1e30
 F32 = jnp.float32
 BF16 = jnp.bfloat16
@@ -170,9 +171,13 @@
     upper = lax.broadcasted_iota(jnp.int32, (width, width), 0) <= lax.broadcasted_iota(
         jnp.int32, (width, width), 1
     )
-    return lax.dot(
-        rows, upper.astype(F32), precision=lax.Precision.HIGHEST, preferred_element_type=F32
-    )
+    upper = upper.astype(BF16)
+    total = jnp.zeros_like(rows)
+    for _ in range(3):
+        part = rows.astype(BF16)
+        rows = rows - part.astype(F32)
+        total = total + jnp.dot(part, upper, preferred_element_type=F32)
+    return total
 
 
 def whole(*shape):
@@ -383,8 +388,8 @@
         load = jnp.exp(log_sum[:, CHUNK - 1 : CHUNK] - log_sum)
         parts[...] = as_parts(jnp.where(pos >= last_doc, step_ref[...] * load, 0.0), 2)
 
-    for k in range(PAIRS):
-        pair = pl.program_id(0) * PAIRS + k
+    for k in range(MANY):
+        pair = pl.program_id(0) * MANY + k
         xs = channels(own_ref, pair)
         driven = (spread_heads(parts[...], pair, LANES) * xs).astype(BF16)
         out_ref[k] = jnp.dot(turned[...], driven, preferred_element_type=F32).astype(BF16)
@@ -395,14 +400,14 @@
         ends_kernel,
         grid_spec=pltpu.PrefetchScalarGridSpec(
             num_scalar_prefetch=1,
-            grid=(SEQ // PAIRS,),
+            grid=(SEQ // MANY,),
             in_specs=[
                 whole(SEQ, OWNER_ROWS, LANES),
                 whole(GROUP_HEADS, 1),
                 whole(GROUP_HEADS, 1),
             ],
             out_specs=[
-                pl.BlockSpec((PAIRS, STATE, LANES), lambda g, *_: (g, 0, 0)),
+                pl.BlockSpec((MANY, STATE, LANES), lambda g, *_: (g, 0, 0)),
                 whole(GROUP_HEADS, CHUNK),
                 whole(GROUP_HEADS, CHUNK),
             ],
@@ -616,8 +621,8 @@
                     s, st * Q_ROWS : (st + 1) * Q_ROWS, :
                 ]
 
-    for k in range(PAIRS):
-        pair = pl.program_id(0) * PAIRS + k
+    for k in range(MANY):
+        pair = pl.program_id(0) * MANY + k
         cols = slice(k * LANES, (k + 1) * LANES)
         reached = jnp.dot(c_ref[...], state_ref[k], preferred_element_type=F32)
         reached = spread_heads(reach_ref[...], pair, LANES) * reached
@@ -627,16 +632,16 @@
 def finish(both, inner_out, c_rows, reach):
     return pl.pallas_call(
         finish_kernel,
-        grid=(SEQ // PAIRS,),
+        grid=(SEQ // MANY,),
         in_specs=[
-            pl.BlockSpec((PAIRS, STATE, LANES), lambda g: (g, 0, 0)),
+            pl.BlockSpec((MANY, STATE, LANES), lambda g: (g, 0, 0)),
             pl.BlockSpec((SEQ, HALF, LANES), lambda g: (0, 1, 0)),
-            pl.BlockSpec((CHUNK, PAIRS * LANES), lambda g: (0, g)),
+            pl.BlockSpec((CHUNK, MANY * LANES), lambda g: (0, g)),
             whole(CHUNK, STATE),
             whole(CHUNK, 2 * GROUP_HEADS),
         ],
         out_specs=[
-            pl.BlockSpec((CHUNK, PAIRS * LANES), lambda g: (0, g)),
+            pl.BlockSpec((CHUNK, MANY * LANES), lambda g: (0, g)),
             whole(CHUNK, PER * LANES),
         ],
         out_shape=[

time: 229 us -> 227 us (level); the launches traced: 227 us -> 228 us
  starting transfers between devices: 19.8 us -> 22.1 us
    all_to_all x1, waiting for transfers between devices: 11.7 us -> 14.3 us  [shards(): own_rows = exchange(to_owners, 'seq')]
  transfers between devices with their start and end apart: 4 -> 4, of which waited for: 4 -> 3; matrix products, arithmetic and copies ran while one was open for 6% -> 6% of each run, Pallas kernels for 24% -> 24%
where the time goes in v5:
time: 227 us; the launch traced here: 228 us
  blocking collectives  70.1 us (31%)
  Pallas kernels  65.9 us (29%)
  waiting for transfers between devices  33.3 us (15%)
  starting transfers between devices  22.1 us (10%)
  local copies, waits for them, and re-layouts  19.4 us (9%)
  between operations  14.2 us (6%)
  other arithmetic  3.01 us (1%)
    all_to_all x1, blocking collectives, shards(): hop = exchange(to_heads.reshape(STRETCHES, HOP_ROWS, LANES), ('seq', 'mp'))  59.3 us
    pallas_call x2, Pallas kernels, attend(): pl.pallas_call(functools.partial(attend_kernel, begin), grid_spec=pltpu.P...  31.1 us
    all_to_all x1, waiting for transfers between devices, shards(): both = exchange(chain(bounds, arrived, totals, early, late), 'seq')  14.7 us
    all_to_all x1, waiting for transfers between devices, shards(): own_rows = exchange(to_owners, 'seq')  14.3 us
    all_to_all x1, blocking collectives, shards(): exchange(pack_kv(stretch_kv), 'mp')  10.8 us
    all_to_all x1, starting transfers between devices, shards(): arrived = exchange(own_ends, 'seq')  10.8 us
    pallas_call x1, Pallas kernels, inner(): pl.pallas_call(inner_kernel, grid_spec=pltpu.PrefetchScalarGridSpec(num_s...  10.6 us
    unnamed x30, local copies, waits for them, and re-layouts  9.56 us
  transfers between devices with their start and end apart: 4, of which 3 were waited for; matrix products, arithmetic and copies ran while one was open for 6% of the time, Pallas kernels for 24%

profile of v5, /device:TPU:2, one launch (start us, length us, event | category | flops | bytes accessed | tf_op | source)
XLA Modules:
  0.0 228.0 jit_solution(10270546613301885723)
XLA Ops:
  7.2 0.0 all-gather.2.cloned.1.call-start
  7.2 0.0 copy-start.8
  7.2 0.9 copy-done.8
  8.2 0.6 pack_kv.1
  8.7 10.8 %all_to_all.25 = bf16[8,128,128]{2,1,0:T(8,128)(2,1)} all-to-all(bf16[8,128,128]{2,1,0:T(8,128)(2,1)S(1)} %pack_kv.1), channel_id=1, replica_groups=mesh['seq'=16,'mp'=8] {'mp'}, dimensions={0} | all-to-all | bytes 524288 | tf_op jit(solution)/shard_map/all_to_all | solution.py:680
  19.6 0.0 all-gather.2.cloned.1.call-update
  19.6 0.9 copy.29
  20.5 0.7 reshape.122.dt_ref
  21.2 1.2 dynamic_slice.24
  22.4 0.8 dynamic_slice.23
  23.2 0.7 add_convert_fusion
  23.9 0.6 broadcast_in_dim.62.info_ref
  24.5 7.1 %pack.1 = bf16[16,8,120,128]{3,2,1,0:T(8,128)(2,1)} custom-call(bf16[64,16384]{1,0:T(8,128)(2,1)} %x_ref.1, bf16[64,2,2048]{2,1,0:T(2,128)(2,1)} %bc_ref.1, bf16[64,8192]{1,0:T(8,128)(2,1)} %q_ref.1, bf16[128,128]{1,0:T(8,128)(2,1)} %reshape.122.dt_ref, f32[8,128]{1,0:T(8,128)} %broadcast_in_dim.62.info_ref), custom_call_target="tpu_custom_call" | custom-call | bytes 9437184 | tf_op jit(solution)/shard_map/pack/pallas_call | solution.py:71
  31.6 59.3 %all_to_all.26.hop_ref = bf16[128,120,128]{2,1,0:T(8,128)(2,1)S(1)} all-to-all(bf16[128,120,128]{2,1,0:T(8,128)(2,1)} %bitcast.16), channel_id=1, replica_groups=mesh['seq'=16,'mp'=8] {'seq','mp'}, dimensions={0} | all-to-all | bytes 7864320 | tf_op jit(solution)/shard_map/all_to_all | solution.py:684
  91.0 0.1 slice_convert_fusion
  91.1 0.2 slice_reduce_fusion
  91.3 1.0 select_reduce_fusion.inv_ref
  92.2 0.6 copy-done.11
  92.8 6.2 %place.1 = (bf16[16,656,128]{2,1,0:T(8,128)(2,1)}, bf16[16,256,128]{2,1,0:T(8,128)(2,1)}) custom-call(s32[128]{0:T(128)} %select_reduce_fusion.inv_ref, bf16[128,120,128]{2,1,0:T(8,128)(2,1)} %copy-done.11), custom_call_target="tpu_custom_call" | custom-call | bytes 6291456 | tf_op jit(solution)/shard_map/place/pallas_call | solution.py:134
  99.0 3.9 %all-to-all-start.2 = ((bf16[16,656,128]{2,1,0:T(8,128)(2,1)}), bf16[16,656,128]{2,1,0:T(8,128)(2,1)S(1)}, u32[]{:S(2)}, u32[]{:S(2)}) async-start(bf16[16,656,128]{2,1,0:T(8,128)(2,1)} %get-tuple-element.14), calls=%async_computation.2 | async-start | bytes 5373952 | tf_op jit(solution)/shard_map/all_to_all | solution.py:694
  102.9 0.0 copy-done.12
  102.9 0.0 copy-done.13
  102.9 0.1 dynamic-slice_bitcast_fusion
  103.0 0.1 copy.30.bias_ref
  103.1 0.1 copy.31.rate_ref
  103.2 0.1 dynamic_slice.29
  103.2 0.1 dynamic-slice_negate_fusion
  103.3 0.1 copy.32
  103.4 0.8 convert_reduce_fusion
  104.2 4.4 %stack.35.bounds_ref = s32[8]{0:T(128)} concatenate(s32[1]{0:T(128)} %bitcast.3, s32[1]{0:T(128)} %bitcast.4, s32[1]{0:T(128)} %bitcast.5, s32[1]{0:T(128)} %bitcast.6, s32[1]{0:T(128)} %bitcast.7, s32[1]{0:T(128)} %bitcast.8, s32[1]{0:T(128)} %bitcast.9, s32[1]{0:T(128)} %bitcast.10), dimensions={0} | concatenate | bytes 64 | tf_op jit(solution)/shard_map/stack | solution.py:690
  108.7 4.3 %all-gather.2.cloned.1.call-done.kv_hbm = bf16[128,128,128]{2,1,0:T(8,128)(2,1)} async-done(((bf16[8,128,128]{2,1,0:T(8,128)(2,1)}), bf16[128,128,128]{2,1,0:T(8,128)(2,1)}) %all-gather.2.cloned.1.call-update) | async-done | bytes 4194320 | tf_op jit(solution)/shard_map/all_gather | solution.py:680
  113.0 13.6 %attend0.1.early_ref = bf16[8,256,128]{2,1,0:T(8,128)(2,1)} custom-call(s32[128]{0:T(128)} %select_reduce_fusion.inv_ref, s32[8]{0:T(128)} %stack.35.bounds_ref, bf16[128,128,128]{2,1,0:T(8,128)(2,1)} %all-gather.2.cloned.1.call-done.kv_hbm, bf16[16,256,128]{2,1,0:T(8,128)(2,1)} %get-tuple-element.12.q_hbm), custom_call_target="tpu_custom_call" | custom-call | flops 4000000000 | bytes 6291456 | tf_op jit(solution)/shard_map/attend0/pallas_call | solution.py:303
  126.6 14.3 %all-to-all-done.2.own_ref = bf16[16,656,128]{2,1,0:T(8,128)(2,1)S(1)} async-done(((bf16[16,656,128]{2,1,0:T(8,128)(2,1)}), bf16[16,656,128]{2,1,0:T(8,128)(2,1)S(1)}, u32[]{:S(2)}, u32[]{:S(2)}) %all-to-all-start.2) | async-done | bytes 2687008 | tf_op jit(solution)/shard_map/all_to_all | solution.py:694
  140.9 0.0 copy-done.9
  140.9 5.5 %ends.1 = (bf16[16,256,128]{2,1,0:T(8,128)(2,1)S(1)}, f32[32,512]{1,0:T(8,128)S(1)}, f32[32,512]{1,0:T(8,128)S(1)}) custom-call(s32[8]{0:T(128)S(1)} %copy-done.9, bf16[16,656,128]{2,1,0:T(8,128)(2,1)S(1)} %all-to-all-done.2.own_ref, f32[32,1]{1,0:T(8,128)S(1)} %copy.30.bias_ref, f32[32,1]{1,0:T(8,128)S(1)} %copy.31.rate_ref), custom_call_target="tpu_custom_call" | custom-call | flops 1000000000 | bytes 4194304 | tf_op jit(solution)/shard_map/ends/pallas_call | solution.py:399
  146.5 0.0 copy-start.5
  146.5 1.0 copy-done.5
  147.4 0.0 copy-done.1
  147.4 10.8 %all-to-all-start.3 = ((bf16[16,256,128]{2,1,0:T(8,128)(2,1)}), bf16[16,256,128]{2,1,0:T(8,128)(2,1)S(1)}, u32[]{:S(2)}, u32[]{:S(2)}) async-start(bf16[16,256,128]{2,1,0:T(8,128)(2,1)} %copy-done.5), calls=%async_computation.3 | async-start | bytes 2097152 | tf_op jit(solution)/shard_map/all_to_all | solution.py:702
  158.2 0.1 fusion
  158.4 0.1 broadcast_multiply_fusion
  158.5 0.1 select_reduce_fusion.1
  158.6 0.1 copy.33
  158.6 0.1 broadcast_in_dim.70
  158.7 0.1 reshape.124.total_ref
  158.8 17.5 %attend8.1.late_ref = bf16[8,256,128]{2,1,0:T(8,128)(2,1)} custom-call(s32[128]{0:T(128)} %select_reduce_fusion.inv_ref, s32[8]{0:T(128)} %stack.35.bounds_ref, bf16[128,128,128]{2,1,0:T(8,128)(2,1)} %all-gather.2.cloned.1.call-done.kv_hbm, bf16[16,256,128]{2,1,0:T(8,128)(2,1)} %get-tuple-element.12.q_hbm), custom_call_target="tpu_custom_call" | custom-call | flops 4000000000 | bytes 6291456 | tf_op jit(solution)/shard_map/attend8/pallas_call | solution.py:303
  176.4 0.0 all-to-all-done.3.ends_ref
  176.4 0.0 copy-done.6
  176.4 1.0 copy-done.7
  177.4 0.8 chain.1
  178.3 0.0 copy-start
  178.3 1.3 copy-done
  179.6 7.4 %all-to-all-start.4 = ((bf16[16,512,128]{2,1,0:T(8,128)(2,1)}), bf16[16,512,128]{2,1,0:T(8,128)(2,1)S(1)}, u32[]{:S(2)}, u32[]{:S(2)}) async-start(bf16[16,512,128]{2,1,0:T(8,128)(2,1)} %copy-done), calls=%async_computation.4 | async-start | bytes 4194304 | tf_op jit(solution)/shard_map/all_to_all | solution.py:711
  187.0 0.1 dynamic_slice.30
  187.0 0.1 reshape.125
  187.1 0.1 broadcast_in_dim.71
  187.2 0.1 broadcast_in_dim.72.gain_ref
  187.3 1.8 copy-done.2
  189.1 10.6 %inner.1 = (bf16[512,2048]{1,0:T(8,128)(2,1)S(1)}, bf16[512,256]{1,0:T(8,128)(2,1)S(1)}, bf16[512,64]{1,0:T(8,128)(2,1)S(1)}) custom-call(s32[8]{0:T(128)S(1)} %copy-done.10, bf16[16,656,128]{2,1,0:T(8,128)(2,1)S(1)} %copy-done.2, f32[32,512]{1,0:T(8,128)S(1)} %get-tuple-element.17.step_ref, f32[32,512]{1,0:T(8,128)S(1)} %get-tuple-element.18.decay_ref, ...), custom_call_target="tpu_custom_call" | custom-call | flops 4000000000 | bytes 8388608 | tf_op jit(solution)/shard_map/inner/pallas_call | solution.py:572
  199.6 0.0 copy-start.3
  199.6 1.3 copy-done.3
  201.0 14.7 %all-to-all-done.4.state_ref.attn_ref = bf16[16,512,128]{2,1,0:T(8,128)(2,1)S(1)} async-done(((bf16[16,512,128]{2,1,0:T(8,128)(2,1)}), bf16[16,512,128]{2,1,0:T(8,128)(2,1)S(1)}, u32[]{:S(2)}, u32[]{:S(2)}) %all-to-all-start.4) | async-done | bytes 2097184 | tf_op jit(solution)/shard_map/all_to_all | solution.py:711
  215.6 1.6 copy-done.4
  217.2 3.9 %finish.1 = (bf16[512,2048]{1,0:T(8,128)(2,1)}, bf16[512,1024]{1,0:T(8,128)(2,1)}) custom-call(bf16[16,512,128]{2,1,0:T(8,128)(2,1)S(1)} %all-to-all-done.4.state_ref.attn_ref, bf16[16,512,128]{2,1,0:T(8,128)(2,1)S(1)} %all-to-all-done.4.state_ref.attn_ref, bf16[512,2048]{1,0:T(8,128)(2,1)S(1)} %copy-done.4, bf16[512,256]{1,0:T(8,128)(2,1)S(1)} %get-tuple-element.20.c_ref, ...), custom_call_target="tpu_custom_call" | custom-call | flops 1000000000 | bytes 9437184 | tf_op jit(solution)/shard_map/finish/pallas_call | solution.py:633
  (17 shorter events, 0.0 us)
Async XLA Ops:
  7.2 105.8 %all-gather.2.cloned.1.call-start = ((), (), s32[]{:S(2)}) async-start(), calls=%async_computation.5 | async-start | bytes 4456448 | tf_op jit(solution)/shard_map/all_gather | solution.py:680
  7.2 1.0 copy-start.8
  91.0 1.9 copy-start.11
  99.0 3.9 %copy-start.12 = (f32[256]{0:T(256)S(1)}, f32[256]{0:T(256)}, u32[]{:S(2)}) copy-start(f32[256]{0:T(256)} %param.18) | copy-start | bytes 3076
  99.0 3.9 %copy-start.13 = (f32[256]{0:T(256)S(1)}, f32[256]{0:T(256)}, u32[]{:S(2)}) copy-start(f32[256]{0:T(256)} %param.17) | copy-start | bytes 3076
  99.0 41.9 %all-to-all-start.2 = ((bf16[16,656,128]{2,1,0:T(8,128)(2,1)}), bf16[16,656,128]{2,1,0:T(8,128)(2,1)S(1)}, u32[]{:S(2)}, u32[]{:S(2)}) async-start(bf16[16,656,128]{2,1,0:T(8,128)(2,1)} %get-tuple-element.14), calls=%async_computation.2 | async-start | bytes 5373952 | tf_op jit(solution)/shard_map/all_to_all | solution.py:694
  113.0 27.9 %copy-start.9 = (s32[8]{0:T(128)S(1)}, s32[8]{0:T(128)}, u32[]{:S(2)}) copy-start(s32[8]{0:T(128)} %stack.35.bounds_ref) | copy-start | bytes 100
  140.9 6.5 %copy-start.1 = (bf16[16,656,128]{2,1,0:T(8,128)(2,1)}, bf16[16,656,128]{2,1,0:T(8,128)(2,1)S(1)}, u32[]{:S(2)}) copy-start(bf16[16,656,128]{2,1,0:T(8,128)(2,1)S(1)} %all-to-all-done.2.own_ref) | copy-start | bytes 8060932
  146.5 1.0 copy-start.5
  147.4 28.9 %all-to-all-start.3 = ((bf16[16,256,128]{2,1,0:T(8,128)(2,1)}), bf16[16,256,128]{2,1,0:T(8,128)(2,1)S(1)}, u32[]{:S(2)}, u32[]{:S(2)}) async-start(bf16[16,256,128]{2,1,0:T(8,128)(2,1)} %copy-done.5), calls=%async_computation.3 | async-start | bytes 2097152 | tf_op jit(solution)/shard_map/all_to_all | solution.py:702
  158.8 17.6 %copy-start.6 = (bf16[8,256,128]{2,1,0:T(8,128)(2,1)S(1)}, bf16[8,256,128]{2,1,0:T(8,128)(2,1)}, u32[]{:S(2)}) copy-start(bf16[8,256,128]{2,1,0:T(8,128)(2,1)} %attend0.1.early_ref) | copy-start | bytes 1572868
  158.8 17.6 %copy-start.10 = (s32[8]{0:T(128)S(1)}, s32[8]{0:T(128)}, u32[]{:S(2)}) copy-start(s32[8]{0:T(128)} %stack.35.bounds_ref) | copy-start | bytes 100
  176.4 1.0 copy-start.7
  178.3 1.3 copy-start
  179.6 7.4 %copy-start.14 = (f32[256]{0:T(256)S(1)}, f32[256]{0:T(256)}, u32[]{:S(2)}) copy-start(f32[256]{0:T(256)} %param.19) | copy-start | bytes 3076
  179.6 36.1 %all-to-all-start.4 = ((bf16[16,512,128]{2,1,0:T(8,128)(2,1)}), bf16[16,512,128]{2,1,0:T(8,128)(2,1)S(1)}, u32[]{:S(2)}, u32[]{:S(2)}) async-start(bf16[16,512,128]{2,1,0:T(8,128)(2,1)} %copy-done), calls=%async_computation.4 | async-start | bytes 4194304 | tf_op jit(solution)/shard_map/all_to_all | solution.py:711
  187.3 1.8 copy-start.2
  199.6 1.3 copy-start.3
  215.6 1.6 copy-start.4
Sparse Core Ops, SparseCore 0:
  19.7 93.2 all-gather.1

commit v6 on v5

--- a/solution.py
+++ b/solution.py
@@ -38,7 +38,7 @@
 K_AT, V_AT, G_ROWS = 0, 64, 128
 GROUP_HEADS = SSM_HEADS // GROUPS
 PAIRS = 2
-MANY = 4
+MANY = 8
 NEG_BIG = -1e30
 F32 = jnp.float32
 BF16 = jnp.bfloat16

time: 227 us -> 228 us (level); the launches traced: 228 us -> 227 us
  no operation moved by 1% of the time
where the time goes in v6:
time: 228 us; the launch traced here: 227 us
  blocking collectives  70.1 us (31%)
  Pallas kernels  64.5 us (28%)
  waiting for transfers between devices  33.4 us (15%)
  starting transfers between devices  22 us (10%)
  local copies, waits for them, and re-layouts  19.4 us (9%)
  between operations  14.2 us (6%)
  other arithmetic  3.01 us (1%)
    all_to_all x1, blocking collectives, shards(): hop = exchange(to_heads.reshape(STRETCHES, HOP_ROWS, LANES), ('seq', 'mp'))  59.3 us
    pallas_call x2, Pallas kernels, attend(): pl.pallas_call(functools.partial(attend_kernel, begin), grid_spec=pltpu.P...  30.5 us
    all_to_all x1, waiting for transfers between devices, shards(): both = exchange(chain(bounds, arrived, totals, early, late), 'seq')  14.7 us
    all_to_all x1, waiting for transfers between devices, shards(): own_rows = exchange(to_owners, 'seq')  14.4 us
    all_to_all x1, blocking collectives, shards(): exchange(pack_kv(stretch_kv), 'mp')  10.8 us
    all_to_all x1, starting transfers between devices, shards(): arrived = exchange(own_ends, 'seq')  10.8 us
    pallas_call x1, Pallas kernels, inner(): pl.pallas_call(inner_kernel, grid_spec=pltpu.PrefetchScalarGridSpec(num_s...  10.6 us
    unnamed x30, local copies, waits for them, and re-layouts  9.56 us
  transfers between devices with their start and end apart: 4, of which 3 were waited for; matrix products, arithmetic and copies ran while one was open for 6% of the time, Pallas kernels for 24%

profile of v6, /device:TPU:2, one launch (start us, length us, event | category | flops | bytes accessed | tf_op | source)
XLA Modules:
  0.0 226.7 jit_solution(13120222018920009601)
XLA Ops:
  7.2 0.0 all-gather.2.cloned.1.call-start
  7.2 0.0 copy-start.8
  7.2 0.9 copy-done.8
  8.2 0.6 pack_kv.1
  8.7 10.8 %all_to_all.25 = bf16[8,128,128]{2,1,0:T(8,128)(2,1)} all-to-all(bf16[8,128,128]{2,1,0:T(8,128)(2,1)S(1)} %pack_kv.1), channel_id=1, replica_groups=mesh['seq'=16,'mp'=8] {'mp'}, dimensions={0} | all-to-all | bytes 524288 | tf_op jit(solution)/shard_map/all_to_all | solution.py:680
  19.6 0.0 all-gather.2.cloned.1.call-update
  19.6 0.9 copy.29
  20.5 0.7 reshape.122.dt_ref
  21.2 1.2 dynamic_slice.24
  22.4 0.8 dynamic_slice.23
  23.2 0.7 add_convert_fusion
  23.9 0.6 broadcast_in_dim.62.info_ref
  24.5 7.1 %pack.1 = bf16[16,8,120,128]{3,2,1,0:T(8,128)(2,1)} custom-call(bf16[64,16384]{1,0:T(8,128)(2,1)} %x_ref.1, bf16[64,2,2048]{2,1,0:T(2,128)(2,1)} %bc_ref.1, bf16[64,8192]{1,0:T(8,128)(2,1)} %q_ref.1, bf16[128,128]{1,0:T(8,128)(2,1)} %reshape.122.dt_ref, f32[8,128]{1,0:T(8,128)} %broadcast_in_dim.62.info_ref), custom_call_target="tpu_custom_call" | custom-call | bytes 9437184 | tf_op jit(solution)/shard_map/pack/pallas_call | solution.py:71
  31.6 59.3 %all_to_all.26.hop_ref = bf16[128,120,128]{2,1,0:T(8,128)(2,1)S(1)} all-to-all(bf16[128,120,128]{2,1,0:T(8,128)(2,1)} %bitcast.16), channel_id=1, replica_groups=mesh['seq'=16,'mp'=8] {'seq','mp'}, dimensions={0} | all-to-all | bytes 7864320 | tf_op jit(solution)/shard_map/all_to_all | solution.py:684
  91.0 0.1 slice_convert_fusion
  91.1 0.2 slice_reduce_fusion
  91.3 1.0 select_reduce_fusion.inv_ref
  92.2 0.6 copy-done.11
  92.8 6.2 %place.1 = (bf16[16,656,128]{2,1,0:T(8,128)(2,1)}, bf16[16,256,128]{2,1,0:T(8,128)(2,1)}) custom-call(s32[128]{0:T(128)} %select_reduce_fusion.inv_ref, bf16[128,120,128]{2,1,0:T(8,128)(2,1)} %copy-done.11), custom_call_target="tpu_custom_call" | custom-call | bytes 6291456 | tf_op jit(solution)/shard_map/place/pallas_call | solution.py:134
  99.0 3.9 %all-to-all-start.2 = ((bf16[16,656,128]{2,1,0:T(8,128)(2,1)}), bf16[16,656,128]{2,1,0:T(8,128)(2,1)S(1)}, u32[]{:S(2)}, u32[]{:S(2)}) async-start(bf16[16,656,128]{2,1,0:T(8,128)(2,1)} %get-tuple-element.14), calls=%async_computation.2 | async-start | bytes 5373952 | tf_op jit(solution)/shard_map/all_to_all | solution.py:694
  102.9 0.0 copy-done.12
  102.9 0.0 copy-done.13
  102.9 0.1 dynamic-slice_bitcast_fusion
  103.0 0.1 copy.30.bias_ref
  103.1 0.1 copy.31.rate_ref
  103.2 0.1 dynamic_slice.29
  103.2 0.1 dynamic-slice_negate_fusion
  103.3 0.1 copy.32
  103.4 0.8 convert_reduce_fusion
  104.2 4.4 %stack.35.bounds_ref = s32[8]{0:T(128)} concatenate(s32[1]{0:T(128)} %bitcast.3, s32[1]{0:T(128)} %bitcast.4, s32[1]{0:T(128)} %bitcast.5, s32[1]{0:T(128)} %bitcast.6, s32[1]{0:T(128)} %bitcast.7, s32[1]{0:T(128)} %bitcast.8, s32[1]{0:T(128)} %bitcast.9, s32[1]{0:T(128)} %bitcast.10), dimensions={0} | concatenate | bytes 64 | tf_op jit(solution)/shard_map/stack | solution.py:690
  108.7 4.3 %all-gather.2.cloned.1.call-done.kv_hbm = bf16[128,128,128]{2,1,0:T(8,128)(2,1)} async-done(((bf16[8,128,128]{2,1,0:T(8,128)(2,1)}), bf16[128,128,128]{2,1,0:T(8,128)(2,1)}) %all-gather.2.cloned.1.call-update) | async-done | bytes 4194320 | tf_op jit(solution)/shard_map/all_gather | solution.py:680
  113.0 13.6 %attend0.1.early_ref = bf16[8,256,128]{2,1,0:T(8,128)(2,1)} custom-call(s32[128]{0:T(128)} %select_reduce_fusion.inv_ref, s32[8]{0:T(128)} %stack.35.bounds_ref, bf16[128,128,128]{2,1,0:T(8,128)(2,1)} %all-gather.2.cloned.1.call-done.kv_hbm, bf16[16,256,128]{2,1,0:T(8,128)(2,1)} %get-tuple-element.12.q_hbm), custom_call_target="tpu_custom_call" | custom-call | flops 4000000000 | bytes 6291456 | tf_op jit(solution)/shard_map/attend0/pallas_call | solution.py:303
  126.6 14.4 %all-to-all-done.2.own_ref = bf16[16,656,128]{2,1,0:T(8,128)(2,1)S(1)} async-done(((bf16[16,656,128]{2,1,0:T(8,128)(2,1)}), bf16[16,656,128]{2,1,0:T(8,128)(2,1)S(1)}, u32[]{:S(2)}, u32[]{:S(2)}) %all-to-all-start.2) | async-done | bytes 2687008 | tf_op jit(solution)/shard_map/all_to_all | solution.py:694
  141.0 0.0 copy-done.9
  141.1 5.2 %ends.1 = (bf16[16,256,128]{2,1,0:T(8,128)(2,1)S(1)}, f32[32,512]{1,0:T(8,128)S(1)}, f32[32,512]{1,0:T(8,128)S(1)}) custom-call(s32[8]{0:T(128)S(1)} %copy-done.9, bf16[16,656,128]{2,1,0:T(8,128)(2,1)S(1)} %all-to-all-done.2.own_ref, f32[32,1]{1,0:T(8,128)S(1)} %copy.30.bias_ref, f32[32,1]{1,0:T(8,128)S(1)} %copy.31.rate_ref), custom_call_target="tpu_custom_call" | custom-call | flops 1000000000 | bytes 4194304 | tf_op jit(solution)/shard_map/ends/pallas_call | solution.py:399
  146.3 0.0 copy-start.5
  146.3 1.0 copy-done.5
  147.2 0.0 copy-done.1
  147.2 10.8 %all-to-all-start.3 = ((bf16[16,256,128]{2,1,0:T(8,128)(2,1)}), bf16[16,256,128]{2,1,0:T(8,128)(2,1)S(1)}, u32[]{:S(2)}, u32[]{:S(2)}) async-start(bf16[16,256,128]{2,1,0:T(8,128)(2,1)} %copy-done.5), calls=%async_computation.3 | async-start | bytes 2097152 | tf_op jit(solution)/shard_map/all_to_all | solution.py:702
  158.0 0.1 fusion
  158.1 0.1 broadcast_multiply_fusion
  158.2 0.1 select_reduce_fusion.1
  158.3 0.1 copy.33
  158.4 0.1 broadcast_in_dim.70
  158.5 0.1 reshape.124.total_ref
  158.6 16.9 %attend8.1.late_ref = bf16[8,256,128]{2,1,0:T(8,128)(2,1)} custom-call(s32[128]{0:T(128)} %select_reduce_fusion.inv_ref, s32[8]{0:T(128)} %stack.35.bounds_ref, bf16[128,128,128]{2,1,0:T(8,128)(2,1)} %all-gather.2.cloned.1.call-done.kv_hbm, bf16[16,256,128]{2,1,0:T(8,128)(2,1)} %get-tuple-element.12.q_hbm), custom_call_target="tpu_custom_call" | custom-call | flops 4000000000 | bytes 6291456 | tf_op jit(solution)/shard_map/attend8/pallas_call | solution.py:303
  175.5 0.0 all-to-all-done.3.ends_ref
  175.5 0.0 copy-done.6
  175.5 1.0 copy-done.7
  176.5 0.8 chain.1
  177.3 0.0 copy-start
  177.3 1.3 copy-done
  178.7 7.4 %all-to-all-start.4 = ((bf16[16,512,128]{2,1,0:T(8,128)(2,1)}), bf16[16,512,128]{2,1,0:T(8,128)(2,1)S(1)}, u32[]{:S(2)}, u32[]{:S(2)}) async-start(bf16[16,512,128]{2,1,0:T(8,128)(2,1)} %copy-done), calls=%async_computation.4 | async-start | bytes 4194304 | tf_op jit(solution)/shard_map/all_to_all | solution.py:711
  186.0 0.0 copy-done.14
  186.0 0.1 dynamic_slice.30
  186.1 0.1 reshape.125
  186.2 0.1 broadcast_in_dim.71
  186.3 0.1 broadcast_in_dim.72.gain_ref
  186.4 1.8 copy-done.2
  188.1 10.6 %inner.1 = (bf16[512,2048]{1,0:T(8,128)(2,1)S(1)}, bf16[512,256]{1,0:T(8,128)(2,1)S(1)}, bf16[512,64]{1,0:T(8,128)(2,1)S(1)}) custom-call(s32[8]{0:T(128)S(1)} %copy-done.10, bf16[16,656,128]{2,1,0:T(8,128)(2,1)S(1)} %copy-done.2, f32[32,512]{1,0:T(8,128)S(1)} %get-tuple-element.17.step_ref, f32[32,512]{1,0:T(8,128)S(1)} %get-tuple-element.18.decay_ref, ...), custom_call_target="tpu_custom_call" | custom-call | flops 4000000000 | bytes 8388608 | tf_op jit(solution)/shard_map/inner/pallas_call | solution.py:572
  198.7 1.3 copy-done.3
  200.1 14.7 %all-to-all-done.4.state_ref.attn_ref = bf16[16,512,128]{2,1,0:T(8,128)(2,1)S(1)} async-done(((bf16[16,512,128]{2,1,0:T(8,128)(2,1)}), bf16[16,512,128]{2,1,0:T(8,128)(2,1)S(1)}, u32[]{:S(2)}, u32[]{:S(2)}) %all-to-all-start.4) | async-done | bytes 2097184 | tf_op jit(solution)/shard_map/all_to_all | solution.py:711
  214.7 1.6 copy-done.4
  216.3 3.6 %finish.1 = (bf16[512,2048]{1,0:T(8,128)(2,1)}, bf16[512,1024]{1,0:T(8,128)(2,1)}) custom-call(bf16[16,512,128]{2,1,0:T(8,128)(2,1)S(1)} %all-to-all-done.4.state_ref.attn_ref, bf16[16,512,128]{2,1,0:T(8,128)(2,1)S(1)} %all-to-all-done.4.state_ref.attn_ref, bf16[512,2048]{1,0:T(8,128)(2,1)S(1)} %copy-done.4, bf16[512,256]{1,0:T(8,128)(2,1)S(1)} %get-tuple-element.20.c_ref, ...), custom_call_target="tpu_custom_call" | custom-call | flops 1000000000 | bytes 9437184 | tf_op jit(solution)/shard_map/finish/pallas_call | solution.py:633
  (17 shorter events, 0.0 us)
Async XLA Ops:
  7.2 105.8 %all-gather.2.cloned.1.call-start = ((), (), s32[]{:S(2)}) async-start(), calls=%async_computation.5 | async-start | bytes 4456448 | tf_op jit(solution)/shard_map/all_gather | solution.py:680
  7.2 1.0 copy-start.8
  91.0 1.9 copy-start.11
  99.0 3.9 %copy-start.12 = (f32[256]{0:T(256)S(1)}, f32[256]{0:T(256)}, u32[]{:S(2)}) copy-start(f32[256]{0:T(256)} %param.18) | copy-start | bytes 3076
  99.0 3.9 %copy-start.13 = (f32[256]{0:T(256)S(1)}, f32[256]{0:T(256)}, u32[]{:S(2)}) copy-start(f32[256]{0:T(256)} %param.17) | copy-start | bytes 3076
  99.0 42.0 %all-to-all-start.2 = ((bf16[16,656,128]{2,1,0:T(8,128)(2,1)}), bf16[16,656,128]{2,1,0:T(8,128)(2,1)S(1)}, u32[]{:S(2)}, u32[]{:S(2)}) async-start(bf16[16,656,128]{2,1,0:T(8,128)(2,1)} %get-tuple-element.14), calls=%async_computation.2 | async-start | bytes 5373952 | tf_op jit(solution)/shard_map/all_to_all | solution.py:694
  113.0 28.1 %copy-start.9 = (s32[8]{0:T(128)S(1)}, s32[8]{0:T(128)}, u32[]{:S(2)}) copy-start(s32[8]{0:T(128)} %stack.35.bounds_ref) | copy-start | bytes 100
  141.1 6.2 %copy-start.1 = (bf16[16,656,128]{2,1,0:T(8,128)(2,1)}, bf16[16,656,128]{2,1,0:T(8,128)(2,1)S(1)}, u32[]{:S(2)}) copy-start(bf16[16,656,128]{2,1,0:T(8,128)(2,1)S(1)} %all-to-all-done.2.own_ref) | copy-start | bytes 8060932
  146.3 1.0 copy-start.5
  147.2 28.2 %all-to-all-start.3 = ((bf16[16,256,128]{2,1,0:T(8,128)(2,1)}), bf16[16,256,128]{2,1,0:T(8,128)(2,1)S(1)}, u32[]{:S(2)}, u32[]{:S(2)}) async-start(bf16[16,256,128]{2,1,0:T(8,128)(2,1)} %copy-done.5), calls=%async_computation.3 | async-start | bytes 2097152 | tf_op jit(solution)/shard_map/all_to_all | solution.py:702
  158.6 16.9 %copy-start.6 = (bf16[8,256,128]{2,1,0:T(8,128)(2,1)S(1)}, bf16[8,256,128]{2,1,0:T(8,128)(2,1)}, u32[]{:S(2)}) copy-start(bf16[8,256,128]{2,1,0:T(8,128)(2,1)} %attend0.1.early_ref) | copy-start | bytes 1572868
  158.6 16.9 %copy-start.10 = (s32[8]{0:T(128)S(1)}, s32[8]{0:T(128)}, u32[]{:S(2)}) copy-start(s32[8]{0:T(128)} %stack.35.bounds_ref) | copy-start | bytes 100
  175.5 1.0 copy-start.7
  177.3 1.3 copy-start
  178.7 7.4 %copy-start.14 = (f32[256]{0:T(256)S(1)}, f32[256]{0:T(256)}, u32[]{:S(2)}) copy-start(f32[256]{0:T(256)} %param.19) | copy-start | bytes 3076
  178.7 36.1 %all-to-all-start.4 = ((bf16[16,512,128]{2,1,0:T(8,128)(2,1)}), bf16[16,512,128]{2,1,0:T(8,128)(2,1)S(1)}, u32[]{:S(2)}, u32[]{:S(2)}) async-start(bf16[16,512,128]{2,1,0:T(8,128)(2,1)} %copy-done), calls=%async_computation.4 | async-start | bytes 4194304 | tf_op jit(solution)/shard_map/all_to_all | solution.py:711
  186.4 1.8 copy-start.2
  198.7 1.3 copy-start.3
  214.7 1.6 copy-start.4
Sparse Core Ops, SparseCore 0:
  19.7 93.2 all-gather.1
